TPU v7x, 128 devices: a whole 4x4x4 slice. The times are simulated.
128 devices in a mesh: dp: 8 (over x, z_hi), fsdp: 16 (over z_lo, y, core).
Axes of the slice: x: 4, y: 4, z: 4 (z_hi: 2, z_lo: 2; z = z_hi * 2 + z_lo), core: 2. Of those that a mesh axis runs over, the one named last changes fastest.
Arguments:
- hidden: bfloat16 [16, 1536, 1024], P('fsdp', 'dp'), may hold values from -6 to 6
- lengths: int32 [16, 3], P('fsdp'), may hold values from 1 to 1534, as said below
- w_query: bfloat16 [1024, 2048], P(('dp', 'fsdp')), may hold values from -0.1875 to 0.1875
- w_key: bfloat16 [1024, 1024], P(('dp', 'fsdp')), may hold values from -0.1875 to 0.1875
- w_value: bfloat16 [1024, 1024], P(('dp', 'fsdp')), may hold values from -0.1875 to 0.1875
- w_out: bfloat16 [2048, 1024], P(('dp', 'fsdp')), may hold values from -0.75 to 0.75
- w_gate: bfloat16 [1024, 3072], P(('dp', 'fsdp')), may hold values from -0.1875 to 0.1875
- w_up: bfloat16 [1024, 3072], P(('dp', 'fsdp')), may hold values from -0.1875 to 0.1875
- w_down: bfloat16 [3072, 1024], P(('dp', 'fsdp')), may hold values from -0.109375 to 0.109375
- gains: bfloat16 [2304], P(('dp', 'fsdp')), may hold values from 0.099609375 to 1.8984375
- cotangent: bfloat16 [16, 1536, 1024], P('fsdp', 'dp'), may hold values from -6 to 6
Outputs:
- activations: bfloat16 [16, 1536, 1024], P('fsdp', 'dp')
- input_grad: float32 [16, 1536, 1024], P('fsdp', 'dp')
- grad_query: float32 [1024, 2048], P(('dp', 'fsdp'))
- grad_key: float32 [1024, 1024], P(('dp', 'fsdp'))
- grad_value: float32 [1024, 1024], P(('dp', 'fsdp'))
- grad_out: float32 [2048, 1024], P(('dp', 'fsdp'))
- grad_gate: float32 [1024, 3072], P(('dp', 'fsdp'))
- grad_up: float32 [1024, 3072], P(('dp', 'fsdp'))
- grad_down: float32 [3072, 1024], P(('dp', 'fsdp'))
- grad_gains: float32 [2304], P(('dp', 'fsdp'))
Inputs may be any that keep to these rules, and one draw needn't show every extreme that they name: `lengths`: in each pack the first and the last document hold 1 to 96 tokens each and the middle one the rest of the 1536 tokens.
All inputs are finite; a program needn't handle non-finite values.
Results may differ from a plain program's by a relative error of at most 0.017.
Values may be sent and summed in bfloat16 or wider, within the bound.
No kernel may reach another device: no remote copies, remote signals or barrier semaphores. Data moves between devices by JAX's collectives and lax.ppermute only.
A program may use at most 192 MiB of HBM per device.

v0:
```python
import jax
import jax.numpy as jnp
from jax import lax
from jax.experimental import pallas as pl
from jax.experimental.pallas import tpu as pltpu
from jax.sharding import Mesh
from jax.sharding import PartitionSpec as P

HEADS = 16
KV_HEADS = 8
HEAD = 128
EPSILON = 1e-06
ROPE_BASE = 1000000.0
DEVICES = 128
WIDTH = 1024
FF = 3072
TOK = 192
PACK = 1536
BLOCK = 256
LOG2E = 1.4426950408889634
SCALE = HEAD ** (-0.5)
VMEM_LIMIT = 48 * 1024 * 1024
VMEM_MOST = 58 * 1024 * 1024

AXES = ("x", "zh", "zl", "y", "core")
RING = ("x", "core")
PLANE = ("zh", "zl", "y")
XA, XB, ZA, ZB, YA, YB, CORE = 32, 96, 8, 24, 2, 6, 1
RING_STEPS = ((XA, XB), (XB, XA))
RING_SPOTS = ((0, 1, 3, 2), (0, 2, 3, 1))
PLANE_STEPS = ((YA, ZA), (YB, ZB), (ZA, YA), (ZB, YB))
BIT = {YA: 1, YB: 2, ZA: 3, ZB: 4}


def swap(values, mask, other_mask=None):
    masks = (mask, mask if other_mask is None else other_mask)
    return lax.ppermute(values, AXES, [(k, k ^ masks[k & 1]) for k in range(DEVICES)])


def crossed(k):
    return k ^ 17 if (k >> 4 ^ k) & 1 else k


def cross(values):
    return lax.ppermute(values, AXES, [(k, crossed(k)) for k in range(DEVICES)])


def cross_and_swap(values, masks):
    return lax.ppermute(
        values, AXES, [(crossed(k ^ masks[k & 1]), k) for k in range(DEVICES)]
    )


def swap_and_cross(values, masks):
    return lax.ppermute(
        values, AXES, [(k, crossed(k ^ masks[k & 1])) for k in range(DEVICES)]
    )


def after(value, *others):
    return lax.optimization_barrier((value, *others))[0] if others else value


def low(values):
    return values.astype(jnp.bfloat16)


def wide(values):
    return values.astype(jnp.float32)


def dot(left, right):
    return jnp.dot(left, right, preferred_element_type=jnp.float32)


def contract_rows(left, right):
    return lax.dot_general(
        left, right, (((0,), (0,)), ((), ())), preferred_element_type=jnp.float32
    )


def contract_cols(left, right):
    return lax.dot_general(
        left, right, (((1,), (1,)), ((), ())), preferred_element_type=jnp.float32
    )


def norm_scale(values):
    return lax.rsqrt(jnp.mean(values * values, axis=-1, keepdims=True) + EPSILON)


def norm_back(values, gain, grad):
    scale = norm_scale(values)
    normal = values * scale
    inner = grad * gain
    return scale * (inner - normal * jnp.mean(inner * normal, axis=-1, keepdims=True))


def rope(values, cosine, sine):
    return values * cosine + pltpu.roll(values, 64, 1) * sine


def rope_back(grad, cosine, sine):
    return grad * cosine + pltpu.roll(grad * sine, 64, 1)


def ring_specs(columns, stride=1):
    return [
        pl.BlockSpec((TOK, columns), lambda x, spots: (spots[x] * stride, 0)),
        pl.BlockSpec((TOK, columns), lambda x, spots: (spots[4 + x] * stride, 0)),
    ]


def pack_spec(columns):
    return pl.BlockSpec((2 * TOK, columns), lambda x, spots: (x, 0))


def whole_spec(shape):
    return pl.BlockSpec(shape, lambda x, spots: (0, 0))


def own_rows(spots):
    return pl.ds(pl.multiple_of(spots[8] * TOK, TOK), TOK)


def other_rows(spots):
    return pl.ds(pl.multiple_of((1 - spots[8]) * TOK, TOK), TOK)


def ring_call(
    kernel, name, in_specs, out_specs, out_shape, flops, spots, *operands, scratch=(), limit=VMEM_LIMIT
):
    return pl.pallas_call(
        kernel,
        grid_spec=pltpu.PrefetchScalarGridSpec(
            num_scalar_prefetch=1,
            grid=(4,),
            in_specs=in_specs,
            out_specs=out_specs,
            scratch_shapes=scratch,
        ),
        out_shape=[jax.ShapeDtypeStruct(shape, dtype) for shape, dtype in out_shape],
        compiler_params=pltpu.CompilerParams(vmem_limit_bytes=limit),
        cost_estimate=pl.CostEstimate(flops=flops, bytes_accessed=12000000, transcendentals=0),
        name=name,
    )(spots, *operands)


def qkv_kernel(
    spots, own_ref, other_ref, heads_ref, ga_ref, gq_ref, gk_ref, cos_ref, sin_ref,
    normed_ref, pre_ref, qkv_ref, w_ref,
):
    @pl.when(pl.program_id(0) == 0)
    def _():
        for z in range(4):
            for y in range(4):
                block = jnp.where(spots[9] == 1, y * 4 + z, z * 4 + y)
                for x in range(4):
                    row = (x * 16 + z * 4 + y) * 16
                    w_ref[row : row + 16, :] = heads_ref[block, x * 16 : x * 16 + 16, :512]

    for ref, rows in ((own_ref, own_rows(spots)), (other_ref, other_rows(spots))):
        x = wide(ref[...])
        normed_ref[rows, :] = low(x * norm_scale(x) * ga_ref[...])
    pre = dot(normed_ref[...], w_ref[...])
    pre_ref[...] = pre[:, : 3 * HEAD]
    cosine, sine = cos_ref[...], sin_ref[...]
    for h in range(3):
        u = pre[:, h * HEAD : (h + 1) * HEAD]
        gain = gk_ref[...] if h == 2 else gq_ref[...]
        normal = u * norm_scale(u) * gain
        qkv_ref[:, h * HEAD : (h + 1) * HEAD] = low(rope(normal, cosine, sine))
    qkv_ref[:, 3 * HEAD :] = low(pre[:, 3 * HEAD :])


def project(spots, own, other, heads, gain_attn, gain_query, gain_key, cosine, sine):
    return ring_call(
        qkv_kernel,
        "project",
        ring_specs(WIDTH, 2)
        + [pl.BlockSpec(heads.shape, lambda x, spots: (0, 0, 0))]
        + [whole_spec((1, WIDTH)), whole_spec((1, HEAD)), whole_spec((1, HEAD))]
        + [pack_spec(HEAD), pack_spec(HEAD)],
        [pack_spec(WIDTH), pack_spec(3 * HEAD), pack_spec(512), whole_spec((WIDTH, 512))],
        [
            ((PACK, WIDTH), jnp.bfloat16),
            ((PACK, 3 * HEAD), jnp.float32),
            ((PACK, 512), jnp.bfloat16),
            ((WIDTH, 512), jnp.bfloat16),
        ],
        1610612736, spots, own, other, heads, gain_attn, gain_query, gain_key, cosine, sine,
    )


def to_ring_kernel(spots, rows_ref, w_ref, own_ref, other_ref):
    own_ref[...] = low(dot(rows_ref[own_rows(spots), :], w_ref[...]))
    other_ref[...] = low(dot(rows_ref[other_rows(spots), :], w_ref[...]))


def to_ring(spots, rows, weights):
    half = ((PACK // 2, WIDTH), jnp.bfloat16)
    return ring_call(
        to_ring_kernel, "to_ring", [pack_spec(256), whole_spec((256, WIDTH))], ring_specs(WIDTH),
        [half, half], 800000000, spots, rows, weights,
    )


def to_pack_kernel(spots, own_ref, other_ref, w_ref, rows_ref):
    rows_ref[own_rows(spots), :] = low(dot(own_ref[...], w_ref[...]))
    rows_ref[other_rows(spots), :] = low(dot(other_ref[...], w_ref[...]))


def to_pack(spots, own, other, weights):
    return ring_call(
        to_pack_kernel, "to_pack", ring_specs(own.shape[1]) + [whole_spec(weights.shape)],
        [pack_spec(WIDTH)], [((PACK, WIDTH), jnp.bfloat16)], 1200000000, spots, own, other, weights,
    )[0]


def out_back_kernel(spots, own_ref, other_ref, attended_ref, w_ref, d_attended_ref, d_w_ref, rows_ref):
    @pl.when(pl.program_id(0) == 0)
    def _():
        d_w_ref[...] = jnp.zeros_like(d_w_ref)

    rows_ref[own_rows(spots), :] = own_ref[...]
    rows_ref[other_rows(spots), :] = other_ref[...]
    d_attended_ref[...] = low(contract_cols(rows_ref[...], w_ref[...]))
    d_w_ref[...] += contract_rows(attended_ref[...], rows_ref[...])


def out_back(spots, own, other, attended, weights):
    return ring_call(
        out_back_kernel, "out_back",
        ring_specs(WIDTH) + [pack_spec(256), whole_spec((256, WIDTH))],
        [pack_spec(256), whole_spec((256, WIDTH))],
        [((PACK, 256), jnp.bfloat16), ((256, WIDTH), jnp.float32)],
        1600000000, spots, own, other, attended, weights,
        scratch=[pltpu.VMEM((2 * TOK, WIDTH), jnp.bfloat16)],
    )


def row_start(rows, ends):
    first, second = ends
    return jnp.where(rows >= second, second, jnp.where(rows >= first, first, 0))


def block_mask(q_block, k_block, ends, transposed):
    last = PACK // BLOCK - 1
    q_axis, k_axis = (1, 0) if transposed else (0, 1)
    q_rows = q_block * BLOCK + lax.broadcasted_iota(jnp.int32, (BLOCK, BLOCK), q_axis)
    k_rows = k_block * BLOCK + lax.broadcasted_iota(jnp.int32, (BLOCK, BLOCK), k_axis)
    mask = None
    if k_block == q_block:
        mask = k_rows <= q_rows
    if k_block == 0 or q_block == last:
        begun = k_rows >= row_start(q_rows, ends)
        mask = begun if mask is None else mask & begun
    return mask


def for_each_block(step):
    for q_block in range(PACK // BLOCK):

        @pl.when(pl.program_id(0) == q_block)
        def _(q_block=q_block):
            step(q_block)


def attend_kernel(ends_ref, q_ref, k_ref, v_ref, out_ref, inverse_ref):
    ends = (ends_ref[0], ends_ref[1])

    def step(q_block):
        seen = (q_block + 1) * BLOCK
        for h in range(2):
            columns = slice(h * HEAD, (h + 1) * HEAD)
            scores = contract_cols(q_ref[:, columns], k_ref[:seen, :])
            part, shifted = 0.0, []
            for k_block in range(q_block + 1):
                block = scores[:, k_block * BLOCK : (k_block + 1) * BLOCK]
                block = jnp.exp2(block * (SCALE * LOG2E))
                mask = block_mask(q_block, k_block, ends, False)
                if mask is not None:
                    block = jnp.where(mask, block, 0.0)
                part += block[:, :HEAD] + block[:, HEAD:]
                shifted.append(low(block))
            total = dot(jnp.concatenate(shifted, axis=1), v_ref[:seen, :])
            row_total = jnp.sum(part, axis=1, keepdims=True)
            out_ref[:, columns] = low(total * (1.0 / row_total))
            across = jnp.sum(jnp.swapaxes(part, 0, 1), axis=0, keepdims=True)
            inverse_ref[h : h + 1, :] = 1.0 / across

    for_each_block(step)


def attend(ends, qkv):
    return pl.pallas_call(
        attend_kernel,
        grid_spec=pltpu.PrefetchScalarGridSpec(
            num_scalar_prefetch=1,
            grid=(PACK // BLOCK,),
            in_specs=[
                pl.BlockSpec((BLOCK, 2 * HEAD), lambda q, ends: (q, 0)),
                pl.BlockSpec((PACK, HEAD), lambda q, ends: (0, 2)),
                pl.BlockSpec((PACK, HEAD), lambda q, ends: (0, 3)),
            ],
            out_specs=[
                pl.BlockSpec((BLOCK, 2 * HEAD), lambda q, ends: (q, 0)),
                pl.BlockSpec((2, BLOCK), lambda q, ends: (0, q)),
            ],
        ),
        out_shape=[
            jax.ShapeDtypeStruct((PACK, 2 * HEAD), jnp.bfloat16),
            jax.ShapeDtypeStruct((2, PACK), jnp.float32),
        ],
        compiler_params=pltpu.CompilerParams(vmem_limit_bytes=VMEM_LIMIT),
        cost_estimate=pl.CostEstimate(flops=3000000000, bytes_accessed=4000000, transcendentals=3000000),
        name="attend",
    )(ends, qkv, qkv, qkv)


def attend_back_kernel(
    ends_ref, q_ref, k_ref, v_ref, grad_ref, out_ref, inverse_ref, dq_ref, dk_ref, dv_ref
):
    ends = (ends_ref[0], ends_ref[1])

    @pl.when(pl.program_id(0) == 0)
    def _():
        dk_ref[...] = jnp.zeros_like(dk_ref)
        dv_ref[...] = jnp.zeros_like(dv_ref)

    def both_heads(ref):
        return jnp.concatenate([ref[:, :HEAD], ref[:, HEAD:]], axis=0)

    def step(q_block):
        seen = (q_block + 1) * BLOCK
        queries, grads = both_heads(q_ref), both_heads(grad_ref)
        product = wide(grads) * wide(both_heads(out_ref))
        delta = jnp.sum(jnp.swapaxes(product, 0, 1), axis=0, keepdims=True)
        inverse = jnp.concatenate([inverse_ref[0:1, :], inverse_ref[1:2, :]], axis=1)
        scores = contract_cols(k_ref[:seen, :], queries)
        d_probs = contract_cols(v_ref[:seen, :], grads)
        probs, d_scores = [], []
        for k_block in range(q_block + 1):
            rows = slice(k_block * BLOCK, (k_block + 1) * BLOCK)
            prob = jnp.exp2(scores[rows] * (SCALE * LOG2E)) * inverse
            mask = block_mask(q_block, k_block, ends, True)
            if mask is not None:
                prob = jnp.where(jnp.concatenate([mask, mask], axis=1), prob, 0.0)
            d_scores.append(low(prob * ((d_probs[rows] - delta) * SCALE)))
            probs.append(low(prob))
        probs = jnp.concatenate(probs, axis=0)
        d_scores = jnp.concatenate(d_scores, axis=0)
        dk_ref[:seen, :] += dot(d_scores, queries)
        dv_ref[:seen, :] += dot(probs, grads)
        d_queries = contract_rows(d_scores, k_ref[:seen, :])
        dq_ref[:, :HEAD] = d_queries[:BLOCK]
        dq_ref[:, HEAD:] = d_queries[BLOCK:]

    for_each_block(step)


def attend_back(ends, qkv, grad, out, inverse):
    by_block = pl.BlockSpec((BLOCK, 2 * HEAD), lambda q, ends: (q, 0))
    whole = pl.BlockSpec((PACK, HEAD), lambda q, ends: (0, 0))
    return pl.pallas_call(
        attend_back_kernel,
        grid_spec=pltpu.PrefetchScalarGridSpec(
            num_scalar_prefetch=1,
            grid=(PACK // BLOCK,),
            in_specs=[
                by_block,
                pl.BlockSpec((PACK, HEAD), lambda q, ends: (0, 2)),
                pl.BlockSpec((PACK, HEAD), lambda q, ends: (0, 3)),
                by_block,
                by_block,
                pl.BlockSpec((2, BLOCK), lambda q, ends: (0, q)),
            ],
            out_specs=[by_block, whole, whole],
        ),
        out_shape=[
            jax.ShapeDtypeStruct((PACK, 2 * HEAD), jnp.float32),
            jax.ShapeDtypeStruct((PACK, HEAD), jnp.float32),
            jax.ShapeDtypeStruct((PACK, HEAD), jnp.float32),
        ],
        compiler_params=pltpu.CompilerParams(vmem_limit_bytes=VMEM_LIMIT),
        cost_estimate=pl.CostEstimate(flops=8000000000, bytes_accessed=8000000, transcendentals=3000000),
        name="attend_back",
    )(ends, qkv, qkv, qkv, grad, out, inverse)


def qkv_back_kernel(
    spots, pre_ref, dq_ref, dk_ref, dv_ref, cos_ref, sin_ref, normed_ref, w_ref, gq_ref, gk_ref,
    d_pre_ref, d_attn_ref, d_head_ref, own_ref, other_ref, rows_ref,
):
    @pl.when(pl.program_id(0) == 0)
    def _():
        d_attn_ref[...] = jnp.zeros_like(d_attn_ref)
        d_head_ref[...] = jnp.zeros_like(d_head_ref)

    cosine, sine = cos_ref[...], sin_ref[...]
    for h in range(3):
        u = pre_ref[:, h * HEAD : (h + 1) * HEAD]
        gain = gk_ref[...] if h == 2 else gq_ref[...]
        grad = dk_ref[...] if h == 2 else dq_ref[:, h * HEAD : (h + 1) * HEAD]
        grad = rope_back(grad, cosine, sine)
        row = 1 if h == 2 else 0
        d_head_ref[row : row + 1, :] += jnp.sum(
            grad * u * norm_scale(u), axis=0, keepdims=True
        )
        d_pre_ref[:, h * HEAD : (h + 1) * HEAD] = low(norm_back(u, gain, grad))
    d_pre_ref[:, 3 * HEAD :] = low(dv_ref[...])
    d_normed = dot(d_pre_ref[...], w_ref[...])
    d_attn_ref[...] += jnp.sum(wide(normed_ref[...]) * d_normed, axis=0, keepdims=True)
    rows_ref[...] = low(d_normed)
    own_ref[...] = rows_ref[own_rows(spots), :]
    other_ref[...] = rows_ref[other_rows(spots), :]


def project_back(spots, pre, d_query, d_key, d_value, cosine, sine, normed, weights, gain_query, gain_key):
    half = ((PACK // 2, WIDTH), jnp.bfloat16)
    return ring_call(
        qkv_back_kernel,
        "project_back",
        [pack_spec(3 * HEAD), pack_spec(2 * HEAD), pack_spec(HEAD), pack_spec(HEAD)]
        + [pack_spec(HEAD), pack_spec(HEAD), pack_spec(WIDTH)]
        + [whole_spec((512, WIDTH)), whole_spec((1, HEAD)), whole_spec((1, HEAD))],
        [pack_spec(512), whole_spec((1, WIDTH)), whole_spec((2, HEAD))] + ring_specs(WIDTH),
        [((PACK, 512), jnp.bfloat16), ((1, WIDTH), jnp.float32), ((2, HEAD), jnp.float32), half, half],
        1610612736, spots, pre, d_query, d_key, d_value, cosine, sine, normed, weights, gain_query, gain_key,
        scratch=[pltpu.VMEM((2 * TOK, WIDTH), jnp.bfloat16)], limit=VMEM_MOST,
    )


def exchange(values, axes):
    return lax.all_to_all(values, axes, split_axis=0, concat_axis=0, tiled=True)


def plane_order(core, blocks):
    return jnp.where(core == 1, jnp.swapaxes(blocks, 0, 1), blocks)


def plane_bit(index, masks):
    return jnp.where(index & 1 == 1, index >> BIT[masks[1]], index >> BIT[masks[0]]) & 1


def gather_plane_step(index, block, step):
    got = swap(block, *PLANE_STEPS[step])
    return jnp.where(
        plane_bit(index, PLANE_STEPS[step]) == 1,
        jnp.concatenate([got, block], axis=0),
        jnp.concatenate([block, got], axis=0),
    )


def gather_plane_end(index, block):
    shape = block.shape[1:]
    return plane_order(index & 1, block.reshape((4, 4) + shape)).reshape((16,) + shape)


def gather_ring(rows, beside=((), ())):
    for masks, others in zip(RING_STEPS, beside):
        rows = jnp.concatenate([rows, after(swap(rows, *masks), *others)], axis=0)
    return rows


def scatter_ring(own, other, steps=2):
    totals = [wide(own) + wide(swap(other, CORE))]
    for masks in RING_STEPS[: -steps - 1 : -1]:
        half = totals[-1].shape[0] // 2
        totals.append(totals[-1][:half] + wide(swap(low(totals[-1][half:]), *masks)))
    return totals


def exchange_ring(index, blocks):
    core, x = index & 1, index >> 5
    shape = blocks.shape[1:]
    blocks = blocks.reshape((4, 2) + shape)
    take = lambda array, at, axis: lax.dynamic_slice_in_dim(array, at, 1, axis)
    got = swap(take(blocks, 1 - core, 1), CORE)
    keep = take(blocks, core, 1)
    blocks = jnp.concatenate(
        [jnp.where(core == 1, got, keep), jnp.where(core == 1, keep, got)], axis=1
    )
    parts = [take(blocks, x, 0)] + [
        swap(take(blocks, x ^ k, 0), k << 5) for k in range(1, 4)
    ]
    parts = jnp.concatenate(parts, axis=0)
    parts = jnp.where(x & 1 == 1, parts.reshape((2, 2, 2) + shape)[:, ::-1].reshape(parts.shape), parts)
    parts = jnp.where(x & 2 == 2, parts.reshape((2, 4) + shape)[::-1].reshape(parts.shape), parts)
    return parts.reshape((8,) + shape)


def tiles_tall(block):
    lead = block.shape[:-2]
    n = len(lead)
    block = block.reshape(lead + (-1, 8, 8, HEAD))
    block = block.transpose(tuple(range(n)) + (n + 2, n + 1, n, n + 3))
    return block.reshape(lead + (64, -1))


def tiles_flat(block):
    lead = block.shape[:-2]
    n = len(lead)
    block = block.reshape(lead + (8, 8, -1, HEAD))
    block = block.transpose(tuple(range(n)) + (n + 2, n + 1, n, n + 3))
    return block.reshape(lead + (-1, WIDTH))


def rows_by_device(blocks):
    n = blocks.shape[-1]
    return blocks.reshape(16, 4, 2, 8, n).transpose(1, 0, 2, 3, 4).reshape(WIDTH, n)


def rows_by_plane(rows):
    n = rows.shape[-1]
    return rows.reshape(4, 16, 2, 8, n).transpose(1, 0, 2, 3, 4).reshape(16, 64, n)


def on_device(
    hidden, lengths, w_query, w_key, w_value, w_out, w_gate, w_up, w_down, gains, cotangent
):
    index = lax.axis_index(AXES).astype(jnp.int32)
    core, x = index & 1, index >> 5
    straight = (index >> 4 & 1) == core
    spot_of = lambda c: jnp.where(c == 1, jnp.asarray(RING_SPOTS[1]), jnp.asarray(RING_SPOTS[0]))
    chips = x ^ jnp.arange(4, dtype=jnp.int32)
    spots = jnp.concatenate(
        [spot_of(core)[chips], spot_of(1 - core)[chips], core[None], core[None]]
    ).astype(jnp.int32)

    first = cross(jnp.concatenate([hidden[0], cotangent[0], w_out], axis=0))
    second = cross_and_swap(jnp.concatenate([hidden[0], cotangent[0]], axis=0), RING_STEPS[0])
    local = jnp.concatenate(
        [
            w_query.reshape(8, KV_HEADS, 256).transpose(1, 0, 2),
            w_key.reshape(8, KV_HEADS, HEAD).transpose(1, 0, 2),
            w_value.reshape(8, KV_HEADS, HEAD).transpose(1, 0, 2),
            jnp.broadcast_to(jnp.pad(gains[None, None, :], ((0, 0), (0, 7), (0, 110))), (8, 8, 128)),
        ]
        + [
            weight.reshape(8, 4, 16, 2, 24).transpose(1, 3, 0, 2, 4).reshape(8, 8, 384)
            for weight in (w_gate, w_up)
        ],
        axis=2,
    )
    local = exchange(local, RING).reshape(64, 1408)
    inputs, d_result = first[:TOK], first[TOK : 2 * TOK]
    heads = jnp.concatenate([local[:, :640], tiles_tall(first[2 * TOK :])], axis=1)[None]
    for step in range(4):
        heads = gather_plane_step(index, heads, step)
    gain_all = plane_order(core, heads[:, ::8, 512:530].reshape(4, 4, 8, 18))
    gain_all = gain_all.reshape(16, 4, 2, 18).transpose(1, 0, 2, 3)
    gain_all = wide(gain_all.reshape(1, -1))
    gain_attn, gain_mlp = gain_all[:, :WIDTH], gain_all[:, WIDTH : 2 * WIDTH]
    gain_query = gain_all[:, 2 * WIDTH : 2 * WIDTH + HEAD]
    gain_key = gain_all[:, 2 * WIDTH + HEAD :]

    rows_own = jnp.concatenate([first[: 2 * TOK], second], axis=0)
    rows_own = jnp.concatenate([rows_own, swap(rows_own, *RING_STEPS[1])], axis=0)
    rows_other = swap(rows_own, CORE)
    lengths = jnp.where(straight, lengths, swap(lengths, CORE))
    ends = jnp.stack([lengths[0, 0], lengths[0, 0] + lengths[0, 1]]).astype(jnp.int32)
    token = jnp.arange(PACK, dtype=jnp.int32)
    position = wide(token - row_start(token, (ends[0], ends[1])))
    inverse = jnp.power(ROPE_BASE, -2.0 * jnp.arange(HEAD // 2, dtype=jnp.float32) / HEAD)
    angle = position[:, None] * inverse[None, :]
    cosine, sine = jnp.cos(angle), jnp.sin(angle)
    cosine = jnp.concatenate([cosine, cosine], axis=1)
    sine = jnp.concatenate([-sine, sine], axis=1)

    normed, pre, qkv, w_heads = project(
        spots, rows_own, rows_other, heads, gain_attn, gain_query, gain_key, cosine, sine
    )
    heads = after(heads, qkv)
    attended, inverse_total = attend(ends, qkv)
    w_rows = plane_order(core, heads[..., 640:].reshape(4, 4, 64, 256)).reshape(16, 64, 256)
    w_rows = tiles_flat(w_rows).reshape(2, 8, 16, WIDTH).transpose(1, 0, 2, 3).reshape(256, WIDTH)
    out_own, out_other = to_ring(spots, attended, w_rows)
    middle_steps = scatter_ring(out_own, out_other)
    d_result_own, d_result_other = (
        rows.reshape(4, 2, TOK, WIDTH)[:, 1].reshape(-1, WIDTH)
        for rows in (after(rows_own, middle_steps[0]), after(rows_other, middle_steps[1]))
    )

    units = jnp.concatenate([local[:, 640:], tiles_tall(w_down)], axis=1)[None]
    units = gather_plane_step(index, after(units, out_own), 0)
    units = gather_plane_step(index, after(units, middle_steps[0]), 1)
    units = gather_plane_step(index, after(units, middle_steps[1]), 2)
    middle = wide(inputs) + middle_steps[2]
    middle_scale = norm_scale(middle)
    mixed = low(middle * middle_scale * gain_mlp)
    mixed_own = gather_ring(mixed)
    mixed_other = swap(mixed_own, CORE)
    units = gather_plane_step(index, units, 3)
    units = plane_order(core, units.reshape(4, 4, 64, 1152)).reshape(16, 64, 1152)
    full_units = rows_by_device(units[..., :768])
    full_down = tiles_flat(units[..., 768:]).reshape(384, WIDTH)

    def feed_forward(rows, d_rows):
        pre = dot(rows, full_units)
        gate_pre, up_pre = pre[:, :384], pre[:, 384:]
        sigmoid = 1.0 / (1.0 + jnp.exp(-gate_pre))
        silu = gate_pre * sigmoid
        act = low(silu * up_pre)
        d_act = contract_cols(d_rows, full_down)
        d_gate = low(d_act * up_pre * (sigmoid + silu * (1.0 - sigmoid)))
        d_up = low(d_act * silu)
        d_pre = jnp.concatenate([d_gate, d_up], axis=1)
        return act, d_pre, low(contract_cols(d_pre, full_units))

    act_own, d_pre_own, d_mixed_own = feed_forward(mixed_own, d_result_own)
    act_other, d_pre_other, d_mixed_other = feed_forward(mixed_other, d_result_other)
    d_mixed_steps = scatter_ring(d_mixed_own, d_mixed_other)
    d_mixed = d_mixed_steps[-1]
    d_middle = wide(d_result) + norm_back(middle, gain_mlp, d_mixed)
    d_gain_mlp = jnp.sum(middle * middle_scale * d_mixed, axis=0)

    late = lambda array: after(array, d_mixed_steps[0])
    grad_units = contract_rows(mixed_own, late(d_pre_own)) + contract_rows(mixed_other, late(d_pre_other))
    grad_units = low(grad_units)
    late = lambda array: after(array, d_mixed_steps[1], grad_units)
    grad_down = contract_rows(late(act_own), d_result_own) + contract_rows(late(act_other), d_result_other)
    grad_down = low(grad_down).reshape(16, 3, 8, 8, HEAD).transpose(0, 3, 2, 1, 4)
    grads = jnp.concatenate([rows_by_plane(grad_units), grad_down.reshape(16, 64, 384)], axis=2)
    act_own, act_other = (after(act, grads) for act in (act_own, act_other))
    result = to_pack(spots, act_own, act_other, full_down)
    d_branch_own = gather_ring(low(d_middle), ((grads,), (result,)))
    d_branch_other = swap(d_branch_own, CORE)
    grads = exchange(grads, PLANE)
    result = lax.psum_scatter(after(result, d_branch_own), RING, scatter_dimension=0, tiled=True)
    d_middle_home = jnp.where(straight, d_middle, wide(cross(after(low(d_middle), d_branch_own))))

    d_attended, grad_out = out_back(spots, d_branch_own, d_branch_other, attended, w_rows)
    d_query, d_key, d_value = attend_back(ends, qkv, d_attended, attended, inverse_total)
    d_query, grads, grad_out = lax.optimization_barrier((d_query, grads, grad_out))
    grad_out = low(grad_out).reshape(8, 2, 16, WIDTH).transpose(1, 0, 2, 3).reshape(16, 16, WIDTH)
    grad_out = exchange(grad_out, PLANE)
    d_pre, d_gain_attn, d_gain_heads, d_normed_own, d_normed_other = project_back(
        spots, pre, d_query, d_key, d_value, cosine, sine, normed, w_heads.T, gain_query, gain_key
    )
    d_normed_steps = scatter_ring(d_normed_own, d_normed_other, 1)
    halves = low(d_normed_steps[1][:TOK]), low(d_normed_steps[1][TOK:])
    d_normed = wide(cross(halves[0])) + wide(swap_and_cross(halves[1], RING_STEPS[0]))
    input_grad = d_middle_home + norm_back(wide(hidden[0]), gain_attn, d_normed)

    d_gains = jnp.concatenate(
        [(d_gain_attn / gain_attn)[0], d_gain_mlp, d_gain_heads.reshape(-1)]
    )
    payload = jnp.concatenate(
        [
            low(contract_rows(normed, d_pre)).reshape(DEVICES, 8, 512),
            low(jnp.pad(d_gains.reshape(DEVICES, 1, 18), ((0, 0), (0, 7), (0, 110)))),
        ],
        axis=2,
    )
    heads_grad = wide(exchange(payload, AXES)).reshape(4, 16, 2, 8, 640)
    heads_grad = jnp.sum(heads_grad, axis=1).reshape(8, 8, 640)

    grads, grad_out = (after(array, d_normed_steps[0]) for array in (grads, grad_out))
    sums = jnp.sum(wide(grads), axis=0)
    units_grad = wide(exchange_ring(index, low(sums[:, :768]).reshape(8, 8, 768)))
    sum_down = tiles_flat(sums[:, 768:])
    sum_out = jnp.sum(wide(grad_out), axis=0)
    sum_out = jnp.where(straight, sum_out, wide(cross(low(sum_out))))
    activations = cross(after(low(middle + wide(result)), d_normed_steps[0]))
    by_unit = lambda grad: (
        grad.reshape(4, 2, 8, 16, 24).transpose(2, 0, 3, 1, 4).reshape(8, FF)
    )
    sum_query = heads_grad[..., :256].transpose(1, 0, 2).reshape(8, -1)
    sum_key = heads_grad[..., 256:384].transpose(1, 0, 2).reshape(8, -1)
    sum_value = heads_grad[..., 384:512].transpose(1, 0, 2).reshape(8, -1)
    sum_gains = jnp.sum(heads_grad[:, 0, 512:530], axis=0)
    return (
        activations[None],
        input_grad[None],
        sum_query,
        sum_key,
        sum_value,
        sum_out,
        by_unit(units_grad[..., :384]),
        by_unit(units_grad[..., 384:]),
        sum_down,
        sum_gains,
    )


def solution(mesh):
    chips = Mesh(mesh.devices.reshape(4, 2, 2, 4, 2), AXES)
    rows = P(AXES, None)
    tokens = P(("zl", "y", "core"), ("x", "zh"), None)
    lengths = P(("zl", "y", "core"), None)
    return jax.shard_map(
        on_device,
        mesh=chips,
        in_specs=(tokens, lengths, *([rows] * 7), P(AXES), tokens),
        out_specs=(tokens, tokens, *([rows] * 7), P(AXES)),
        check_vma=False,
    )
```

profile of v0, /device:TPU:1, one launch (start us, length us, event | category | flops | bytes accessed | tf_op | source)
XLA Modules:
  0.0 393.3 jit_solution(2541727601708314612)
XLA Ops:
  8.5 7.0 %collective-permute-start = (bf16[400,1024]{1,0:T(8,128)(2,1)S(1)}, bf16[400,1024]{1,0:T(8,128)(2,1)S(1)}, u32[]{:S(2)}, u32[]{:S(2)}) collective-permute-start(bf16[400,1024]{1,0:T(8,128)(2,1)S(1)} %pad_maximum_fusion.7), channel_id=1, source_target_pairs={{0,0},{1,16},{2,2},{3,18},{4,4},{5,20},{6,6},{7,22},{8,8},{9,24},{... | collective-permute-start | bytes 2457608 | tf_op jit(solution)/shard_map/ppermute | solution.py:45
  18.8 14.4 %collective-permute-done = bf16[400,1024]{1,0:T(8,128)(2,1)S(1)} collective-permute-done((bf16[400,1024]{1,0:T(8,128)(2,1)S(1)}, bf16[400,1024]{1,0:T(8,128)(2,1)S(1)}, u32[]{:S(2)}, u32[]{:S(2)}) %collective-permute-start) | collective-permute-done | bytes 819232 | tf_op jit(solution)/shard_map/ppermute | solution.py:45
  40.2 5.3 %all-to-all-start = ((bf16[8,8,1408]{2,1,0:T(8,128)(2,1)}), bf16[8,8,1408]{2,1,0:T(8,128)(2,1)S(1)}, u32[]{:S(2)}, u32[]{:S(2)}) async-start(bf16[8,8,1408]{2,1,0:T(8,128)(2,1)} %constant_dynamic-update-slice_fusion), calls=%async_computation | async-start | bytes 360448 | tf_op jit(solution)/shard_map/all_to_all | solution.py:435
  45.6 14.5 %all-to-all-done = bf16[8,8,1408]{2,1,0:T(8,128)(2,1)S(1)} async-done(((bf16[8,8,1408]{2,1,0:T(8,128)(2,1)}), bf16[8,8,1408]{2,1,0:T(8,128)(2,1)S(1)}, u32[]{:S(2)}, u32[]{:S(2)}) %all-to-all-start) | async-done | bytes 180256 | tf_op jit(solution)/shard_map/all_to_all | solution.py:435
  60.9 3.4 pad_maximum_fusion.own_ref
  65.2 2.8 collective-permute-start.6
  69.2 2.4 collective-permute-done.6
  74.7 4.7 %collective-permute-done.7 = bf16[4,64,896]{2,1,0:T(8,128)(2,1)S(1)} collective-permute-done((bf16[4,64,896]{2,1,0:T(8,128)(2,1)S(1)}, bf16[4,64,896]{2,1,0:T(8,128)(2,1)S(1)}, u32[]{:S(2)}, u32[]{:S(2)}) %collective-permute-start.7) | collective-permute-done | bytes 458784 | tf_op jit(solution)/shard_map/ppermute | solution.py:37
  82.5 2.8 fusion.13
  85.8 7.8 %collective-permute-done.8 = bf16[8,64,896]{2,1,0:T(8,128)(2,1)S(1)} collective-permute-done((bf16[8,64,896]{2,1,0:T(8,128)(2,1)S(1)}, bf16[8,64,896]{2,1,0:T(8,128)(2,1)S(1)}, u32[]{:S(2)}, u32[]{:S(2)}) %collective-permute-start.8) | collective-permute-done | bytes 917536 | tf_op jit(solution)/shard_map/ppermute | solution.py:37
  94.3 8.6 %project.1 = (bf16[1536,1024]{1,0:T(8,128)(2,1)}, f32[1536,384]{1,0:T(8,128)}, bf16[1536,512]{1,0:T(8,128)(2,1)S(1)}, bf16[1024,512]{1,0:T(8,128)(2,1)S(1)}) custom-call(s32[10]{0:T(128)S(1)} %pad_add_fusion.spots, bf16[1536,1024]{1,0:T(8,128)(2,1)} %pad_maximum_fusion.own_ref, bf16[1536,1024]{1,0:T(8,128)(2,1)} %collective-permute-done.4.other_ref, ...), custom_call_target="tpu_custom_call" | custom-call | flops 1610612736 | bytes 12000000 | tf_op jit(solution)/shard_map/project/pallas_call | solution.py:133
  106.5 5.9 %attend.1 = (bf16[1536,256]{1,0:T(8,128)(2,1)S(1)}, f32[2,1536]{1,0:T(2,128)S(1)}) custom-call(s32[2]{0:T(128)S(1)} %pad_add_fusion.1.ends_ref, bf16[1536,512]{1,0:T(8,128)(2,1)S(1)} %copy-done.13, bf16[1536,512]{1,0:T(8,128)(2,1)S(1)} %copy-done.13, bf16[1536,512]{1,0:T(8,128)(2,1)S(1)} %copy-done.13), custom_call_target="tpu_custom_call" | custom-call | flops 3000000000 | bytes 4000000 | tf_op jit(solution)/shard_map/attend/pallas_call | solution.py:296
  114.5 2.7 collective-permute-start.9
  117.1 3.0 collective-permute-done.9
  122.1 4.3 %collective-permute-done.14 = bf16[1,64,1152]{2,1,0:T(8,128)(2,1)S(1)} collective-permute-done((bf16[1,64,1152]{2,1,0:T(8,128)(2,1)S(1)}, bf16[1,64,1152]{2,1,0:T(8,128)(2,1)S(1)}, u32[]{:S(2)}, u32[]{:S(2)}) %collective-permute-start.14) | collective-permute-done | bytes 147488 | tf_op jit(solution)/shard_map/ppermute | solution.py:37
  126.4 2.8 collective-permute-start.15
  129.2 3.0 collective-permute-done.10
  135.1 5.4 %collective-permute-done.11 = bf16[192,1024]{1,0:T(8,128)(2,1)S(1)} collective-permute-done((bf16[192,1024]{1,0:T(8,128)(2,1)S(1)}, bf16[192,1024]{1,0:T(8,128)(2,1)S(1)}, u32[]{:S(2)}, u32[]{:S(2)}) %collective-permute-start.11) | collective-permute-done | bytes 393248 | tf_op jit(solution)/shard_map/ppermute | solution.py:37
  144.3 2.6 collective-permute-start.17
  148.9 11.1 %collective-permute-done.13 = bf16[384,1024]{1,0:T(8,128)(2,1)S(1)} collective-permute-done((bf16[384,1024]{1,0:T(8,128)(2,1)S(1)}, bf16[384,1024]{1,0:T(8,128)(2,1)S(1)}, u32[]{:S(2)}, u32[]{:S(2)}) %collective-permute-start.13) | collective-permute-done | bytes 786464 | tf_op jit(solution)/shard_map/ppermute | solution.py:37
  160.2 4.5 %collective-permute-start.18 = (bf16[768,1024]{1,0:T(8,128)(2,1)S(1)}, bf16[768,1024]{1,0:T(8,128)(2,1)S(1)}, u32[]{:S(2)}, u32[]{:S(2)}) collective-permute-start(bf16[768,1024]{1,0:T(8,128)(2,1)S(1)} %pad_maximum_fusion.3), channel_id=1, source_target_pairs={{0,1},{1,0},{2,3},{3,2},{4,5},{5,4},{6,7},{7,6},{8,9},{9,8},{10,11... | collective-permute-start | bytes 4718600 | tf_op jit(solution)/shard_map/ppermute | solution.py:37
  180.3 9.5 %collective-permute-done.20 = bf16[384,1024]{1,0:T(8,128)(2,1)S(1)} collective-permute-done((bf16[384,1024]{1,0:T(8,128)(2,1)S(1)}, bf16[384,1024]{1,0:T(8,128)(2,1)S(1)}, u32[]{:S(2)}, u32[]{:S(2)}) %collective-permute-start.20) | collective-permute-done | bytes 786464 | tf_op jit(solution)/shard_map/ppermute | solution.py:37
  195.0 3.1 collective-permute-done.21
  204.6 3.0 collective-permute-done.22
  207.7 4.1 %to_pack.1 = bf16[1536,1024]{1,0:T(8,128)(2,1)} custom-call(s32[10]{0:T(128)S(1)} %pad_add_fusion.spots, bf16[768,384]{1,0:T(8,128)(2,1)S(1)} %get-tuple-element.64.own_ref, bf16[768,384]{1,0:T(8,128)(2,1)S(1)} %get-tuple-element.65.other_ref, bf16[384,1024]{1,0:T(8,128)(2,1)S(1)} %bitcast.173), custom_call_target="tpu_custom_call" | custom-call | flops 1200000000 | bytes 12000000 | tf_op jit(solution)/shard_map/to_pack/pallas_call | solution.py:133
  211.8 7.1 %collective-permute-done.23 = bf16[384,1024]{1,0:T(8,128)(2,1)} collective-permute-done((bf16[384,1024]{1,0:T(8,128)(2,1)S(1)}, bf16[384,1024]{1,0:T(8,128)(2,1)}, u32[]{:S(2)}, u32[]{:S(2)}) %collective-permute-start.23) | collective-permute-done | bytes 786464 | tf_op jit(solution)/shard_map/ppermute | solution.py:37
  220.2 4.2 %collective-permute-start.24 = (bf16[768,1024]{1,0:T(8,128)(2,1)S(1)}, bf16[768,1024]{1,0:T(8,128)(2,1)}, u32[]{:S(2)}, u32[]{:S(2)}) collective-permute-start(bf16[768,1024]{1,0:T(8,128)(2,1)S(1)} %pad_maximum_fusion.4.own_ref), channel_id=1, source_target_pairs={{0,1},{1,0},{2,3},{3,2},{4,5},{5,4},{6,7},{7,6},{8,9},{9,8},{10,11... | collective-permute-start | bytes 4718600 | tf_op jit(solution)/shard_map/ppermute | solution.py:37
  224.4 6.3 %all-to-all-start.1 = ((bf16[16,64,1152]{2,1,0:T(8,128)(2,1)}), bf16[16,64,1152]{2,1,0:T(8,128)(2,1)}, u32[]{:S(2)}, u32[]{:S(2)}) async-start(bf16[16,64,1152]{2,1,0:T(8,128)(2,1)} %pad_maximum_fusion.1), calls=%async_computation.2 | async-start | bytes 4718592 | tf_op jit(solution)/shard_map/all_to_all | solution.py:435
  233.5 4.9 %out_back.1 = (bf16[1536,256]{1,0:T(8,128)(2,1)S(1)}, f32[256,1024]{1,0:T(8,128)S(1)}) custom-call(s32[10]{0:T(128)S(1)} %pad_add_fusion.spots, bf16[768,1024]{1,0:T(8,128)(2,1)S(1)} %pad_maximum_fusion.4.own_ref, bf16[768,1024]{1,0:T(8,128)(2,1)} %collective-permute-done.24.other_ref, bf16[1536,256]{1,0:T(8,128)(2,1)S(1)} %copy-done.15, ...), custom_call_target="tpu_custom_call" | custom-call | flops 1600000000 | bytes 12000000 | tf_op jit(solution)/shard_map/out_back/pallas_call | solution.py:133
  238.4 10.7 %attend_back.1 = (f32[1536,256]{1,0:T(8,128)S(1)}, f32[1536,128]{1,0:T(8,128)S(1)}, f32[1536,128]{1,0:T(8,128)S(1)}) custom-call(s32[2]{0:T(128)S(1)} %pad_add_fusion.1.ends_ref, bf16[1536,512]{1,0:T(8,128)(2,1)} %copy-done.12, bf16[1536,512]{1,0:T(8,128)(2,1)} %copy-done.12, bf16[1536,512]{1,0:T(8,128)(2,1)} %copy-done.12, ...), custom_call_target="tpu_custom_call" | custom-call | flops 8000000000 | bytes 8000000 | tf_op jit(solution)/shard_map/attend_back/pallas_call | solution.py:365
  252.0 15.4 %all-to-all-done.1 = bf16[16,64,1152]{2,1,0:T(8,128)(2,1)} async-done(((bf16[16,64,1152]{2,1,0:T(8,128)(2,1)}), bf16[16,64,1152]{2,1,0:T(8,128)(2,1)}, u32[]{:S(2)}, u32[]{:S(2)}) %all-to-all-start.1) | async-done | bytes 2359328 | tf_op jit(solution)/shard_map/all_to_all | solution.py:435
  267.4 12.9 %project_back.1 = (bf16[1536,512]{1,0:T(8,128)(2,1)}, f32[1,1024]{1,0:T(1,128)}, f32[2,128]{1,0:T(2,128)}, bf16[768,1024]{1,0:T(8,128)(2,1)}, bf16[768,1024]{1,0:T(8,128)(2,1)}) custom-call(s32[10]{0:T(128)} %copy-done.9, f32[1536,384]{1,0:T(8,128)} %get-tuple-element.69.pre_ref, f32[1536,256]{1,0:T(8,128)} %copy-done.4, f32[1536,128]{1,0:T(8,128)} %copy-done.7, ...), custom_call_target="tpu_custom_call" | custom-call | flops 1610612736 | bytes 12000000 | tf_op jit(solution)/shard_map/project_back/pallas_call | solution.py:133
  282.0 4.2 %fusion.2 = bf16[128,8,512]{2,1,0:T(8,128)(2,1)S(1)} fusion(bf16[1536,1024]{1,0:T(8,128)(2,1)} %get-tuple-element.77.normed_ref, bf16[1536,512]{1,0:T(8,128)(2,1)} %get-tuple-element.83), kind=kOutput, calls=%fused_computation.29 | convolution fusion | flops 1611137024 | bytes 5767168 | tf_op jit(solution)/shard_map/dot_general | solution.py:77
  287.4 7.4 %all-to-all-start.2 = ((bf16[128,8,640]{2,1,0:T(8,128)(2,1)}), bf16[128,8,640]{2,1,0:T(8,128)(2,1)}, u32[]{:S(2)}, u32[]{:S(2)}) async-start(bf16[128,8,640]{2,1,0:T(8,128)(2,1)} %fusion.3), calls=%async_computation.3 | async-start | bytes 2621440 | tf_op jit(solution)/shard_map/all_to_all | solution.py:435
  296.2 4.5 %collective-permute-start.27 = (bf16[192,1024]{1,0:T(8,128)(2,1)S(1)}, bf16[192,1024]{1,0:T(8,128)(2,1)}, u32[]{:S(2)}, u32[]{:S(2)}) collective-permute-start(bf16[192,1024]{1,0:T(8,128)(2,1)S(1)} %copy-done.21), channel_id=1, source_target_pairs={{0,0},{1,16},{2,2},{3,18},{4,4},{5,20},{6,6},{7,22},{8,8},{9,24},{... | collective-permute-start | bytes 1179656 | tf_op jit(solution)/shard_map/ppermute | solution.py:45
  301.6 15.1 %all-to-all-done.2 = bf16[128,8,640]{2,1,0:T(8,128)(2,1)} async-done(((bf16[128,8,640]{2,1,0:T(8,128)(2,1)}), bf16[128,8,640]{2,1,0:T(8,128)(2,1)}, u32[]{:S(2)}, u32[]{:S(2)}) %all-to-all-start.2) | async-done | bytes 1310752 | tf_op jit(solution)/shard_map/all_to_all | solution.py:435
  316.7 3.6 all-to-all-start.3
  323.6 3.7 convert_add_fusion
  327.3 3.4 all-to-all-done.3
  336.5 2.3 collective-permute-start.31
  341.1 3.1 collective-permute-start.34
  347.1 4.4 %collective-permute-done.33 = bf16[1,2,8,768]{3,2,1,0:T(8,128)(2,1)S(1)} collective-permute-done((bf16[1,2,8,768]{3,2,1,0:T(8,128)(2,1)S(1)}, bf16[1,2,8,768]{3,2,1,0:T(8,128)(2,1)S(1)}, u32[]{:S(2)}, u32[]{:S(2)}) %collective-permute-start.33) | collective-permute-done | bytes 24608 | tf_op jit(solution)/shard_map/ppermute | solution.py:37
  351.4 2.7 collective-permute-done.34
  357.5 4.5 %collective-permute-start.29 = (bf16[192,1024]{1,0:T(8,128)(2,1)}, bf16[192,1024]{1,0:T(8,128)(2,1)S(1)}, u32[]{:S(2)}, u32[]{:S(2)}) collective-permute-start(bf16[192,1024]{1,0:T(8,128)(2,1)} %get-tuple-element.102), channel_id=1, source_target_pairs={{0,0},{1,16},{2,2},{3,18},{4,4},{5,20},{6,6},{7,22},{8,8},{9,24},{... | collective-permute-start | bytes 1179656 | tf_op jit(solution)/shard_map/ppermute | solution.py:45
  362.0 2.6 collective-permute-start.30
  368.9 3.5 collective-permute-done.29
  374.9 4.5 %collective-permute-start.26 = (bf16[192,1024]{1,0:T(8,128)(2,1)S(1)}, bf16[192,1024]{1,0:T(8,128)(2,1)S(1)}, u32[]{:S(2)}, u32[]{:S(2)}) collective-permute-start(bf16[192,1024]{1,0:T(8,128)(2,1)S(1)} %add_convert_fusion.2), channel_id=1, source_target_pairs={{0,0},{1,16},{2,2},{3,18},{4,4},{5,20},{6,6},{7,22},{8,8},{9,24},{... | collective-permute-start | bytes 1179656 | tf_op jit(solution)/shard_map/ppermute | solution.py:45
  381.8 3.7 collective-permute-done.26
  (262 shorter events, 103.2 us)
Async XLA Ops:
  7.2 113.9 %copy-start = (bf16[24,1024]{1,0:T(8,128)(2,1)S(1)}, bf16[24,1024]{1,0:T(8,128)(2,1)}, u32[]{:S(2)}) copy-start(bf16[24,1024]{1,0:T(8,128)(2,1)} %param.23) | copy-start | bytes 147460
  8.5 24.7 %collective-permute-start = (bf16[400,1024]{1,0:T(8,128)(2,1)S(1)}, bf16[400,1024]{1,0:T(8,128)(2,1)S(1)}, u32[]{:S(2)}, u32[]{:S(2)}) collective-permute-start(bf16[400,1024]{1,0:T(8,128)(2,1)S(1)} %pad_maximum_fusion.7), channel_id=1, source_target_pairs={{0,0},{1,16},{2,2},{3,18},{4,4},{5,20},{6,6},{7,22},{8,8},{9,24},{... | collective-permute-start | bytes 2457608 | tf_op jit(solution)/shard_map/ppermute | solution.py:45
  16.5 18.6 %collective-permute-start.2 = (bf16[384,1024]{1,0:T(8,128)(2,1)}, bf16[384,1024]{1,0:T(8,128)(2,1)S(1)}, u32[]{:S(2)}, u32[]{:S(2)}) collective-permute-start(bf16[384,1024]{1,0:T(8,128)(2,1)} %pad_maximum_fusion.8), channel_id=1, source_target_pairs={{32,0},{112,1},{34,2},{114,3},{36,4},{116,5},{38,6},{118,7},{40,8}... | collective-permute-start | bytes 2359304 | tf_op jit(solution)/shard_map/ppermute | solution.py:49
  33.2 26.8 %copy-start.22 = (bf16[400,1024]{1,0:T(8,128)(2,1)}, bf16[400,1024]{1,0:T(8,128)(2,1)S(1)}, u32[]{:S(2)}) copy-start(bf16[400,1024]{1,0:T(8,128)(2,1)S(1)} %collective-permute-done) | copy-start | bytes 2457604
  33.3 12.1 %copy-start.36 = (s32[1,3]{1,0:T(1,128)S(1)}, s32[1,3]{1,0:T(1,128)}, u32[]{:S(2)}) copy-start(s32[1,3]{1,0:T(1,128)} %param.16) | copy-start | bytes 40
  36.4 24.5 %collective-permute-start.3 = (bf16[768,1024]{1,0:T(8,128)(2,1)}, bf16[768,1024]{1,0:T(8,128)(2,1)}, u32[]{:S(2)}, u32[]{:S(2)}) collective-permute-start(bf16[768,1024]{1,0:T(8,128)(2,1)} %pad_maximum_fusion.2), channel_id=1, source_target_pairs={{0,96},{1,33},{2,98},{3,35},{4,100},{5,37},{6,102},{7,39},{8,104},... | collective-permute-start | bytes 4718600 | tf_op jit(solution)/shard_map/ppermute | solution.py:37
  40.2 19.8 %all-to-all-start = ((bf16[8,8,1408]{2,1,0:T(8,128)(2,1)}), bf16[8,8,1408]{2,1,0:T(8,128)(2,1)S(1)}, u32[]{:S(2)}, u32[]{:S(2)}) async-start(bf16[8,8,1408]{2,1,0:T(8,128)(2,1)} %constant_dynamic-update-slice_fusion), calls=%async_computation | async-start | bytes 360448 | tf_op jit(solution)/shard_map/all_to_all | solution.py:435
  45.5 26.6 %collective-permute-start.1 = (s32[1,3]{1,0:T(1,128)S(1)}, s32[1,3]{1,0:T(1,128)S(1)}, u32[]{:S(2)}, u32[]{:S(2)}) collective-permute-start(s32[1,3]{1,0:T(1,128)S(1)} %copy-done.36), channel_id=1, source_target_pairs={{0,1},{1,0},{2,3},{3,2},{4,5},{5,4},{6,7},{7,6},{8,9},{9,8},{10,11... | collective-permute-start | bytes 44 | tf_op jit(solution)/shard_map/ppermute | solution.py:37
  60.1 5.0 %collective-permute-start.5 = (bf16[1,64,896]{2,1,0:T(8,128)(2,1)S(1)}, bf16[1,64,896]{2,1,0:T(8,128)(2,1)S(1)}, u32[]{:S(2)}, u32[]{:S(2)}) collective-permute-start(bf16[1,64,896]{2,1,0:T(8,128)(2,1)S(1)} %maximum_bitcast_fusion.1), channel_id=1, source_target_pairs={{0,2},{1,9},{2,0},{3,11},{4,6},{5,13},{6,4},{7,15},{8,10},{9,1},{1... | collective-permute-start | bytes 344072 | tf_op jit(solution)/shard_map/ppermute | solution.py:37
  64.3 30.0 %collective-permute-start.4 = (bf16[1536,1024]{1,0:T(8,128)(2,1)}, bf16[1536,1024]{1,0:T(8,128)(2,1)}, u32[]{:S(2)}, u32[]{:S(2)}) collective-permute-start(bf16[1536,1024]{1,0:T(8,128)(2,1)} %pad_maximum_fusion.own_ref), channel_id=1, source_target_pairs={{0,1},{1,0},{2,3},{3,2},{4,5},{5,4},{6,7},{7,6},{8,9},{9,8},{10,11... | collective-permute-start | bytes 9437192 | tf_op jit(solution)/shard_map/ppermute | solution.py:37
  65.2 6.5 %collective-permute-start.6 = (bf16[2,64,896]{2,1,0:T(8,128)(2,1)S(1)}, bf16[2,64,896]{2,1,0:T(8,128)(2,1)S(1)}, u32[]{:S(2)}, u32[]{:S(2)}) collective-permute-start(bf16[2,64,896]{2,1,0:T(8,128)(2,1)S(1)} %maximum_select_fusion.7), channel_id=1, source_target_pairs={{0,6},{1,25},{2,4},{3,27},{4,2},{5,29},{6,0},{7,31},{8,14},{9,17},... | collective-permute-start | bytes 688136 | tf_op jit(solution)/shard_map/ppermute | solution.py:37
  71.7 7.7 %collective-permute-start.7 = (bf16[4,64,896]{2,1,0:T(8,128)(2,1)S(1)}, bf16[4,64,896]{2,1,0:T(8,128)(2,1)S(1)}, u32[]{:S(2)}, u32[]{:S(2)}) collective-permute-start(bf16[4,64,896]{2,1,0:T(8,128)(2,1)S(1)} %maximum_select_fusion.5), channel_id=1, source_target_pairs={{0,8},{1,3},{2,10},{3,1},{4,12},{5,7},{6,14},{7,5},{8,0},{9,11},{1... | collective-permute-start | bytes 1376264 | tf_op jit(solution)/shard_map/ppermute | solution.py:37
  72.1 160.3 %copy-start.9 = (s32[10]{0:T(128)}, s32[10]{0:T(128)S(1)}, u32[]{:S(2)}) copy-start(s32[10]{0:T(128)S(1)} %pad_add_fusion.spots) | copy-start | bytes 124
  79.6 14.0 %collective-permute-start.8 = (bf16[8,64,896]{2,1,0:T(8,128)(2,1)S(1)}, bf16[8,64,896]{2,1,0:T(8,128)(2,1)S(1)}, u32[]{:S(2)}, u32[]{:S(2)}) collective-permute-start(bf16[8,64,896]{2,1,0:T(8,128)(2,1)S(1)} %maximum_select_fusion.3), channel_id=1, source_target_pairs={{0,24},{1,7},{2,26},{3,5},{4,28},{5,3},{6,30},{7,1},{8,16},{9,15},... | collective-permute-start | bytes 2752520 | tf_op jit(solution)/shard_map/ppermute | solution.py:37
  114.5 5.7 %collective-permute-start.9 = (bf16[768,1024]{1,0:T(8,128)(2,1)S(1)}, bf16[768,1024]{1,0:T(8,128)(2,1)S(1)}, u32[]{:S(2)}, u32[]{:S(2)}) collective-permute-start(bf16[768,1024]{1,0:T(8,128)(2,1)S(1)} %get-tuple-element.54), channel_id=1, source_target_pairs={{0,1},{1,0},{2,3},{3,2},{4,5},{5,4},{6,7},{7,6},{8,9},{9,8},{10,11... | collective-permute-start | bytes 4718600 | tf_op jit(solution)/shard_map/ppermute | solution.py:37
  121.0 11.2 %collective-permute-start.10 = (bf16[384,1024]{1,0:T(8,128)(2,1)S(1)}, bf16[384,1024]{1,0:T(8,128)(2,1)S(1)}, u32[]{:S(2)}, u32[]{:S(2)}) collective-permute-start(bf16[384,1024]{1,0:T(8,128)(2,1)S(1)} %slice.283), channel_id=1, source_target_pairs={{0,96},{1,33},{2,98},{3,35},{4,100},{5,37},{6,102},{7,39},{8,104},... | collective-permute-start | bytes 2359304 | tf_op jit(solution)/shard_map/ppermute | solution.py:37
  121.8 4.6 %collective-permute-start.14 = (bf16[1,64,1152]{2,1,0:T(8,128)(2,1)S(1)}, bf16[1,64,1152]{2,1,0:T(8,128)(2,1)S(1)}, u32[]{:S(2)}, u32[]{:S(2)}) collective-permute-start(bf16[1,64,1152]{2,1,0:T(8,128)(2,1)S(1)} %maximum_bitcast_fusion), channel_id=1, source_target_pairs={{0,2},{1,9},{2,0},{3,11},{4,6},{5,13},{6,4},{7,15},{8,10},{9,1},{1... | collective-permute-start | bytes 442376 | tf_op jit(solution)/shard_map/ppermute | solution.py:37
  126.4 8.4 %collective-permute-start.15 = (bf16[2,64,1152]{2,1,0:T(8,128)(2,1)S(1)}, bf16[2,64,1152]{2,1,0:T(8,128)(2,1)S(1)}, u32[]{:S(2)}, u32[]{:S(2)}) collective-permute-start(bf16[2,64,1152]{2,1,0:T(8,128)(2,1)S(1)} %maximum_select_fusion.6), channel_id=1, source_target_pairs={{0,6},{1,25},{2,4},{3,27},{4,2},{5,29},{6,0},{7,31},{8,14},{9,17},... | collective-permute-start | bytes 884744 | tf_op jit(solution)/shard_map/ppermute | solution.py:37
  132.6 7.9 %collective-permute-start.11 = (bf16[192,1024]{1,0:T(8,128)(2,1)S(1)}, bf16[192,1024]{1,0:T(8,128)(2,1)S(1)}, u32[]{:S(2)}, u32[]{:S(2)}) collective-permute-start(bf16[192,1024]{1,0:T(8,128)(2,1)S(1)} %slice.285), channel_id=1, source_target_pairs={{0,32},{1,97},{2,34},{3,99},{4,36},{5,101},{6,38},{7,103},{8,40},{... | collective-permute-start | bytes 1179656 | tf_op jit(solution)/shard_map/ppermute | solution.py:37
  135.0 9.1 %collective-permute-start.16 = (bf16[4,64,1152]{2,1,0:T(8,128)(2,1)S(1)}, bf16[4,64,1152]{2,1,0:T(8,128)(2,1)S(1)}, u32[]{:S(2)}, u32[]{:S(2)}) collective-permute-start(bf16[4,64,1152]{2,1,0:T(8,128)(2,1)S(1)} %maximum_select_fusion.4), channel_id=1, source_target_pairs={{0,8},{1,3},{2,10},{3,1},{4,12},{5,7},{6,14},{7,5},{8,0},{9,11},{1... | collective-permute-start | bytes 1769480 | tf_op jit(solution)/shard_map/ppermute | solution.py:37
  140.7 57.8 %copy-start.16 = (f32[192,1024]{1,0:T(8,128)}, f32[192,1024]{1,0:T(8,128)S(1)}, u32[]{:S(2)}) copy-start(f32[192,1024]{1,0:T(8,128)S(1)} %get-tuple-element.95) | copy-start | bytes 2359300
  140.9 7.9 %collective-permute-start.12 = (bf16[192,1024]{1,0:T(8,128)(2,1)S(1)}, bf16[192,1024]{1,0:T(8,128)(2,1)S(1)}, u32[]{:S(2)}, u32[]{:S(2)}) collective-permute-start(bf16[192,1024]{1,0:T(8,128)(2,1)S(1)} %multiply_convert_fusion.6), channel_id=1, source_target_pairs={{0,32},{1,97},{2,34},{3,99},{4,36},{5,101},{6,38},{7,103},{8,40},{... | collective-permute-start | bytes 1179656 | tf_op jit(solution)/shard_map/ppermute | solution.py:37
  144.3 21.9 %collective-permute-start.17 = (bf16[8,64,1152]{2,1,0:T(8,128)(2,1)S(1)}, bf16[8,64,1152]{2,1,0:T(8,128)(2,1)S(1)}, u32[]{:S(2)}, u32[]{:S(2)}) collective-permute-start(bf16[8,64,1152]{2,1,0:T(8,128)(2,1)S(1)} %maximum_select_fusion.2), channel_id=1, source_target_pairs={{0,24},{1,7},{2,26},{3,5},{4,28},{5,3},{6,30},{7,1},{8,16},{9,15},... | collective-permute-start | bytes 3538952 | tf_op jit(solution)/shard_map/ppermute | solution.py:37
  148.8 11.2 %collective-permute-start.13 = (bf16[384,1024]{1,0:T(8,128)(2,1)S(1)}, bf16[384,1024]{1,0:T(8,128)(2,1)S(1)}, u32[]{:S(2)}, u32[]{:S(2)}) collective-permute-start(bf16[384,1024]{1,0:T(8,128)(2,1)S(1)} %pad_maximum_fusion.11), channel_id=1, source_target_pairs={{0,96},{1,33},{2,98},{3,35},{4,100},{5,37},{6,102},{7,39},{8,104},... | collective-permute-start | bytes 2359304 | tf_op jit(solution)/shard_map/ppermute | solution.py:37
  160.2 7.5 %collective-permute-start.18 = (bf16[768,1024]{1,0:T(8,128)(2,1)S(1)}, bf16[768,1024]{1,0:T(8,128)(2,1)S(1)}, u32[]{:S(2)}, u32[]{:S(2)}) collective-permute-start(bf16[768,1024]{1,0:T(8,128)(2,1)S(1)} %pad_maximum_fusion.3), channel_id=1, source_target_pairs={{0,1},{1,0},{2,3},{3,2},{4,5},{5,4},{6,7},{7,6},{8,9},{9,8},{10,11... | collective-permute-start | bytes 4718600 | tf_op jit(solution)/shard_map/ppermute | solution.py:37
  171.9 4.8 %collective-permute-start.19 = (bf16[768,1024]{1,0:T(8,128)(2,1)S(1)}, bf16[768,1024]{1,0:T(8,128)(2,1)S(1)}, u32[]{:S(2)}, u32[]{:S(2)}) collective-permute-start(bf16[768,1024]{1,0:T(8,128)(2,1)S(1)} %convolution_convert_fusion), channel_id=1, source_target_pairs={{0,1},{1,0},{2,3},{3,2},{4,5},{5,4},{6,7},{7,6},{8,9},{9,8},{10,11... | collective-permute-start | bytes 4718600 | tf_op jit(solution)/shard_map/ppermute | solution.py:37
  178.2 11.6 %collective-permute-start.20 = (bf16[384,1024]{1,0:T(8,128)(2,1)S(1)}, bf16[384,1024]{1,0:T(8,128)(2,1)S(1)}, u32[]{:S(2)}, u32[]{:S(2)}) collective-permute-start(bf16[384,1024]{1,0:T(8,128)(2,1)S(1)} %slice.282), channel_id=1, source_target_pairs={{0,96},{1,33},{2,98},{3,35},{4,100},{5,37},{6,102},{7,39},{8,104},... | collective-permute-start | bytes 2359304 | tf_op jit(solution)/shard_map/ppermute | solution.py:37
  190.2 7.9 %collective-permute-start.21 = (bf16[192,1024]{1,0:T(8,128)(2,1)S(1)}, bf16[192,1024]{1,0:T(8,128)(2,1)S(1)}, u32[]{:S(2)}, u32[]{:S(2)}) collective-permute-start(bf16[192,1024]{1,0:T(8,128)(2,1)S(1)} %slice.284), channel_id=1, source_target_pairs={{0,32},{1,97},{2,34},{3,99},{4,36},{5,101},{6,38},{7,103},{8,40},{... | collective-permute-start | bytes 1179656 | tf_op jit(solution)/shard_map/ppermute | solution.py:37
  199.7 19.2 %copy-start.20 = (bf16[192,1024]{1,0:T(8,128)(2,1)}, bf16[192,1024]{1,0:T(8,128)(2,1)S(1)}, u32[]{:S(2)}) copy-start(bf16[192,1024]{1,0:T(8,128)(2,1)S(1)} %get-tuple-element.82) | copy-start | bytes 1179652
  199.7 7.8 %collective-permute-start.22 = (bf16[192,1024]{1,0:T(8,128)(2,1)S(1)}, bf16[192,1024]{1,0:T(8,128)(2,1)S(1)}, u32[]{:S(2)}, u32[]{:S(2)}) collective-permute-start(bf16[192,1024]{1,0:T(8,128)(2,1)S(1)} %get-tuple-element.82), channel_id=1, source_target_pairs={{0,32},{1,97},{2,34},{3,99},{4,36},{5,101},{6,38},{7,103},{8,40},{... | collective-permute-start | bytes 1179656 | tf_op jit(solution)/shard_map/ppermute | solution.py:37
  207.6 11.3 %collective-permute-start.23 = (bf16[384,1024]{1,0:T(8,128)(2,1)S(1)}, bf16[384,1024]{1,0:T(8,128)(2,1)}, u32[]{:S(2)}, u32[]{:S(2)}) collective-permute-start(bf16[384,1024]{1,0:T(8,128)(2,1)S(1)} %pad_maximum_fusion.12), channel_id=1, source_target_pairs={{0,96},{1,33},{2,98},{3,35},{4,100},{5,37},{6,102},{7,39},{8,104},... | collective-permute-start | bytes 2359304 | tf_op jit(solution)/shard_map/ppermute | solution.py:37
  220.2 12.2 %collective-permute-start.24 = (bf16[768,1024]{1,0:T(8,128)(2,1)S(1)}, bf16[768,1024]{1,0:T(8,128)(2,1)}, u32[]{:S(2)}, u32[]{:S(2)}) collective-permute-start(bf16[768,1024]{1,0:T(8,128)(2,1)S(1)} %pad_maximum_fusion.4.own_ref), channel_id=1, source_target_pairs={{0,1},{1,0},{2,3},{3,2},{4,5},{5,4},{6,7},{7,6},{8,9},{9,8},{10,11... | collective-permute-start | bytes 4718600 | tf_op jit(solution)/shard_map/ppermute | solution.py:37
  224.4 43.0 %all-to-all-start.1 = ((bf16[16,64,1152]{2,1,0:T(8,128)(2,1)}), bf16[16,64,1152]{2,1,0:T(8,128)(2,1)}, u32[]{:S(2)}, u32[]{:S(2)}) async-start(bf16[16,64,1152]{2,1,0:T(8,128)(2,1)} %pad_maximum_fusion.1), calls=%async_computation.2 | async-start | bytes 4718592 | tf_op jit(solution)/shard_map/all_to_all | solution.py:435
  230.8 143.0 %reduce-scatter.2.cloned.1.call-start = ((), (), s32[]{:S(2)}) async-start(), calls=%async_computation.5 | async-start | bytes 3538944 | tf_op jit(solution)/shard_map/reduce_scatter | solution.py:630
  287.4 29.3 %all-to-all-start.2 = ((bf16[128,8,640]{2,1,0:T(8,128)(2,1)}), bf16[128,8,640]{2,1,0:T(8,128)(2,1)}, u32[]{:S(2)}, u32[]{:S(2)}) async-start(bf16[128,8,640]{2,1,0:T(8,128)(2,1)} %fusion.3), calls=%async_computation.3 | async-start | bytes 2621440 | tf_op jit(solution)/shard_map/all_to_all | solution.py:435
  294.8 28.8 %collective-permute-start.25 = (bf16[768,1024]{1,0:T(8,128)(2,1)}, bf16[768,1024]{1,0:T(8,128)(2,1)}, u32[]{:S(2)}, u32[]{:S(2)}) collective-permute-start(bf16[768,1024]{1,0:T(8,128)(2,1)} %get-tuple-element.80), channel_id=1, source_target_pairs={{0,1},{1,0},{2,3},{3,2},{4,5},{5,4},{6,7},{7,6},{8,9},{9,8},{10,11... | collective-permute-start | bytes 4718600 | tf_op jit(solution)/shard_map/ppermute | solution.py:37
  296.2 83.2 %collective-permute-start.27 = (bf16[192,1024]{1,0:T(8,128)(2,1)S(1)}, bf16[192,1024]{1,0:T(8,128)(2,1)}, u32[]{:S(2)}, u32[]{:S(2)}) collective-permute-start(bf16[192,1024]{1,0:T(8,128)(2,1)S(1)} %copy-done.21), channel_id=1, source_target_pairs={{0,0},{1,16},{2,2},{3,18},{4,4},{5,20},{6,6},{7,22},{8,8},{9,24},{... | collective-permute-start | bytes 1179656 | tf_op jit(solution)/shard_map/ppermute | solution.py:45
  301.6 22.0 %copy-start.25 = (bf16[768,1024]{1,0:T(8,128)(2,1)S(1)}, bf16[768,1024]{1,0:T(8,128)(2,1)}, u32[]{:S(2)}) copy-start(bf16[768,1024]{1,0:T(8,128)(2,1)} %get-tuple-element.79) | copy-start | bytes 4718596
  316.7 14.0 %all-to-all-start.3 = ((bf16[16,16,1024]{2,1,0:T(8,128)(2,1)}), bf16[16,16,1024]{2,1,0:T(8,128)(2,1)S(1)}, u32[]{:S(2)}, u32[]{:S(2)}) async-start(bf16[16,16,1024]{2,1,0:T(8,128)(2,1)} %bitcast.73), calls=%async_computation.4 | async-start | bytes 1048576 | tf_op jit(solution)/shard_map/all_to_all | solution.py:435
  332.7 7.0 %collective-permute-start.32 = (bf16[4,1,8,768]{3,2,1,0:T(8,128)(2,1)S(1)}, bf16[4,1,8,768]{3,2,1,0:T(8,128)(2,1)S(1)}, u32[]{:S(2)}, u32[]{:S(2)}) collective-permute-start(bf16[4,1,8,768]{3,2,1,0:T(8,128)(2,1)S(1)} %constant_dynamic-slice_fusion), channel_id=1, source_target_pairs={{0,1},{1,0},{2,3},{3,2},{4,5},{5,4},{6,7},{7,6},{8,9},{9,8},{10,11... | collective-permute-start | bytes 147464 | tf_op jit(solution)/shard_map/ppermute | solution.py:37
  336.5 7.7 %collective-permute-start.31 = (bf16[16,1024]{1,0:T(8,128)(2,1)S(1)}, bf16[16,1024]{1,0:T(8,128)(2,1)S(1)}, u32[]{:S(2)}, u32[]{:S(2)}) collective-permute-start(bf16[16,1024]{1,0:T(8,128)(2,1)S(1)} %convert_element_type.195), channel_id=1, source_target_pairs={{0,0},{1,16},{2,2},{3,18},{4,4},{5,20},{6,6},{7,22},{8,8},{9,24},{... | collective-permute-start | bytes 98312 | tf_op jit(solution)/shard_map/ppermute | solution.py:45
  339.5 15.3 %collective-permute-start.28 = (bf16[384,1024]{1,0:T(8,128)(2,1)S(1)}, bf16[384,1024]{1,0:T(8,128)(2,1)S(1)}, u32[]{:S(2)}, u32[]{:S(2)}) collective-permute-start(bf16[384,1024]{1,0:T(8,128)(2,1)S(1)} %slice.281), channel_id=1, source_target_pairs={{0,96},{1,33},{2,98},{3,35},{4,100},{5,37},{6,102},{7,39},{8,104},... | collective-permute-start | bytes 2359304 | tf_op jit(solution)/shard_map/ppermute | solution.py:37
  339.7 11.7 %collective-permute-start.33 = (bf16[1,2,8,768]{3,2,1,0:T(8,128)(2,1)S(1)}, bf16[1,2,8,768]{3,2,1,0:T(8,128)(2,1)S(1)}, u32[]{:S(2)}, u32[]{:S(2)}) collective-permute-start(bf16[1,2,8,768]{3,2,1,0:T(8,128)(2,1)S(1)} %get-tuple-element.111), channel_id=1, source_target_pairs={{0,32},{1,33},{2,34},{3,35},{4,36},{5,37},{6,38},{7,39},{8,40},{9,... | collective-permute-start | bytes 73736 | tf_op jit(solution)/shard_map/ppermute | solution.py:37
  341.1 13.0 %collective-permute-start.34 = (bf16[1,2,8,768]{3,2,1,0:T(8,128)(2,1)S(1)}, bf16[1,2,8,768]{3,2,1,0:T(8,128)(2,1)S(1)}, u32[]{:S(2)}, u32[]{:S(2)}) collective-permute-start(bf16[1,2,8,768]{3,2,1,0:T(8,128)(2,1)S(1)} %get-tuple-element.112), channel_id=1, source_target_pairs={{0,64},{1,65},{2,66},{3,67},{4,68},{5,69},{6,70},{7,71},{8,72},{9,... | collective-permute-start | bytes 73736 | tf_op jit(solution)/shard_map/ppermute | solution.py:37
  344.2 9.9 %collective-permute-start.35 = (bf16[1,2,8,768]{3,2,1,0:T(8,128)(2,1)S(1)}, bf16[1,2,8,768]{3,2,1,0:T(8,128)(2,1)S(1)}, u32[]{:S(2)}, u32[]{:S(2)}) collective-permute-start(bf16[1,2,8,768]{3,2,1,0:T(8,128)(2,1)S(1)} %get-tuple-element.113), channel_id=1, source_target_pairs={{0,96},{1,97},{2,98},{3,99},{4,100},{5,101},{6,102},{7,103},{8,104... | collective-permute-start | bytes 73736 | tf_op jit(solution)/shard_map/ppermute | solution.py:37
  357.5 15.0 %collective-permute-start.29 = (bf16[192,1024]{1,0:T(8,128)(2,1)}, bf16[192,1024]{1,0:T(8,128)(2,1)S(1)}, u32[]{:S(2)}, u32[]{:S(2)}) collective-permute-start(bf16[192,1024]{1,0:T(8,128)(2,1)} %get-tuple-element.102), channel_id=1, source_target_pairs={{0,0},{1,16},{2,2},{3,18},{4,4},{5,20},{6,6},{7,22},{8,8},{9,24},{... | collective-permute-start | bytes 1179656 | tf_op jit(solution)/shard_map/ppermute | solution.py:45
  362.0 10.5 %collective-permute-start.30 = (bf16[192,1024]{1,0:T(8,128)(2,1)}, bf16[192,1024]{1,0:T(8,128)(2,1)}, u32[]{:S(2)}, u32[]{:S(2)}) collective-permute-start(bf16[192,1024]{1,0:T(8,128)(2,1)} %get-tuple-element.103), channel_id=1, source_target_pairs={{0,32},{1,112},{2,34},{3,114},{4,36},{5,116},{6,38},{7,118},{8,40}... | collective-permute-start | bytes 1179656 | tf_op jit(solution)/shard_map/ppermute | solution.py:55
  374.9 10.6 %collective-permute-start.26 = (bf16[192,1024]{1,0:T(8,128)(2,1)S(1)}, bf16[192,1024]{1,0:T(8,128)(2,1)S(1)}, u32[]{:S(2)}, u32[]{:S(2)}) collective-permute-start(bf16[192,1024]{1,0:T(8,128)(2,1)S(1)} %add_convert_fusion.2), channel_id=1, source_target_pairs={{0,0},{1,16},{2,2},{3,18},{4,4},{5,20},{6,6},{7,22},{8,8},{9,24},{... | collective-permute-start | bytes 1179656 | tf_op jit(solution)/shard_map/ppermute | solution.py:45
  (32 other events, 186.4 us)
Sparse Core Ops, SparseCore 0:
  234.0 34.3 reduce-scatter.1
where the time goes:
time: 399 us; the launch traced here: 393 us
  waiting for transfers between devices  146 us (37%)
  starting transfers between devices  93.7 us (23%)
  Pallas kernels  49.2 us (12%)
  other arithmetic  37.8 us (9%)
  local copies, waits for them, and re-layouts  32.3 us (8%)
  matrix products  17.1 us (4%)
  between operations  16.8 us (4%)
    ppermute x29, waiting for transfers between devices, swap(): lax.ppermute(values, AXES, [(k, k ^ masks[k & 1]) for k in range(DEVICES)])  74.6 us
    all_to_all x4, waiting for transfers between devices, exchange(): return lax.all_to_all(values, axes, split_axis=0, concat_axis=0, tiled=True)  48.4 us
    ppermute x29, starting transfers between devices, swap(): lax.ppermute(values, AXES, [(k, k ^ masks[k & 1]) for k in range(DEVICES)])  44.6 us
    pallas_call x5, Pallas kernels, ring_call(): pl.pallas_call(kernel, grid_spec=pltpu.PrefetchScalarGridSpec(num_scalar_...  32.6 us
    ppermute x5, starting transfers between devices, cross(): return lax.ppermute(values, AXES, [(k, crossed(k)) for k in range(DEVICES)])  22.8 us
    all_to_all x4, starting transfers between devices, exchange(): return lax.all_to_all(values, axes, split_axis=0, concat_axis=0, tiled=True)  22.6 us
    ppermute x5, waiting for transfers between devices, cross(): return lax.ppermute(values, AXES, [(k, crossed(k)) for k in range(DEVICES)])  21.7 us
    unnamed x85, local copies, waits for them, and re-layouts  12.4 us
  transfers between devices with their start and end apart: 41, of which 25 were waited for; matrix products, arithmetic and copies ran while one was open for 17% of the time, Pallas kernels for 8%

commit v1 on v0

--- a/solution.py
+++ b/solution.py
@@ -20,7 +20,6 @@
 LOG2E = 1.4426950408889634
 SCALE = HEAD ** (-0.5)
 VMEM_LIMIT = 48 * 1024 * 1024
-VMEM_MOST = 58 * 1024 * 1024
 
 AXES = ("x", "zh", "zl", "y", "core")
 RING = ("x", "core")
@@ -104,10 +103,10 @@
     return grad * cosine + pltpu.roll(grad * sine, 64, 1)
 
 
-def ring_specs(columns, stride=1):
+def ring_specs(columns):
     return [
-        pl.BlockSpec((TOK, columns), lambda x, spots: (spots[x] * stride, 0)),
-        pl.BlockSpec((TOK, columns), lambda x, spots: (spots[4 + x] * stride, 0)),
+        pl.BlockSpec((TOK, columns), lambda x, spots: (spots[x], 0)),
+        pl.BlockSpec((TOK, columns), lambda x, spots: (spots[4 + x], 0)),
     ]
 
 
@@ -127,9 +126,21 @@
     return pl.ds(pl.multiple_of((1 - spots[8]) * TOK, TOK), TOK)
 
 
-def ring_call(
-    kernel, name, in_specs, out_specs, out_shape, flops, spots, *operands, scratch=(), limit=VMEM_LIMIT
-):
+def shaped(shape, dtype, kept=False):
+    return pltpu.HBM(shape, dtype) if kept else jax.ShapeDtypeStruct(shape, dtype)
+
+
+def in_hbm(array):
+    return pltpu.with_memory_space_constraint(array, pltpu.HBM)
+
+
+def cost(microseconds):
+    return pl.CostEstimate(
+        flops=0, bytes_accessed=int(microseconds * 3.6e6), transcendentals=0
+    )
+
+
+def ring_call(kernel, name, in_specs, out_specs, out_shape, time, spots, *operands, scratch=()):
     return pl.pallas_call(
         kernel,
         grid_spec=pltpu.PrefetchScalarGridSpec(
@@ -139,16 +150,16 @@
             out_specs=out_specs,
             scratch_shapes=scratch,
         ),
-        out_shape=[jax.ShapeDtypeStruct(shape, dtype) for shape, dtype in out_shape],
-        compiler_params=pltpu.CompilerParams(vmem_limit_bytes=limit),
-        cost_estimate=pl.CostEstimate(flops=flops, bytes_accessed=12000000, transcendentals=0),
+        out_shape=out_shape,
+        compiler_params=pltpu.CompilerParams(vmem_limit_bytes=VMEM_LIMIT),
+        cost_estimate=cost(time),
         name=name,
     )(spots, *operands)
 
 
 def qkv_kernel(
     spots, own_ref, other_ref, heads_ref, ga_ref, gq_ref, gk_ref, cos_ref, sin_ref,
-    normed_ref, pre_ref, qkv_ref, w_ref,
+    normed_ref, pre_ref, qkv_ref, kept_ref, across_ref, w_ref,
 ):
     @pl.when(pl.program_id(0) == 0)
     def _():
@@ -158,6 +169,7 @@
                 for x in range(4):
                     row = (x * 16 + z * 4 + y) * 16
                     w_ref[row : row + 16, :] = heads_ref[block, x * 16 : x * 16 + 16, :512]
+        across_ref[...] = w_ref[...].T
 
     for ref, rows in ((own_ref, own_rows(spots)), (other_ref, other_rows(spots))):
         x = wide(ref[...])
@@ -171,37 +183,53 @@
         normal = u * norm_scale(u) * gain
         qkv_ref[:, h * HEAD : (h + 1) * HEAD] = low(rope(normal, cosine, sine))
     qkv_ref[:, 3 * HEAD :] = low(pre[:, 3 * HEAD :])
+    kept_ref[...] = qkv_ref[...]
 
 
 def project(spots, own, other, heads, gain_attn, gain_query, gain_key, cosine, sine):
     return ring_call(
         qkv_kernel,
         "project",
-        ring_specs(WIDTH, 2)
+        ring_specs(WIDTH)
         + [pl.BlockSpec(heads.shape, lambda x, spots: (0, 0, 0))]
         + [whole_spec((1, WIDTH)), whole_spec((1, HEAD)), whole_spec((1, HEAD))]
         + [pack_spec(HEAD), pack_spec(HEAD)],
-        [pack_spec(WIDTH), pack_spec(3 * HEAD), pack_spec(512), whole_spec((WIDTH, 512))],
+        [pack_spec(WIDTH), pack_spec(3 * HEAD), pack_spec(512), pack_spec(512)]
+        + [whole_spec((512, WIDTH))],
         [
-            ((PACK, WIDTH), jnp.bfloat16),
-            ((PACK, 3 * HEAD), jnp.float32),
-            ((PACK, 512), jnp.bfloat16),
-            ((WIDTH, 512), jnp.bfloat16),
+            shaped((PACK, WIDTH), jnp.bfloat16, True),
+            shaped((PACK, 3 * HEAD), jnp.float32, True),
+            shaped((PACK, 512), jnp.bfloat16),
+            shaped((PACK, 512), jnp.bfloat16, True),
+            shaped((512, WIDTH), jnp.bfloat16, True),
         ],
-        1610612736, spots, own, other, heads, gain_attn, gain_query, gain_key, cosine, sine,
-    )
-
-
-def to_ring_kernel(spots, rows_ref, w_ref, own_ref, other_ref):
+        8, spots, own, other, heads, gain_attn, gain_query, gain_key, cosine, sine,
+        scratch=[pltpu.VMEM((WIDTH, 512), jnp.bfloat16)],
+    )
+
+
+def to_ring_kernel(spots, rows_ref, heads_ref, own_ref, other_ref, w_ref):
+    @pl.when(pl.program_id(0) == 0)
+    def _():
+        for z in range(4):
+            for y in range(4):
+                block = jnp.where(spots[9] == 1, y * 4 + z, z * 4 + y)
+                row = (z % 2 * 8 + y * 2 + z // 2) * 16
+                for n in range(4):
+                    piece = heads_ref[block, n * 16 : n * 16 + 16, 640:]
+                    w_ref[row : row + 16, n * 256 : n * 256 + 256] = piece
+
     own_ref[...] = low(dot(rows_ref[own_rows(spots), :], w_ref[...]))
     other_ref[...] = low(dot(rows_ref[other_rows(spots), :], w_ref[...]))
 
 
-def to_ring(spots, rows, weights):
-    half = ((PACK // 2, WIDTH), jnp.bfloat16)
+def to_ring(spots, rows, heads):
+    half = shaped((PACK // 2, WIDTH), jnp.bfloat16)
     return ring_call(
-        to_ring_kernel, "to_ring", [pack_spec(256), whole_spec((256, WIDTH))], ring_specs(WIDTH),
-        [half, half], 800000000, spots, rows, weights,
+        to_ring_kernel, "to_ring",
+        [pack_spec(256), pl.BlockSpec(heads.shape, lambda x, spots: (0, 0, 0))],
+        ring_specs(WIDTH) + [whole_spec((256, WIDTH))],
+        [half, half, shaped((256, WIDTH), jnp.bfloat16, True)], 3, spots, rows, heads,
     )
 
 
@@ -213,19 +241,27 @@
 def to_pack(spots, own, other, weights):
     return ring_call(
         to_pack_kernel, "to_pack", ring_specs(own.shape[1]) + [whole_spec(weights.shape)],
-        [pack_spec(WIDTH)], [((PACK, WIDTH), jnp.bfloat16)], 1200000000, spots, own, other, weights,
+        [pack_spec(WIDTH)], [shaped((PACK, WIDTH), jnp.bfloat16)], 4, spots, own, other, weights,
     )[0]
 
 
-def out_back_kernel(spots, own_ref, other_ref, attended_ref, w_ref, d_attended_ref, d_w_ref, rows_ref):
-    @pl.when(pl.program_id(0) == 0)
+def out_back_kernel(
+    spots, own_ref, other_ref, attended_ref, w_ref, d_attended_ref, d_w_ref, rows_ref, total_ref
+):
+    step = pl.program_id(0)
+
+    @pl.when(step == 0)
     def _():
-        d_w_ref[...] = jnp.zeros_like(d_w_ref)
+        total_ref[...] = jnp.zeros_like(total_ref)
 
     rows_ref[own_rows(spots), :] = own_ref[...]
     rows_ref[other_rows(spots), :] = other_ref[...]
     d_attended_ref[...] = low(contract_cols(rows_ref[...], w_ref[...]))
-    d_w_ref[...] += contract_rows(attended_ref[...], rows_ref[...])
+    total_ref[...] += contract_rows(attended_ref[...], rows_ref[...])
+
+    @pl.when(step == pl.num_programs(0) - 1)
+    def _():
+        d_w_ref[...] = low(total_ref[...])
 
 
 def out_back(spots, own, other, attended, weights):
@@ -233,9 +269,9 @@
         out_back_kernel, "out_back",
         ring_specs(WIDTH) + [pack_spec(256), whole_spec((256, WIDTH))],
         [pack_spec(256), whole_spec((256, WIDTH))],
-        [((PACK, 256), jnp.bfloat16), ((256, WIDTH), jnp.float32)],
-        1600000000, spots, own, other, attended, weights,
-        scratch=[pltpu.VMEM((2 * TOK, WIDTH), jnp.bfloat16)],
+        [shaped((PACK, 256), jnp.bfloat16), shaped((256, WIDTH), jnp.bfloat16, True)],
+        5, spots, own, other, in_hbm(attended), in_hbm(weights),
+        scratch=[pltpu.VMEM((2 * TOK, WIDTH), jnp.bfloat16), pltpu.VMEM((256, WIDTH), jnp.float32)],
     )
 
 
@@ -266,7 +302,7 @@
             step(q_block)
 
 
-def attend_kernel(ends_ref, q_ref, k_ref, v_ref, out_ref, inverse_ref):
+def attend_kernel(ends_ref, q_ref, k_ref, v_ref, out_ref, kept_ref, inverse_ref):
     ends = (ends_ref[0], ends_ref[1])
 
     def step(q_block):
@@ -288,6 +324,7 @@
             out_ref[:, columns] = low(total * (1.0 / row_total))
             across = jnp.sum(jnp.swapaxes(part, 0, 1), axis=0, keepdims=True)
             inverse_ref[h : h + 1, :] = 1.0 / across
+        kept_ref[...] = out_ref[...]
 
     for_each_block(step)
 
@@ -305,15 +342,17 @@
             ],
             out_specs=[
                 pl.BlockSpec((BLOCK, 2 * HEAD), lambda q, ends: (q, 0)),
+                pl.BlockSpec((BLOCK, 2 * HEAD), lambda q, ends: (q, 0)),
                 pl.BlockSpec((2, BLOCK), lambda q, ends: (0, q)),
             ],
         ),
         out_shape=[
-            jax.ShapeDtypeStruct((PACK, 2 * HEAD), jnp.bfloat16),
-            jax.ShapeDtypeStruct((2, PACK), jnp.float32),
+            shaped((PACK, 2 * HEAD), jnp.bfloat16),
+            shaped((PACK, 2 * HEAD), jnp.bfloat16, True),
+            shaped((2, PACK), jnp.float32, True),
         ],
         compiler_params=pltpu.CompilerParams(vmem_limit_bytes=VMEM_LIMIT),
-        cost_estimate=pl.CostEstimate(flops=3000000000, bytes_accessed=4000000, transcendentals=3000000),
+        cost_estimate=cost(6),
         name="attend",
     )(ends, qkv, qkv, qkv)
 
@@ -360,6 +399,7 @@
 
 
 def attend_back(ends, qkv, grad, out, inverse):
+    qkv, out, inverse = in_hbm(qkv), in_hbm(out), in_hbm(inverse)
     by_block = pl.BlockSpec((BLOCK, 2 * HEAD), lambda q, ends: (q, 0))
     whole = pl.BlockSpec((PACK, HEAD), lambda q, ends: (0, 0))
     return pl.pallas_call(
@@ -383,7 +423,7 @@
             jax.ShapeDtypeStruct((PACK, HEAD), jnp.float32),
         ],
         compiler_params=pltpu.CompilerParams(vmem_limit_bytes=VMEM_LIMIT),
-        cost_estimate=pl.CostEstimate(flops=8000000000, bytes_accessed=8000000, transcendentals=3000000),
+        cost_estimate=cost(11),
         name="attend_back",
     )(ends, qkv, qkv, qkv, grad, out, inverse)
 
@@ -417,7 +457,7 @@
 
 
 def project_back(spots, pre, d_query, d_key, d_value, cosine, sine, normed, weights, gain_query, gain_key):
-    half = ((PACK // 2, WIDTH), jnp.bfloat16)
+    half = shaped((PACK // 2, WIDTH), jnp.bfloat16)
     return ring_call(
         qkv_back_kernel,
         "project_back",
@@ -425,14 +465,12 @@
         + [pack_spec(HEAD), pack_spec(HEAD), pack_spec(WIDTH)]
         + [whole_spec((512, WIDTH)), whole_spec((1, HEAD)), whole_spec((1, HEAD))],
         [pack_spec(512), whole_spec((1, WIDTH)), whole_spec((2, HEAD))] + ring_specs(WIDTH),
-        [((PACK, 512), jnp.bfloat16), ((1, WIDTH), jnp.float32), ((2, HEAD), jnp.float32), half, half],
-        1610612736, spots, pre, d_query, d_key, d_value, cosine, sine, normed, weights, gain_query, gain_key,
-        scratch=[pltpu.VMEM((2 * TOK, WIDTH), jnp.bfloat16)], limit=VMEM_MOST,
-    )
-
-
-def exchange(values, axes):
-    return lax.all_to_all(values, axes, split_axis=0, concat_axis=0, tiled=True)
+        [shaped((PACK, 512), jnp.bfloat16), shaped((1, WIDTH), jnp.float32)]
+        + [shaped((2, HEAD), jnp.float32), half, half],
+        11, spots, in_hbm(pre), d_query, d_key, d_value, in_hbm(cosine), in_hbm(sine), in_hbm(normed),
+        in_hbm(weights), gain_query, gain_key,
+        scratch=[pltpu.VMEM((2 * TOK, WIDTH), jnp.bfloat16)],
+    )
 
 
 def plane_order(core, blocks):
@@ -455,6 +493,19 @@
 def gather_plane_end(index, block):
     shape = block.shape[1:]
     return plane_order(index & 1, block.reshape((4, 4) + shape)).reshape((16,) + shape)
+
+
+def scatter_plane_step(index, blocks, step, *beside):
+    later = plane_bit(index, PLANE_STEPS[step])
+    half = blocks.shape[0] // 2
+    keep = lax.dynamic_slice_in_dim(blocks, later * half, half, axis=0)
+    send = lax.dynamic_slice_in_dim(blocks, (1 - later) * half, half, axis=0)
+    return low(wide(keep) + wide(after(swap(send, *PLANE_STEPS[step]), *beside)))
+
+
+def plane_blocks(core, blocks):
+    shape = blocks.shape[1:]
+    return plane_order(core, blocks.reshape((4, 4) + shape)).reshape((16,) + shape)
 
 
 def gather_ring(rows, beside=((), ())):
@@ -528,8 +579,6 @@
         [spot_of(core)[chips], spot_of(1 - core)[chips], core[None], core[None]]
     ).astype(jnp.int32)
 
-    first = cross(jnp.concatenate([hidden[0], cotangent[0], w_out], axis=0))
-    second = cross_and_swap(jnp.concatenate([hidden[0], cotangent[0]], axis=0), RING_STEPS[0])
     local = jnp.concatenate(
         [
             w_query.reshape(8, KV_HEADS, 256).transpose(1, 0, 2),
@@ -543,10 +592,22 @@
         ],
         axis=2,
     )
-    local = exchange(local, RING).reshape(64, 1408)
-    inputs, d_result = first[:TOK], first[TOK : 2 * TOK]
-    heads = jnp.concatenate([local[:, :640], tiles_tall(first[2 * TOK :])], axis=1)[None]
-    for step in range(4):
+    digits = jnp.pad(low(jnp.stack([lengths[0] // 64, lengths[0] % 64])), ((0, 14), (0, WIDTH - 3)))
+    rows = after(jnp.concatenate([hidden[0], w_out, digits], axis=0), local)
+    d_rows = after(cotangent[0], local)
+    local = exchange_ring(index, local).reshape(64, 1408)
+    first = cross(rows)
+    second = cross_and_swap(rows[:TOK], RING_STEPS[0])
+    d_result = cross(d_rows)
+    d_result_second = cross_and_swap(d_rows, RING_STEPS[0])
+    inputs = first[:TOK]
+    digits = first[TOK + 16 : TOK + 18, :3].astype(jnp.int32)
+    lengths = (digits[0] * 64 + digits[1])[None]
+    pieces = first[TOK : TOK + 16].reshape(16, 4, 256).transpose(1, 0, 2).reshape(64, 256)
+    heads = jnp.concatenate([local[:, :640], pieces], axis=1)[None]
+    heads = gather_plane_step(index, heads, 0)
+    second = after(second, heads)
+    for step in range(1, 4):
         heads = gather_plane_step(index, heads, step)
     gain_all = plane_order(core, heads[:, ::8, 512:530].reshape(4, 4, 8, 18))
     gain_all = gain_all.reshape(16, 4, 2, 18).transpose(1, 0, 2, 3)
@@ -555,10 +616,11 @@
     gain_query = gain_all[:, 2 * WIDTH : 2 * WIDTH + HEAD]
     gain_key = gain_all[:, 2 * WIDTH + HEAD :]
 
-    rows_own = jnp.concatenate([first[: 2 * TOK], second], axis=0)
-    rows_own = jnp.concatenate([rows_own, swap(rows_own, *RING_STEPS[1])], axis=0)
-    rows_other = swap(rows_own, CORE)
-    lengths = jnp.where(straight, lengths, swap(lengths, CORE))
+    def rest_of_ring(rows):
+        rows = jnp.concatenate([rows, swap(rows, *RING_STEPS[1])], axis=0)
+        return rows, swap(rows, CORE)
+
+    inputs_own, inputs_other = rest_of_ring(jnp.concatenate([inputs, second], axis=0))
     ends = jnp.stack([lengths[0, 0], lengths[0, 0] + lengths[0, 1]]).astype(jnp.int32)
     token = jnp.arange(PACK, dtype=jnp.int32)
     position = wide(token - row_start(token, (ends[0], ends[1])))
@@ -568,20 +630,17 @@
     cosine = jnp.concatenate([cosine, cosine], axis=1)
     sine = jnp.concatenate([-sine, sine], axis=1)
 
-    normed, pre, qkv, w_heads = project(
-        spots, rows_own, rows_other, heads, gain_attn, gain_query, gain_key, cosine, sine
-    )
-    heads = after(heads, qkv)
-    attended, inverse_total = attend(ends, qkv)
-    w_rows = plane_order(core, heads[..., 640:].reshape(4, 4, 64, 256)).reshape(16, 64, 256)
-    w_rows = tiles_flat(w_rows).reshape(2, 8, 16, WIDTH).transpose(1, 0, 2, 3).reshape(256, WIDTH)
-    out_own, out_other = to_ring(spots, attended, w_rows)
+    d_result_own = jnp.concatenate([d_result, d_result_second], axis=0)
+    d_result_own = jnp.concatenate([d_result_own, swap(d_result_own, *RING_STEPS[1])], axis=0)
+    heads, d_result, d_result_second = lax.optimization_barrier((heads, d_result, d_result_second))
+    normed, pre, qkv, qkv_kept, w_heads_across = project(
+        spots, inputs_own, inputs_other, heads, gain_attn, gain_query, gain_key, cosine, sine
+    )
+    qkv, d_result_own = lax.optimization_barrier((qkv, d_result_own))
+    attended, attended_kept, inverse_total = attend(ends, qkv)
+    out_own, out_other, w_rows = to_ring(spots, attended, heads)
     middle_steps = scatter_ring(out_own, out_other)
-    d_result_own, d_result_other = (
-        rows.reshape(4, 2, TOK, WIDTH)[:, 1].reshape(-1, WIDTH)
-        for rows in (after(rows_own, middle_steps[0]), after(rows_other, middle_steps[1]))
-    )
-
+    d_result_other = swap(after(d_result_own, middle_steps[0]), CORE)
     units = jnp.concatenate([local[:, 640:], tiles_tall(w_down)], axis=1)[None]
     units = gather_plane_step(index, after(units, out_own), 0)
     units = gather_plane_step(index, after(units, middle_steps[0]), 1)
@@ -592,9 +651,10 @@
     mixed_own = gather_ring(mixed)
     mixed_other = swap(mixed_own, CORE)
     units = gather_plane_step(index, units, 3)
-    units = plane_order(core, units.reshape(4, 4, 64, 1152)).reshape(16, 64, 1152)
+    units = plane_blocks(core, units)
     full_units = rows_by_device(units[..., :768])
     full_down = tiles_flat(units[..., 768:]).reshape(384, WIDTH)
+    full_units, full_down = lax.optimization_barrier((full_units, full_down))
 
     def feed_forward(rows, d_rows):
         pre = dot(rows, full_units)
@@ -617,26 +677,26 @@
 
     late = lambda array: after(array, d_mixed_steps[0])
     grad_units = contract_rows(mixed_own, late(d_pre_own)) + contract_rows(mixed_other, late(d_pre_other))
-    grad_units = low(grad_units)
-    late = lambda array: after(array, d_mixed_steps[1], grad_units)
     grad_down = contract_rows(late(act_own), d_result_own) + contract_rows(late(act_other), d_result_other)
     grad_down = low(grad_down).reshape(16, 3, 8, 8, HEAD).transpose(0, 3, 2, 1, 4)
-    grads = jnp.concatenate([rows_by_plane(grad_units), grad_down.reshape(16, 64, 384)], axis=2)
-    act_own, act_other = (after(act, grads) for act in (act_own, act_other))
+    grads = jnp.concatenate([rows_by_plane(low(grad_units)), grad_down.reshape(16, 64, 384)], axis=2)
+    grads = plane_blocks(core, grads)
+    act_own, act_other = (after(act, d_middle) for act in (act_own, act_other))
     result = to_pack(spots, act_own, act_other, full_down)
-    d_branch_own = gather_ring(low(d_middle), ((grads,), (result,)))
+    d_branch_own = gather_ring(after(low(d_middle), grads), ((), (result,)))
+    sums = scatter_plane_step(index, grads, 3, d_branch_own)
     d_branch_other = swap(d_branch_own, CORE)
-    grads = exchange(grads, PLANE)
     result = lax.psum_scatter(after(result, d_branch_own), RING, scatter_dimension=0, tiled=True)
     d_middle_home = jnp.where(straight, d_middle, wide(cross(after(low(d_middle), d_branch_own))))
 
-    d_attended, grad_out = out_back(spots, d_branch_own, d_branch_other, attended, w_rows)
-    d_query, d_key, d_value = attend_back(ends, qkv, d_attended, attended, inverse_total)
-    d_query, grads, grad_out = lax.optimization_barrier((d_query, grads, grad_out))
-    grad_out = low(grad_out).reshape(8, 2, 16, WIDTH).transpose(1, 0, 2, 3).reshape(16, 16, WIDTH)
-    grad_out = exchange(grad_out, PLANE)
+    d_attended, grad_out = out_back(spots, d_branch_own, d_branch_other, attended_kept, w_rows)
+    d_query, d_key, d_value = attend_back(ends, qkv_kept, d_attended, attended_kept, inverse_total)
+    sums = scatter_plane_step(index, sums, 2, d_query)
+    grad_out = grad_out.reshape(8, 2, 16, 4, 256).transpose(1, 0, 3, 2, 4).reshape(16, 64, 256)
+    grad_out = plane_blocks(core, grad_out)
+    d_query, sums, grad_out = lax.optimization_barrier((d_query, sums, grad_out))
     d_pre, d_gain_attn, d_gain_heads, d_normed_own, d_normed_other = project_back(
-        spots, pre, d_query, d_key, d_value, cosine, sine, normed, w_heads.T, gain_query, gain_key
+        spots, pre, d_query, d_key, d_value, cosine, sine, normed, w_heads_across, gain_query, gain_key
     )
     d_normed_steps = scatter_ring(d_normed_own, d_normed_other, 1)
     halves = low(d_normed_steps[1][:TOK]), low(d_normed_steps[1][TOK:])
@@ -646,26 +706,34 @@
     d_gains = jnp.concatenate(
         [(d_gain_attn / gain_attn)[0], d_gain_mlp, d_gain_heads.reshape(-1)]
     )
+    d_gains = d_gains.reshape(4, 16, 2, 1, 18).transpose(1, 0, 2, 3, 4)
     payload = jnp.concatenate(
         [
-            low(contract_rows(normed, d_pre)).reshape(DEVICES, 8, 512),
-            low(jnp.pad(d_gains.reshape(DEVICES, 1, 18), ((0, 0), (0, 7), (0, 110)))),
+            rows_by_plane(low(contract_rows(normed, d_pre))),
+            low(jnp.pad(d_gains, ((0, 0),) * 3 + ((0, 7), (0, 110)))).reshape(16, 64, 128),
         ],
         axis=2,
     )
-    heads_grad = wide(exchange(payload, AXES)).reshape(4, 16, 2, 8, 640)
-    heads_grad = jnp.sum(heads_grad, axis=1).reshape(8, 8, 640)
-
-    grads, grad_out = (after(array, d_normed_steps[0]) for array in (grads, grad_out))
-    sums = jnp.sum(wide(grads), axis=0)
-    units_grad = wide(exchange_ring(index, low(sums[:, :768]).reshape(8, 8, 768)))
-    sum_down = tiles_flat(sums[:, 768:])
-    sum_out = jnp.sum(wide(grad_out), axis=0)
+    heads_sums = jnp.concatenate([plane_blocks(core, payload), grad_out], axis=2)
+    heads_sums = scatter_plane_step(index, heads_sums, 3, d_normed_steps[0])
+    sums = scatter_plane_step(index, sums, 1, d_normed_steps[0])
+    sums = scatter_plane_step(index, sums, 0)[0]
+    for step in (2, 1, 0):
+        heads_sums = scatter_plane_step(index, heads_sums, step)
+    ring_grads = jnp.concatenate([heads_sums[0, :, :640], sums[:, :768]], axis=1)
+    ring_grads = exchange_ring(index, ring_grads.reshape(8, 8, 1408))
+    heads_grad, units_grad = wide(ring_grads[..., :640]), ring_grads[..., 640:]
+    sum_down = wide(tiles_flat(sums[:, 768:]))
+    sum_out = heads_sums[0, :, 640:].reshape(4, 16, 256).transpose(1, 0, 2).reshape(16, WIDTH)
+    sum_out = wide(sum_out)
     sum_out = jnp.where(straight, sum_out, wide(cross(low(sum_out))))
     activations = cross(after(low(middle + wide(result)), d_normed_steps[0]))
-    by_unit = lambda grad: (
-        grad.reshape(4, 2, 8, 16, 24).transpose(2, 0, 3, 1, 4).reshape(8, FF)
-    )
+    column = jnp.arange(768, dtype=jnp.int32)
+    column = column // 24 % 2 * 384 + column // 48 * 24 + column % 24
+    column = after(column, middle)
+    hits = lax.broadcasted_iota(jnp.int32, (768, 768), 0) == column[None, :]
+    units_grad = units_grad.reshape(4, 2, 8, 2, 384).transpose(3, 2, 0, 1, 4).reshape(64, 768)
+    units_grad = dot(units_grad, hits.astype(jnp.bfloat16)).reshape(2, 8, FF)
     sum_query = heads_grad[..., :256].transpose(1, 0, 2).reshape(8, -1)
     sum_key = heads_grad[..., 256:384].transpose(1, 0, 2).reshape(8, -1)
     sum_value = heads_grad[..., 384:512].transpose(1, 0, 2).reshape(8, -1)
@@ -677,8 +745,8 @@
         sum_key,
         sum_value,
         sum_out,
-        by_unit(units_grad[..., :384]),
-        by_unit(units_grad[..., 384:]),
+        units_grad[0],
+        units_grad[1],
         sum_down,
         sum_gains,
     )

time: 399 us -> 357 us (0.89)
  waiting for transfers between devices: 146 us -> 108 us
  local copies, waits for them, and re-layouts: 32.3 us -> 25.9 us
  Pallas kernels: 49.2 us -> 53.7 us
    all_to_all x4 -> x0, waiting for transfers between devices: 48.4 us -> none  [exchange(): return lax.all_to_all(values, axes, split_axis=0, concat_axis=0, tiled=True)]
    all_to_all x4 -> x0, starting transfers between devices: 22.6 us -> none  [exchange(): return lax.all_to_all(values, axes, split_axis=0, concat_axis=0, tiled=True)]
    ppermute x29 -> x42, waiting for transfers between devices: 74.6 us -> 90.2 us  [swap(): lax.ppermute(values, AXES, [(k, k ^ masks[k & 1]) for k in range(DEVICES)])]
    ppermute x29 -> x42, starting transfers between devices: 44.6 us -> 58.4 us  [swap(): lax.ppermute(values, AXES, [(k, k ^ masks[k & 1]) for k in range(DEVICES)])]
    unnamed x85 -> x73, local copies, waits for them, and re-layouts: 12.4 us -> 5.67 us
    ppermute x5 -> x6, waiting for transfers between devices: 21.7 us -> 15.2 us  [cross(): return lax.ppermute(values, AXES, [(k, crossed(k)) for k in range(DEVICES)])]
    convert_element_type x5 -> x10, other arithmetic: 2.5 us -> 8.17 us  [low(): return values.astype(jnp.bfloat16)]
    ppermute x1 -> x2, starting transfers between devices: 0.94 us -> 6.36 us  [cross_and_swap(): lax.ppermute(values, AXES, [(crossed(k ^ masks[k & 1]), k) for k in range...]
  transfers between devices with their start and end apart: 41 -> 52, of which waited for: 25 -> 27; matrix products, arithmetic and copies ran while one was open for 17% -> 15% of each run, Pallas kernels for 8% -> 6%
where the time goes in v1:
time: 357 us; the launch traced here: 351 us
  waiting for transfers between devices  108 us (30%)
  starting transfers between devices  94.3 us (26%)
  Pallas kernels  53.7 us (15%)
  other arithmetic  37 us (10%)
  local copies, waits for them, and re-layouts  25.9 us (7%)
  between operations  17.3 us (5%)
  matrix products  15.3 us (4%)
    ppermute x42, waiting for transfers between devices, swap(): lax.ppermute(values, AXES, [(k, k ^ masks[k & 1]) for k in range(DEVICES)])  90.2 us
    ppermute x42, starting transfers between devices, swap(): lax.ppermute(values, AXES, [(k, k ^ masks[k & 1]) for k in range(DEVICES)])  58.4 us
    pallas_call x5, Pallas kernels, ring_call(): pl.pallas_call(kernel, grid_spec=pltpu.PrefetchScalarGridSpec(num_scalar_...  36 us
    ppermute x6, starting transfers between devices, cross(): return lax.ppermute(values, AXES, [(k, crossed(k)) for k in range(DEVICES)])  26.1 us
    ppermute x6, waiting for transfers between devices, cross(): return lax.ppermute(values, AXES, [(k, crossed(k)) for k in range(DEVICES)])  15.2 us
    pallas_call x1, Pallas kernels, attend_back(): pl.pallas_call(attend_back_kernel, grid_spec=pltpu.PrefetchScalarGridSpec...  11 us
    convert_element_type x10, other arithmetic, low(): return values.astype(jnp.bfloat16)  8.17 us
  transfers between devices with their start and end apart: 52, of which 27 were waited for; matrix products, arithmetic and copies ran while one was open for 15% of the time, Pallas kernels for 6%

profile of v1, /device:TPU:1, one launch (start us, length us, event | category | flops | bytes accessed | tf_op | source)
XLA Modules:
  0.0 351.0 jit_solution(12632173963525810594)
XLA Ops:
  10.5 6.0 %collective-permute-start.13 = (bf16[192,1024]{1,0:T(8,128)(2,1)}, bf16[192,1024]{1,0:T(8,128)(2,1)S(1)}, u32[]{:S(2)}, u32[]{:S(2)}) collective-permute-start(bf16[192,1024]{1,0:T(8,128)(2,1)} %bitcast.32), channel_id=1, source_target_pairs={{32,0},{112,1},{34,2},{114,3},{36,4},{116,5},{38,6},{118,7},{40,8}... | collective-permute-start | bytes 1179656 | tf_op jit(solution)/shard_map/ppermute | solution.py:48
  16.5 2.3 collective-permute-start.12
  21.0 2.6 collective-permute-start.4
  24.9 5.6 %collective-permute-start = (bf16[224,1024]{1,0:T(8,128)(2,1)S(1)}, bf16[224,1024]{1,0:T(8,128)(2,1)S(1)}, u32[]{:S(2)}, u32[]{:S(2)}) collective-permute-start(bf16[224,1024]{1,0:T(8,128)(2,1)S(1)} %pad_maximum_fusion.13), channel_id=1, source_target_pairs={{0,0},{1,16},{2,2},{3,18},{4,4},{5,20},{6,6},{7,22},{8,8},{9,24},{... | collective-permute-start | bytes 1376264 | tf_op jit(solution)/shard_map/ppermute | solution.py:44
  31.2 11.0 %collective-permute-done = bf16[224,1024]{1,0:T(8,128)(2,1)S(1)} collective-permute-done((bf16[224,1024]{1,0:T(8,128)(2,1)S(1)}, bf16[224,1024]{1,0:T(8,128)(2,1)S(1)}, u32[]{:S(2)}, u32[]{:S(2)}) %collective-permute-start) | collective-permute-done | bytes 458784 | tf_op jit(solution)/shard_map/ppermute | solution.py:44
  50.0 2.9 collective-permute-done.9
  53.0 2.7 collective-permute-start.10
  58.3 3.3 collective-permute-done.10
  61.8 2.6 collective-permute-start.11
  64.4 2.8 collective-permute-done.7
  67.2 2.6 pad_maximum_fusion.1.own_ref
  69.9 2.8 fusion.15
  74.0 3.0 pad_maximum_fusion.2
  78.6 10.4 %project.1 = (bf16[1536,1024]{1,0:T(8,128)(2,1)}, f32[1536,384]{1,0:T(8,128)}, bf16[1536,512]{1,0:T(8,128)(2,1)S(1)}, bf16[1536,512]{1,0:T(8,128)(2,1)}, bf16[512,1024]{1,0:T(8,128)(2,1)}) custom-call(s32[10]{0:T(128)S(1)} %pad_add_fusion.spots, bf16[768,1024]{1,0:T(8,128)(2,1)} %pad_maximum_fusion.1.own_ref, ...), custom_call_target="tpu_custom_call" | custom-call | bytes 28800000 | tf_op jit(solution)/shard_map/project/pallas_call | solution.py:144
  89.0 6.7 %attend.1 = (bf16[1536,256]{1,0:T(8,128)(2,1)S(1)}, bf16[1536,256]{1,0:T(8,128)(2,1)}, f32[2,1536]{1,0:T(2,128)}) custom-call(s32[2]{0:T(128)S(1)} %pad_add_fusion.1.ends_ref, bf16[1536,512]{1,0:T(8,128)(2,1)S(1)} %get-tuple-element.68.q_ref.k_ref.v_ref, bf16[1536,512]{1,0:T(8,128)(2,1)S(1)} %get-tuple-element.68.q_ref.k_ref.v_ref, ...), custom_call_target="tpu_custom_call" | custom-call | bytes 21600000 | tf_op jit(solution)/shard_map/attend/pallas_call | solution.py:333
  95.7 2.9 to_ring.1
  99.9 3.0 collective-permute-done.15
  106.0 3.4 collective-permute-done.20
  109.5 7.2 %collective-permute-start.21 = (bf16[2,64,1152]{2,1,0:T(8,128)(2,1)S(1)}, bf16[2,64,1152]{2,1,0:T(8,128)(2,1)S(1)}, u32[]{:S(2)}, u32[]{:S(2)}) collective-permute-start(bf16[2,64,1152]{2,1,0:T(8,128)(2,1)S(1)} %maximum_select_fusion.6), channel_id=1, source_target_pairs={{0,6},{1,25},{2,4},{3,27},{4,2},{5,29},{6,0},{7,31},{8,14},{9,17},... | collective-permute-start | bytes 884744 | tf_op jit(solution)/shard_map/ppermute | solution.py:36
  121.0 4.0 %collective-permute-done.17 = bf16[192,1024]{1,0:T(8,128)(2,1)S(1)} collective-permute-done((bf16[192,1024]{1,0:T(8,128)(2,1)S(1)}, bf16[192,1024]{1,0:T(8,128)(2,1)S(1)}, u32[]{:S(2)}, u32[]{:S(2)}) %collective-permute-start.17) | collective-permute-done | bytes 393248 | tf_op jit(solution)/shard_map/ppermute | solution.py:36
  127.3 2.7 collective-permute-done.22
  130.6 2.8 collective-permute-done.18
  133.5 11.1 %collective-permute-done.19 = bf16[384,1024]{1,0:T(8,128)(2,1)S(1)} collective-permute-done((bf16[384,1024]{1,0:T(8,128)(2,1)S(1)}, bf16[384,1024]{1,0:T(8,128)(2,1)S(1)}, u32[]{:S(2)}, u32[]{:S(2)}) %collective-permute-start.19) | collective-permute-done | bytes 786464 | tf_op jit(solution)/shard_map/ppermute | solution.py:36
  144.8 6.5 %collective-permute-start.25 = (bf16[768,1024]{1,0:T(8,128)(2,1)S(1)}, bf16[768,1024]{1,0:T(8,128)(2,1)S(1)}, u32[]{:S(2)}, u32[]{:S(2)}) collective-permute-start(bf16[768,1024]{1,0:T(8,128)(2,1)S(1)} %pad_maximum_fusion.3), channel_id=1, source_target_pairs={{0,1},{1,0},{2,3},{3,2},{4,5},{5,4},{6,7},{7,6},{8,9},{9,8},{10,11... | collective-permute-start | bytes 4718600 | tf_op jit(solution)/shard_map/ppermute | solution.py:36
  169.6 8.0 %collective-permute-done.27 = bf16[384,1024]{1,0:T(8,128)(2,1)S(1)} collective-permute-done((bf16[384,1024]{1,0:T(8,128)(2,1)S(1)}, bf16[384,1024]{1,0:T(8,128)(2,1)S(1)}, u32[]{:S(2)}, u32[]{:S(2)}) %collective-permute-start.27) | collective-permute-done | bytes 786464 | tf_op jit(solution)/shard_map/ppermute | solution.py:36
  180.5 5.3 %collective-permute-done.28 = bf16[192,1024]{1,0:T(8,128)(2,1)S(1)} collective-permute-done((bf16[192,1024]{1,0:T(8,128)(2,1)S(1)}, bf16[192,1024]{1,0:T(8,128)(2,1)S(1)}, u32[]{:S(2)}, u32[]{:S(2)}) %collective-permute-start.28) | collective-permute-done | bytes 393248 | tf_op jit(solution)/shard_map/ppermute | solution.py:36
  188.2 2.4 constant_dynamic-slice_fusion.6
  191.3 3.9 %collective-permute-done.29 = bf16[192,1024]{1,0:T(8,128)(2,1)S(1)} collective-permute-done((bf16[192,1024]{1,0:T(8,128)(2,1)S(1)}, bf16[192,1024]{1,0:T(8,128)(2,1)S(1)}, u32[]{:S(2)}, u32[]{:S(2)}) %collective-permute-start.29) | collective-permute-done | bytes 393248 | tf_op jit(solution)/shard_map/ppermute | solution.py:36
  196.1 4.1 %to_pack.1 = bf16[1536,1024]{1,0:T(8,128)(2,1)} custom-call(s32[10]{0:T(128)S(1)} %pad_add_fusion.spots, bf16[768,384]{1,0:T(8,128)(2,1)S(1)} %get-tuple-element.84.own_ref, bf16[768,384]{1,0:T(8,128)(2,1)S(1)} %get-tuple-element.85.other_ref, bf16[384,1024]{1,0:T(8,128)(2,1)S(1)} %bitcast.199), custom_call_target="tpu_custom_call" | custom-call | bytes 14400000 | tf_op jit(solution)/shard_map/to_pack/pallas_call | solution.py:144
  200.3 7.3 %collective-permute-done.30 = bf16[384,1024]{1,0:T(8,128)(2,1)} collective-permute-done((bf16[384,1024]{1,0:T(8,128)(2,1)}, bf16[384,1024]{1,0:T(8,128)(2,1)}, u32[]{:S(2)}, u32[]{:S(2)}) %collective-permute-start.30) | collective-permute-done | bytes 786464 | tf_op jit(solution)/shard_map/ppermute | solution.py:36
  208.8 4.5 %collective-permute-start.31 = (bf16[768,1024]{1,0:T(8,128)(2,1)S(1)}, bf16[768,1024]{1,0:T(8,128)(2,1)S(1)}, u32[]{:S(2)}, u32[]{:S(2)}) collective-permute-start(bf16[768,1024]{1,0:T(8,128)(2,1)S(1)} %constant_dynamic-update-slice_fusion.12.own_ref), channel_id=1, source_target_pairs={{0,1},{1,0},{2,3},{3,2},{4,5},{5,4},{6,7},{7,6},{8,9},{9,8},{10,11... | collective-permute-start | bytes 4718600 | tf_op jit(solution)/shard_map/ppermute | solution.py:36
  218.4 5.8 %out_back.1 = (bf16[1536,256]{1,0:T(8,128)(2,1)S(1)}, bf16[256,1024]{1,0:T(8,128)(2,1)}) custom-call(s32[10]{0:T(128)S(1)} %pad_add_fusion.spots, bf16[768,1024]{1,0:T(8,128)(2,1)S(1)} %constant_dynamic-update-slice_fusion.12.own_ref, bf16[768,1024]{1,0:T(8,128)(2,1)S(1)} %collective-permute-done.31.other_ref, ...), custom_call_target="tpu_custom_call" | custom-call | bytes 18000000 | tf_op jit(solution)/shard_map/out_back/pallas_call | solution.py:144
  224.3 11.0 %attend_back.1 = (f32[1536,256]{1,0:T(8,128)S(1)}, f32[1536,128]{1,0:T(8,128)S(1)}, f32[1536,128]{1,0:T(8,128)S(1)}) custom-call(s32[2]{0:T(128)S(1)} %pad_add_fusion.1.ends_ref, bf16[1536,512]{1,0:T(8,128)(2,1)} %get-tuple-element.90.q_ref.k_ref.v_ref, bf16[1536,512]{1,0:T(8,128)(2,1)} %get-tuple-element.90.q_ref.k_ref.v_ref, ...), custom_call_target="tpu_custom_call" | custom-call | bytes 39600000 | tf_op jit(solution)/shard_map/attend_back/pallas_call | solution.py:405
  236.5 2.3 reshape.290
  242.9 12.8 %project_back.1 = (bf16[1536,512]{1,0:T(8,128)(2,1)S(1)}, f32[1,1024]{1,0:T(1,128)S(1)}, f32[2,128]{1,0:T(2,128)S(1)}, bf16[768,1024]{1,0:T(8,128)(2,1)S(1)}, bf16[768,1024]{1,0:T(8,128)(2,1)}) custom-call(s32[10]{0:T(128)S(1)} %pad_add_fusion.spots, f32[1536,384]{1,0:T(8,128)} %get-tuple-element.89.pre_ref, f32[1536,256]{1,0:T(8,128)} %copy-done.6, ...), custom_call_target="tpu_custom_call" | custom-call | bytes 39600000 | tf_op jit(solution)/shard_map/project_back/pallas_call | solution.py:144
  261.6 5.3 %collective-permute-start.36 = (bf16[192,1024]{1,0:T(8,128)(2,1)}, bf16[192,1024]{1,0:T(8,128)(2,1)}, u32[]{:S(2)}, u32[]{:S(2)}) collective-permute-start(bf16[192,1024]{1,0:T(8,128)(2,1)} %copy-done.17), channel_id=1, source_target_pairs={{0,0},{1,16},{2,2},{3,18},{4,4},{5,20},{6,6},{7,22},{8,8},{9,24},{... | collective-permute-start | bytes 1179656 | tf_op jit(solution)/shard_map/ppermute | solution.py:44
  271.9 7.5 %collective-permute-done.44 = bf16[2,64,1152]{2,1,0:T(8,128)(2,1)S(1)} collective-permute-done((bf16[2,64,1152]{2,1,0:T(8,128)(2,1)S(1)}, bf16[2,64,1152]{2,1,0:T(8,128)(2,1)S(1)}, u32[]{:S(2)}, u32[]{:S(2)}) %collective-permute-start.44) | collective-permute-done | bytes 294944 | tf_op jit(solution)/shard_map/ppermute | solution.py:36
  282.4 6.4 %collective-permute-done.41 = bf16[4,64,896]{2,1,0:T(8,128)(2,1)S(1)} collective-permute-done((bf16[4,64,896]{2,1,0:T(8,128)(2,1)S(1)}, bf16[4,64,896]{2,1,0:T(8,128)(2,1)S(1)}, u32[]{:S(2)}, u32[]{:S(2)}) %collective-permute-start.41) | collective-permute-done | bytes 458784 | tf_op jit(solution)/shard_map/ppermute | solution.py:36
  291.1 4.3 %collective-permute-done.42 = bf16[2,64,896]{2,1,0:T(8,128)(2,1)S(1)} collective-permute-done((bf16[2,64,896]{2,1,0:T(8,128)(2,1)S(1)}, bf16[2,64,896]{2,1,0:T(8,128)(2,1)S(1)}, u32[]{:S(2)}, u32[]{:S(2)}) %collective-permute-start.42) | collective-permute-done | bytes 229408 | tf_op jit(solution)/shard_map/ppermute | solution.py:36
  295.6 4.4 %collective-permute-done.37 = bf16[384,1024]{1,0:T(8,128)(2,1)S(1)} collective-permute-done((bf16[384,1024]{1,0:T(8,128)(2,1)S(1)}, bf16[384,1024]{1,0:T(8,128)(2,1)S(1)}, u32[]{:S(2)}, u32[]{:S(2)}) %collective-permute-start.37) | collective-permute-done | bytes 786464 | tf_op jit(solution)/shard_map/ppermute | solution.py:36
  300.3 5.8 %collective-permute-start.46 = (bf16[4,1,8,1408]{3,2,1,0:T(8,128)(2,1)S(1)}, bf16[4,1,8,1408]{3,2,1,0:T(8,128)(2,1)S(1)}, u32[]{:S(2)}, u32[]{:S(2)}) collective-permute-start(bf16[4,1,8,1408]{3,2,1,0:T(8,128)(2,1)S(1)} %fusion.20), channel_id=1, source_target_pairs={{0,1},{1,0},{2,3},{3,2},{4,5},{5,4},{6,7},{7,6},{8,9},{9,8},{10,11... | collective-permute-start | bytes 270344 | tf_op jit(solution)/shard_map/ppermute | solution.py:36
  306.9 4.5 %collective-permute-start.38 = (bf16[192,1024]{1,0:T(8,128)(2,1)}, bf16[192,1024]{1,0:T(8,128)(2,1)S(1)}, u32[]{:S(2)}, u32[]{:S(2)}) collective-permute-start(bf16[192,1024]{1,0:T(8,128)(2,1)} %get-tuple-element.128), channel_id=1, source_target_pairs={{0,0},{1,16},{2,2},{3,18},{4,4},{5,20},{6,6},{7,22},{8,8},{9,24},{... | collective-permute-start | bytes 1179656 | tf_op jit(solution)/shard_map/ppermute | solution.py:44
  311.4 2.5 collective-permute-start.50
  314.1 3.0 collective-permute-start.48
  320.6 3.4 collective-permute-start.39
  331.6 5.9 %collective-permute-start.35 = (bf16[192,1024]{1,0:T(8,128)(2,1)S(1)}, bf16[192,1024]{1,0:T(8,128)(2,1)S(1)}, u32[]{:S(2)}, u32[]{:S(2)}) collective-permute-start(bf16[192,1024]{1,0:T(8,128)(2,1)S(1)} %add_convert_fusion.6), channel_id=1, source_target_pairs={{0,0},{1,16},{2,2},{3,18},{4,4},{5,20},{6,6},{7,22},{8,8},{9,24},{... | collective-permute-start | bytes 1179656 | tf_op jit(solution)/shard_map/ppermute | solution.py:44
  337.6 2.2 fusion.12
  339.8 3.2 collective-permute-done.35
  (301 shorter events, 97.0 us)
Async XLA Ops:
  7.3 323.2 %reduce-scatter.2.cloned.1.call-start = ((), (), s32[]{:S(2)}) async-start(), calls=%async_computation.1 | async-start | bytes 3538944 | tf_op jit(solution)/shard_map/reduce_scatter | solution.py:689
  10.5 35.9 %collective-permute-start.13 = (bf16[192,1024]{1,0:T(8,128)(2,1)}, bf16[192,1024]{1,0:T(8,128)(2,1)S(1)}, u32[]{:S(2)}, u32[]{:S(2)}) collective-permute-start(bf16[192,1024]{1,0:T(8,128)(2,1)} %bitcast.32), channel_id=1, source_target_pairs={{32,0},{112,1},{34,2},{114,3},{36,4},{116,5},{38,6},{118,7},{40,8}... | collective-permute-start | bytes 1179656 | tf_op jit(solution)/shard_map/ppermute | solution.py:48
  16.5 30.0 %collective-permute-start.12 = (bf16[192,1024]{1,0:T(8,128)(2,1)}, bf16[192,1024]{1,0:T(8,128)(2,1)S(1)}, u32[]{:S(2)}, u32[]{:S(2)}) collective-permute-start(bf16[192,1024]{1,0:T(8,128)(2,1)} %bitcast.32), channel_id=1, source_target_pairs={{0,0},{1,16},{2,2},{3,18},{4,4},{5,20},{6,6},{7,22},{8,8},{9,24},{... | collective-permute-start | bytes 1179656 | tf_op jit(solution)/shard_map/ppermute | solution.py:44
  21.0 9.5 %collective-permute-start.4 = (bf16[1,2,8,1408]{3,2,1,0:T(8,128)(2,1)S(1)}, bf16[1,2,8,1408]{3,2,1,0:T(8,128)(2,1)S(1)}, u32[]{:S(2)}, u32[]{:S(2)}) collective-permute-start(bf16[1,2,8,1408]{3,2,1,0:T(8,128)(2,1)S(1)} %get-tuple-element.142), channel_id=1, source_target_pairs={{0,64},{1,65},{2,66},{3,67},{4,68},{5,69},{6,70},{7,71},{8,72},{9,... | collective-permute-start | bytes 135176 | tf_op jit(solution)/shard_map/ppermute | solution.py:36
  23.7 7.3 %collective-permute-start.5 = (bf16[1,2,8,1408]{3,2,1,0:T(8,128)(2,1)S(1)}, bf16[1,2,8,1408]{3,2,1,0:T(8,128)(2,1)S(1)}, u32[]{:S(2)}, u32[]{:S(2)}) collective-permute-start(bf16[1,2,8,1408]{3,2,1,0:T(8,128)(2,1)S(1)} %get-tuple-element.143), channel_id=1, source_target_pairs={{0,96},{1,97},{2,98},{3,99},{4,100},{5,101},{6,102},{7,103},{8,104... | collective-permute-start | bytes 135176 | tf_op jit(solution)/shard_map/ppermute | solution.py:36
  24.9 17.2 %collective-permute-start = (bf16[224,1024]{1,0:T(8,128)(2,1)S(1)}, bf16[224,1024]{1,0:T(8,128)(2,1)S(1)}, u32[]{:S(2)}, u32[]{:S(2)}) collective-permute-start(bf16[224,1024]{1,0:T(8,128)(2,1)S(1)} %pad_maximum_fusion.13), channel_id=1, source_target_pairs={{0,0},{1,16},{2,2},{3,18},{4,4},{5,20},{6,6},{7,22},{8,8},{9,24},{... | collective-permute-start | bytes 1376264 | tf_op jit(solution)/shard_map/ppermute | solution.py:44
  30.6 18.5 %collective-permute-start.1 = (bf16[192,1024]{1,0:T(8,128)(2,1)S(1)}, bf16[192,1024]{1,0:T(8,128)(2,1)S(1)}, u32[]{:S(2)}, u32[]{:S(2)}) collective-permute-start(bf16[192,1024]{1,0:T(8,128)(2,1)S(1)} %slice.151), channel_id=1, source_target_pairs={{32,0},{112,1},{34,2},{114,3},{36,4},{116,5},{38,6},{118,7},{40,8}... | collective-permute-start | bytes 1179656 | tf_op jit(solution)/shard_map/ppermute | solution.py:48
  46.4 6.6 %collective-permute-start.9 = (bf16[2,64,896]{2,1,0:T(8,128)(2,1)S(1)}, bf16[2,64,896]{2,1,0:T(8,128)(2,1)S(1)}, u32[]{:S(2)}, u32[]{:S(2)}) collective-permute-start(bf16[2,64,896]{2,1,0:T(8,128)(2,1)S(1)} %maximum_select_fusion.7), channel_id=1, source_target_pairs={{0,6},{1,25},{2,4},{3,27},{4,2},{5,29},{6,0},{7,31},{8,14},{9,17},... | collective-permute-start | bytes 688136 | tf_op jit(solution)/shard_map/ppermute | solution.py:36
  47.5 26.4 %collective-permute-start.14 = (bf16[384,1024]{1,0:T(8,128)(2,1)}, bf16[384,1024]{1,0:T(8,128)(2,1)}, u32[]{:S(2)}, u32[]{:S(2)}) collective-permute-start(bf16[384,1024]{1,0:T(8,128)(2,1)} %pad_maximum_fusion.10), channel_id=1, source_target_pairs={{0,96},{1,33},{2,98},{3,35},{4,100},{5,37},{6,102},{7,39},{8,104},... | collective-permute-start | bytes 2359304 | tf_op jit(solution)/shard_map/ppermute | solution.py:36
  50.0 17.1 %collective-permute-start.7 = (bf16[384,1024]{1,0:T(8,128)(2,1)}, bf16[384,1024]{1,0:T(8,128)(2,1)}, u32[]{:S(2)}, u32[]{:S(2)}) collective-permute-start(bf16[384,1024]{1,0:T(8,128)(2,1)} %pad_maximum_fusion.7), channel_id=1, source_target_pairs={{0,96},{1,33},{2,98},{3,35},{4,100},{5,37},{6,102},{7,39},{8,104},... | collective-permute-start | bytes 2359304 | tf_op jit(solution)/shard_map/ppermute | solution.py:36
  53.0 8.5 %collective-permute-start.10 = (bf16[4,64,896]{2,1,0:T(8,128)(2,1)S(1)}, bf16[4,64,896]{2,1,0:T(8,128)(2,1)S(1)}, u32[]{:S(2)}, u32[]{:S(2)}) collective-permute-start(bf16[4,64,896]{2,1,0:T(8,128)(2,1)S(1)} %maximum_select_fusion.5), channel_id=1, source_target_pairs={{0,8},{1,3},{2,10},{3,1},{4,12},{5,7},{6,14},{7,5},{8,0},{9,11},{1... | collective-permute-start | bytes 1376264 | tf_op jit(solution)/shard_map/ppermute | solution.py:36
  61.8 15.3 %collective-permute-start.11 = (bf16[8,64,896]{2,1,0:T(8,128)(2,1)S(1)}, bf16[8,64,896]{2,1,0:T(8,128)(2,1)S(1)}, u32[]{:S(2)}, u32[]{:S(2)}) collective-permute-start(bf16[8,64,896]{2,1,0:T(8,128)(2,1)S(1)} %maximum_select_fusion.3), channel_id=1, source_target_pairs={{0,24},{1,7},{2,26},{3,5},{4,28},{5,3},{6,30},{7,1},{8,16},{9,15},... | collective-permute-start | bytes 2752520 | tf_op jit(solution)/shard_map/ppermute | solution.py:36
  69.7 8.0 %collective-permute-start.8 = (bf16[768,1024]{1,0:T(8,128)(2,1)}, bf16[768,1024]{1,0:T(8,128)(2,1)}, u32[]{:S(2)}, u32[]{:S(2)}) collective-permute-start(bf16[768,1024]{1,0:T(8,128)(2,1)} %pad_maximum_fusion.1.own_ref), channel_id=1, source_target_pairs={{0,1},{1,0},{2,3},{3,2},{4,5},{5,4},{6,7},{7,6},{8,9},{9,8},{10,11... | collective-permute-start | bytes 4718600 | tf_op jit(solution)/shard_map/ppermute | solution.py:36
  98.6 4.3 %collective-permute-start.15 = (bf16[768,1024]{1,0:T(8,128)(2,1)S(1)}, bf16[768,1024]{1,0:T(8,128)(2,1)S(1)}, u32[]{:S(2)}, u32[]{:S(2)}) collective-permute-start(bf16[768,1024]{1,0:T(8,128)(2,1)S(1)} %get-tuple-element.71), channel_id=1, source_target_pairs={{0,1},{1,0},{2,3},{3,2},{4,5},{5,4},{6,7},{7,6},{8,9},{9,8},{10,11... | collective-permute-start | bytes 4718600 | tf_op jit(solution)/shard_map/ppermute | solution.py:36
  103.7 13.1 %collective-permute-start.16 = (bf16[384,1024]{1,0:T(8,128)(2,1)S(1)}, bf16[384,1024]{1,0:T(8,128)(2,1)S(1)}, u32[]{:S(2)}, u32[]{:S(2)}) collective-permute-start(bf16[384,1024]{1,0:T(8,128)(2,1)S(1)} %slice.300), channel_id=1, source_target_pairs={{0,96},{1,33},{2,98},{3,35},{4,100},{5,37},{6,102},{7,39},{8,104},... | collective-permute-start | bytes 2359304 | tf_op jit(solution)/shard_map/ppermute | solution.py:36
  104.7 4.8 %collective-permute-start.20 = (bf16[1,64,1152]{2,1,0:T(8,128)(2,1)S(1)}, bf16[1,64,1152]{2,1,0:T(8,128)(2,1)S(1)}, u32[]{:S(2)}, u32[]{:S(2)}) collective-permute-start(bf16[1,64,1152]{2,1,0:T(8,128)(2,1)S(1)} %maximum_bitcast_fusion), channel_id=1, source_target_pairs={{0,2},{1,9},{2,0},{3,11},{4,6},{5,13},{6,4},{7,15},{8,10},{9,1},{1... | collective-permute-start | bytes 442376 | tf_op jit(solution)/shard_map/ppermute | solution.py:36
  109.5 11.3 %collective-permute-start.21 = (bf16[2,64,1152]{2,1,0:T(8,128)(2,1)S(1)}, bf16[2,64,1152]{2,1,0:T(8,128)(2,1)S(1)}, u32[]{:S(2)}, u32[]{:S(2)}) collective-permute-start(bf16[2,64,1152]{2,1,0:T(8,128)(2,1)S(1)} %maximum_select_fusion.6), channel_id=1, source_target_pairs={{0,6},{1,25},{2,4},{3,27},{4,2},{5,29},{6,0},{7,31},{8,14},{9,17},... | collective-permute-start | bytes 884744 | tf_op jit(solution)/shard_map/ppermute | solution.py:36
  117.1 7.9 %collective-permute-start.17 = (bf16[192,1024]{1,0:T(8,128)(2,1)S(1)}, bf16[192,1024]{1,0:T(8,128)(2,1)S(1)}, u32[]{:S(2)}, u32[]{:S(2)}) collective-permute-start(bf16[192,1024]{1,0:T(8,128)(2,1)S(1)} %slice.302), channel_id=1, source_target_pairs={{0,32},{1,97},{2,34},{3,99},{4,36},{5,101},{6,38},{7,103},{8,40},{... | collective-permute-start | bytes 1179656 | tf_op jit(solution)/shard_map/ppermute | solution.py:36
  120.9 9.1 %collective-permute-start.22 = (bf16[4,64,1152]{2,1,0:T(8,128)(2,1)S(1)}, bf16[4,64,1152]{2,1,0:T(8,128)(2,1)S(1)}, u32[]{:S(2)}, u32[]{:S(2)}) collective-permute-start(bf16[4,64,1152]{2,1,0:T(8,128)(2,1)S(1)} %maximum_select_fusion.4), channel_id=1, source_target_pairs={{0,8},{1,3},{2,10},{3,1},{4,12},{5,7},{6,14},{7,5},{8,0},{9,11},{1... | collective-permute-start | bytes 1769480 | tf_op jit(solution)/shard_map/ppermute | solution.py:36
  125.4 7.9 %collective-permute-start.18 = (bf16[192,1024]{1,0:T(8,128)(2,1)S(1)}, bf16[192,1024]{1,0:T(8,128)(2,1)S(1)}, u32[]{:S(2)}, u32[]{:S(2)}) collective-permute-start(bf16[192,1024]{1,0:T(8,128)(2,1)S(1)} %multiply_convert_fusion.6), channel_id=1, source_target_pairs={{0,32},{1,97},{2,34},{3,99},{4,36},{5,101},{6,38},{7,103},{8,40},{... | collective-permute-start | bytes 1179656 | tf_op jit(solution)/shard_map/ppermute | solution.py:36
  130.3 21.1 %collective-permute-start.23 = (bf16[8,64,1152]{2,1,0:T(8,128)(2,1)S(1)}, bf16[8,64,1152]{2,1,0:T(8,128)(2,1)S(1)}, u32[]{:S(2)}, u32[]{:S(2)}) collective-permute-start(bf16[8,64,1152]{2,1,0:T(8,128)(2,1)S(1)} %maximum_select_fusion.2), channel_id=1, source_target_pairs={{0,24},{1,7},{2,26},{3,5},{4,28},{5,3},{6,30},{7,1},{8,16},{9,15},... | collective-permute-start | bytes 3538952 | tf_op jit(solution)/shard_map/ppermute | solution.py:36
  133.4 11.2 %collective-permute-start.19 = (bf16[384,1024]{1,0:T(8,128)(2,1)S(1)}, bf16[384,1024]{1,0:T(8,128)(2,1)S(1)}, u32[]{:S(2)}, u32[]{:S(2)}) collective-permute-start(bf16[384,1024]{1,0:T(8,128)(2,1)S(1)} %pad_maximum_fusion.11), channel_id=1, source_target_pairs={{0,96},{1,33},{2,98},{3,35},{4,100},{5,37},{6,102},{7,39},{8,104},... | collective-permute-start | bytes 2359304 | tf_op jit(solution)/shard_map/ppermute | solution.py:36
  144.8 9.6 %collective-permute-start.25 = (bf16[768,1024]{1,0:T(8,128)(2,1)S(1)}, bf16[768,1024]{1,0:T(8,128)(2,1)S(1)}, u32[]{:S(2)}, u32[]{:S(2)}) collective-permute-start(bf16[768,1024]{1,0:T(8,128)(2,1)S(1)} %pad_maximum_fusion.3), channel_id=1, source_target_pairs={{0,1},{1,0},{2,3},{3,2},{4,5},{5,4},{6,7},{7,6},{8,9},{9,8},{10,11... | collective-permute-start | bytes 4718600 | tf_op jit(solution)/shard_map/ppermute | solution.py:36
  151.3 5.3 %collective-permute-start.24 = (bf16[768,1024]{1,0:T(8,128)(2,1)S(1)}, bf16[768,1024]{1,0:T(8,128)(2,1)S(1)}, u32[]{:S(2)}, u32[]{:S(2)}) collective-permute-start(bf16[768,1024]{1,0:T(8,128)(2,1)S(1)} %copy-done.9), channel_id=1, source_target_pairs={{0,1},{1,0},{2,3},{3,2},{4,5},{5,4},{6,7},{7,6},{8,9},{9,8},{10,11... | collective-permute-start | bytes 4718600 | tf_op jit(solution)/shard_map/ppermute | solution.py:36
  166.3 11.2 %collective-permute-start.27 = (bf16[384,1024]{1,0:T(8,128)(2,1)S(1)}, bf16[384,1024]{1,0:T(8,128)(2,1)S(1)}, u32[]{:S(2)}, u32[]{:S(2)}) collective-permute-start(bf16[384,1024]{1,0:T(8,128)(2,1)S(1)} %slice.299), channel_id=1, source_target_pairs={{0,96},{1,33},{2,98},{3,35},{4,100},{5,37},{6,102},{7,39},{8,104},... | collective-permute-start | bytes 2359304 | tf_op jit(solution)/shard_map/ppermute | solution.py:36
  177.8 7.9 %collective-permute-start.28 = (bf16[192,1024]{1,0:T(8,128)(2,1)S(1)}, bf16[192,1024]{1,0:T(8,128)(2,1)S(1)}, u32[]{:S(2)}, u32[]{:S(2)}) collective-permute-start(bf16[192,1024]{1,0:T(8,128)(2,1)S(1)} %slice.301), channel_id=1, source_target_pairs={{0,32},{1,97},{2,34},{3,99},{4,36},{5,101},{6,38},{7,103},{8,40},{... | collective-permute-start | bytes 1179656 | tf_op jit(solution)/shard_map/ppermute | solution.py:36
  187.4 7.8 %collective-permute-start.29 = (bf16[192,1024]{1,0:T(8,128)(2,1)S(1)}, bf16[192,1024]{1,0:T(8,128)(2,1)S(1)}, u32[]{:S(2)}, u32[]{:S(2)}) collective-permute-start(bf16[192,1024]{1,0:T(8,128)(2,1)S(1)} %get-tuple-element.107), channel_id=1, source_target_pairs={{0,32},{1,97},{2,34},{3,99},{4,36},{5,101},{6,38},{7,103},{8,40},{... | collective-permute-start | bytes 1179656 | tf_op jit(solution)/shard_map/ppermute | solution.py:36
  190.6 22.6 %collective-permute-start.32 = (bf16[8,64,1152]{2,1,0:T(8,128)(2,1)}, bf16[8,64,1152]{2,1,0:T(8,128)(2,1)}, u32[]{:S(2)}, u32[]{:S(2)}) collective-permute-start(bf16[8,64,1152]{2,1,0:T(8,128)(2,1)} %constant_dynamic-slice_fusion.6), channel_id=1, source_target_pairs={{0,24},{1,7},{2,26},{3,5},{4,28},{5,3},{6,30},{7,1},{8,16},{9,15},... | collective-permute-start | bytes 3538952 | tf_op jit(solution)/shard_map/ppermute | solution.py:36
  196.1 11.5 %collective-permute-start.30 = (bf16[384,1024]{1,0:T(8,128)(2,1)}, bf16[384,1024]{1,0:T(8,128)(2,1)}, u32[]{:S(2)}, u32[]{:S(2)}) collective-permute-start(bf16[384,1024]{1,0:T(8,128)(2,1)} %pad_maximum_fusion.12), channel_id=1, source_target_pairs={{0,96},{1,33},{2,98},{3,35},{4,100},{5,37},{6,102},{7,39},{8,104},... | collective-permute-start | bytes 2359304 | tf_op jit(solution)/shard_map/ppermute | solution.py:36
  208.8 9.7 %collective-permute-start.31 = (bf16[768,1024]{1,0:T(8,128)(2,1)S(1)}, bf16[768,1024]{1,0:T(8,128)(2,1)S(1)}, u32[]{:S(2)}, u32[]{:S(2)}) collective-permute-start(bf16[768,1024]{1,0:T(8,128)(2,1)S(1)} %constant_dynamic-update-slice_fusion.12.own_ref), channel_id=1, source_target_pairs={{0,1},{1,0},{2,3},{3,2},{4,5},{5,4},{6,7},{7,6},{8,9},{9,8},{10,11... | collective-permute-start | bytes 4718600 | tf_op jit(solution)/shard_map/ppermute | solution.py:36
  217.1 19.4 %collective-permute-start.33 = (bf16[4,64,1152]{2,1,0:T(8,128)(2,1)}, bf16[4,64,1152]{2,1,0:T(8,128)(2,1)}, u32[]{:S(2)}, u32[]{:S(2)}) collective-permute-start(bf16[4,64,1152]{2,1,0:T(8,128)(2,1)} %constant_dynamic-slice_fusion.5), channel_id=1, source_target_pairs={{0,8},{1,3},{2,10},{3,1},{4,12},{5,7},{6,14},{7,5},{8,0},{9,11},{1... | collective-permute-start | bytes 1769480 | tf_op jit(solution)/shard_map/ppermute | solution.py:36
  257.6 12.2 %collective-permute-start.34 = (bf16[768,1024]{1,0:T(8,128)(2,1)}, bf16[768,1024]{1,0:T(8,128)(2,1)}, u32[]{:S(2)}, u32[]{:S(2)}) collective-permute-start(bf16[768,1024]{1,0:T(8,128)(2,1)} %get-tuple-element.105), channel_id=1, source_target_pairs={{0,1},{1,0},{2,3},{3,2},{4,5},{5,4},{6,7},{7,6},{8,9},{9,8},{10,11... | collective-permute-start | bytes 4718600 | tf_op jit(solution)/shard_map/ppermute | solution.py:36
  260.3 19.1 %collective-permute-start.40 = (bf16[8,64,896]{2,1,0:T(8,128)(2,1)}, bf16[8,64,896]{2,1,0:T(8,128)(2,1)}, u32[]{:S(2)}, u32[]{:S(2)}) collective-permute-start(bf16[8,64,896]{2,1,0:T(8,128)(2,1)} %fusion.6), channel_id=1, source_target_pairs={{0,24},{1,7},{2,26},{3,5},{4,28},{5,3},{6,30},{7,1},{8,16},{9,15},... | collective-permute-start | bytes 2752520 | tf_op jit(solution)/shard_map/ppermute | solution.py:36
  261.6 76.0 %collective-permute-start.36 = (bf16[192,1024]{1,0:T(8,128)(2,1)}, bf16[192,1024]{1,0:T(8,128)(2,1)}, u32[]{:S(2)}, u32[]{:S(2)}) collective-permute-start(bf16[192,1024]{1,0:T(8,128)(2,1)} %copy-done.17), channel_id=1, source_target_pairs={{0,0},{1,16},{2,2},{3,18},{4,4},{5,20},{6,6},{7,22},{8,8},{9,24},{... | collective-permute-start | bytes 1179656 | tf_op jit(solution)/shard_map/ppermute | solution.py:44
  267.9 11.5 %collective-permute-start.44 = (bf16[2,64,1152]{2,1,0:T(8,128)(2,1)S(1)}, bf16[2,64,1152]{2,1,0:T(8,128)(2,1)S(1)}, u32[]{:S(2)}, u32[]{:S(2)}) collective-permute-start(bf16[2,64,1152]{2,1,0:T(8,128)(2,1)S(1)} %constant_dynamic-slice_fusion.1), channel_id=1, source_target_pairs={{0,6},{1,25},{2,4},{3,27},{4,2},{5,29},{6,0},{7,31},{8,14},{9,17},... | collective-permute-start | bytes 884744 | tf_op jit(solution)/shard_map/ppermute | solution.py:36
  280.9 7.8 %collective-permute-start.41 = (bf16[4,64,896]{2,1,0:T(8,128)(2,1)S(1)}, bf16[4,64,896]{2,1,0:T(8,128)(2,1)S(1)}, u32[]{:S(2)}, u32[]{:S(2)}) collective-permute-start(bf16[4,64,896]{2,1,0:T(8,128)(2,1)S(1)} %constant_dynamic-slice_fusion.4), channel_id=1, source_target_pairs={{0,8},{1,3},{2,10},{3,1},{4,12},{5,7},{6,14},{7,5},{8,0},{9,11},{1... | collective-permute-start | bytes 1376264 | tf_op jit(solution)/shard_map/ppermute | solution.py:36
  281.5 8.8 %collective-permute-start.45 = (bf16[1,64,1152]{2,1,0:T(8,128)(2,1)S(1)}, bf16[1,64,1152]{2,1,0:T(8,128)(2,1)S(1)}, u32[]{:S(2)}, u32[]{:S(2)}) collective-permute-start(bf16[1,64,1152]{2,1,0:T(8,128)(2,1)S(1)} %constant_dynamic-slice_fusion), channel_id=1, source_target_pairs={{0,2},{1,9},{2,0},{3,11},{4,6},{5,13},{6,4},{7,15},{8,10},{9,1},{1... | collective-permute-start | bytes 442376 | tf_op jit(solution)/shard_map/ppermute | solution.py:36
  282.4 17.6 %collective-permute-start.37 = (bf16[384,1024]{1,0:T(8,128)(2,1)S(1)}, bf16[384,1024]{1,0:T(8,128)(2,1)S(1)}, u32[]{:S(2)}, u32[]{:S(2)}) collective-permute-start(bf16[384,1024]{1,0:T(8,128)(2,1)S(1)} %slice.298), channel_id=1, source_target_pairs={{0,96},{1,33},{2,98},{3,35},{4,100},{5,37},{6,102},{7,39},{8,104},... | collective-permute-start | bytes 2359304 | tf_op jit(solution)/shard_map/ppermute | solution.py:36
  288.9 6.5 %collective-permute-start.42 = (bf16[2,64,896]{2,1,0:T(8,128)(2,1)S(1)}, bf16[2,64,896]{2,1,0:T(8,128)(2,1)S(1)}, u32[]{:S(2)}, u32[]{:S(2)}) collective-permute-start(bf16[2,64,896]{2,1,0:T(8,128)(2,1)S(1)} %constant_dynamic-slice_fusion.3), channel_id=1, source_target_pairs={{0,6},{1,25},{2,4},{3,27},{4,2},{5,29},{6,0},{7,31},{8,14},{9,17},... | collective-permute-start | bytes 688136 | tf_op jit(solution)/shard_map/ppermute | solution.py:36
  295.5 4.7 %collective-permute-start.43 = (bf16[1,64,896]{2,1,0:T(8,128)(2,1)S(1)}, bf16[1,64,896]{2,1,0:T(8,128)(2,1)S(1)}, u32[]{:S(2)}, u32[]{:S(2)}) collective-permute-start(bf16[1,64,896]{2,1,0:T(8,128)(2,1)S(1)} %constant_dynamic-slice_fusion.2), channel_id=1, source_target_pairs={{0,2},{1,9},{2,0},{3,11},{4,6},{5,13},{6,4},{7,15},{8,10},{9,1},{1... | collective-permute-start | bytes 344072 | tf_op jit(solution)/shard_map/ppermute | solution.py:36
  300.3 13.7 %collective-permute-start.46 = (bf16[4,1,8,1408]{3,2,1,0:T(8,128)(2,1)S(1)}, bf16[4,1,8,1408]{3,2,1,0:T(8,128)(2,1)S(1)}, u32[]{:S(2)}, u32[]{:S(2)}) collective-permute-start(bf16[4,1,8,1408]{3,2,1,0:T(8,128)(2,1)S(1)} %fusion.20), channel_id=1, source_target_pairs={{0,1},{1,0},{2,3},{3,2},{4,5},{5,4},{6,7},{7,6},{8,9},{9,8},{10,11... | collective-permute-start | bytes 270344 | tf_op jit(solution)/shard_map/ppermute | solution.py:36
  306.9 21.2 %collective-permute-start.38 = (bf16[192,1024]{1,0:T(8,128)(2,1)}, bf16[192,1024]{1,0:T(8,128)(2,1)S(1)}, u32[]{:S(2)}, u32[]{:S(2)}) collective-permute-start(bf16[192,1024]{1,0:T(8,128)(2,1)} %get-tuple-element.128), channel_id=1, source_target_pairs={{0,0},{1,16},{2,2},{3,18},{4,4},{5,20},{6,6},{7,22},{8,8},{9,24},{... | collective-permute-start | bytes 1179656 | tf_op jit(solution)/shard_map/ppermute | solution.py:44
  311.4 6.7 %collective-permute-start.50 = (bf16[16,1024]{1,0:T(8,128)(2,1)S(1)}, bf16[16,1024]{1,0:T(8,128)(2,1)S(1)}, u32[]{:S(2)}, u32[]{:S(2)}) collective-permute-start(bf16[16,1024]{1,0:T(8,128)(2,1)S(1)} %bitcast.247), channel_id=1, source_target_pairs={{0,0},{1,16},{2,2},{3,18},{4,4},{5,20},{6,6},{7,22},{8,8},{9,24},{... | collective-permute-start | bytes 98312 | tf_op jit(solution)/shard_map/ppermute | solution.py:44
  314.1 6.5 %collective-permute-start.47 = (bf16[1,2,8,1408]{3,2,1,0:T(8,128)(2,1)S(1)}, bf16[1,2,8,1408]{3,2,1,0:T(8,128)(2,1)S(1)}, u32[]{:S(2)}, u32[]{:S(2)}) collective-permute-start(bf16[1,2,8,1408]{3,2,1,0:T(8,128)(2,1)S(1)} %get-tuple-element.137), channel_id=1, source_target_pairs={{0,32},{1,33},{2,34},{3,35},{4,36},{5,37},{6,38},{7,39},{8,40},{9,... | collective-permute-start | bytes 135176 | tf_op jit(solution)/shard_map/ppermute | solution.py:36
  314.1 9.8 %collective-permute-start.48 = (bf16[1,2,8,1408]{3,2,1,0:T(8,128)(2,1)S(1)}, bf16[1,2,8,1408]{3,2,1,0:T(8,128)(2,1)S(1)}, u32[]{:S(2)}, u32[]{:S(2)}) collective-permute-start(bf16[1,2,8,1408]{3,2,1,0:T(8,128)(2,1)S(1)} %get-tuple-element.138), channel_id=1, source_target_pairs={{0,64},{1,65},{2,66},{3,67},{4,68},{5,69},{6,70},{7,71},{8,72},{9,... | collective-permute-start | bytes 135176 | tf_op jit(solution)/shard_map/ppermute | solution.py:36
  318.2 5.8 %collective-permute-start.49 = (bf16[1,2,8,1408]{3,2,1,0:T(8,128)(2,1)S(1)}, bf16[1,2,8,1408]{3,2,1,0:T(8,128)(2,1)S(1)}, u32[]{:S(2)}, u32[]{:S(2)}) collective-permute-start(bf16[1,2,8,1408]{3,2,1,0:T(8,128)(2,1)S(1)} %get-tuple-element.139), channel_id=1, source_target_pairs={{0,96},{1,97},{2,98},{3,99},{4,100},{5,101},{6,102},{7,103},{8,104... | collective-permute-start | bytes 135176 | tf_op jit(solution)/shard_map/ppermute | solution.py:36
  320.6 9.6 %collective-permute-start.39 = (bf16[192,1024]{1,0:T(8,128)(2,1)S(1)}, bf16[192,1024]{1,0:T(8,128)(2,1)S(1)}, u32[]{:S(2)}, u32[]{:S(2)}) collective-permute-start(bf16[192,1024]{1,0:T(8,128)(2,1)S(1)} %get-tuple-element.129), channel_id=1, source_target_pairs={{0,32},{1,112},{2,34},{3,114},{4,36},{5,116},{6,38},{7,118},{8,40}... | collective-permute-start | bytes 1179656 | tf_op jit(solution)/shard_map/ppermute | solution.py:54
  331.6 11.3 %collective-permute-start.35 = (bf16[192,1024]{1,0:T(8,128)(2,1)S(1)}, bf16[192,1024]{1,0:T(8,128)(2,1)S(1)}, u32[]{:S(2)}, u32[]{:S(2)}) collective-permute-start(bf16[192,1024]{1,0:T(8,128)(2,1)S(1)} %add_convert_fusion.6), channel_id=1, source_target_pairs={{0,0},{1,16},{2,2},{3,18},{4,4},{5,20},{6,6},{7,22},{8,8},{9,24},{... | collective-permute-start | bytes 1179656 | tf_op jit(solution)/shard_map/ppermute | solution.py:44
  (36 other events, 441.3 us)
Sparse Core Ops, SparseCore 0:
  261.7 37.1 reduce-scatter.1

commit v2 on v1

--- a/solution.py
+++ b/solution.py
@@ -50,12 +50,6 @@
     )
 
 
-def swap_and_cross(values, masks):
-    return lax.ppermute(
-        values, AXES, [(k, crossed(k ^ masks[k & 1])) for k in range(DEVICES)]
-    )
-
-
 def after(value, *others):
     return lax.optimization_barrier((value, *others))[0] if others else value
 
@@ -136,7 +130,7 @@
 
 def cost(microseconds):
     return pl.CostEstimate(
-        flops=0, bytes_accessed=int(microseconds * 3.6e6), transcendentals=0
+        flops=0, bytes_accessed=int(microseconds * 0.1e6), transcendentals=0
     )
 
 
@@ -195,16 +189,16 @@
         + [whole_spec((1, WIDTH)), whole_spec((1, HEAD)), whole_spec((1, HEAD))]
         + [pack_spec(HEAD), pack_spec(HEAD)],
         [pack_spec(WIDTH), pack_spec(3 * HEAD), pack_spec(512), pack_spec(512)]
-        + [whole_spec((512, WIDTH))],
+        + [whole_spec((512, WIDTH)), whole_spec((WIDTH, 512))],
         [
             shaped((PACK, WIDTH), jnp.bfloat16, True),
             shaped((PACK, 3 * HEAD), jnp.float32, True),
             shaped((PACK, 512), jnp.bfloat16),
             shaped((PACK, 512), jnp.bfloat16, True),
             shaped((512, WIDTH), jnp.bfloat16, True),
+            shaped((WIDTH, 512), jnp.bfloat16, True),
         ],
         8, spots, own, other, heads, gain_attn, gain_query, gain_key, cosine, sine,
-        scratch=[pltpu.VMEM((WIDTH, 512), jnp.bfloat16)],
     )
 
 
@@ -261,15 +255,19 @@
 
     @pl.when(step == pl.num_programs(0) - 1)
     def _():
-        d_w_ref[...] = low(total_ref[...])
+        for block in range(16):
+            row = (block % 8 * 2 + block // 8) * 16
+            for n in range(4):
+                piece = total_ref[row : row + 16, n * 256 : n * 256 + 256]
+                d_w_ref[block, n * 16 : n * 16 + 16, :] = low(piece)
 
 
 def out_back(spots, own, other, attended, weights):
     return ring_call(
         out_back_kernel, "out_back",
         ring_specs(WIDTH) + [pack_spec(256), whole_spec((256, WIDTH))],
-        [pack_spec(256), whole_spec((256, WIDTH))],
-        [shaped((PACK, 256), jnp.bfloat16), shaped((256, WIDTH), jnp.bfloat16, True)],
+        [pack_spec(256), pl.BlockSpec((16, 64, 256), lambda x, spots: (0, 0, 0))],
+        [shaped((PACK, 256), jnp.bfloat16), shaped((16, 64, 256), jnp.bfloat16, True)],
         5, spots, own, other, in_hbm(attended), in_hbm(weights),
         scratch=[pltpu.VMEM((2 * TOK, WIDTH), jnp.bfloat16), pltpu.VMEM((256, WIDTH), jnp.float32)],
     )
@@ -429,12 +427,10 @@
 
 
 def qkv_back_kernel(
-    spots, pre_ref, dq_ref, dk_ref, dv_ref, cos_ref, sin_ref, normed_ref, w_ref, gq_ref, gk_ref,
-    d_pre_ref, d_attn_ref, d_head_ref, own_ref, other_ref, rows_ref,
+    spots, pre_ref, dq_ref, dk_ref, dv_ref, cos_ref, sin_ref, gq_ref, gk_ref, d_pre_ref, d_head_ref
 ):
     @pl.when(pl.program_id(0) == 0)
     def _():
-        d_attn_ref[...] = jnp.zeros_like(d_attn_ref)
         d_head_ref[...] = jnp.zeros_like(d_head_ref)
 
     cosine, sine = cos_ref[...], sin_ref[...]
@@ -444,32 +440,37 @@
         grad = dk_ref[...] if h == 2 else dq_ref[:, h * HEAD : (h + 1) * HEAD]
         grad = rope_back(grad, cosine, sine)
         row = 1 if h == 2 else 0
-        d_head_ref[row : row + 1, :] += jnp.sum(
-            grad * u * norm_scale(u), axis=0, keepdims=True
-        )
-        d_pre_ref[:, h * HEAD : (h + 1) * HEAD] = low(norm_back(u, gain, grad))
+        scale = norm_scale(u)
+        normal = u * scale
+        d_head_ref[row : row + 1, :] += jnp.sum(grad * normal, axis=0, keepdims=True)
+        inner = grad * gain
+        inner = scale * (inner - normal * jnp.mean(inner * normal, axis=-1, keepdims=True))
+        d_pre_ref[:, h * HEAD : (h + 1) * HEAD] = low(inner)
     d_pre_ref[:, 3 * HEAD :] = low(dv_ref[...])
-    d_normed = dot(d_pre_ref[...], w_ref[...])
-    d_attn_ref[...] += jnp.sum(wide(normed_ref[...]) * d_normed, axis=0, keepdims=True)
-    rows_ref[...] = low(d_normed)
-    own_ref[...] = rows_ref[own_rows(spots), :]
-    other_ref[...] = rows_ref[other_rows(spots), :]
-
-
-def project_back(spots, pre, d_query, d_key, d_value, cosine, sine, normed, weights, gain_query, gain_key):
-    half = shaped((PACK // 2, WIDTH), jnp.bfloat16)
+
+
+def project_back(spots, pre, d_query, d_key, d_value, cosine, sine, gain_query, gain_key):
     return ring_call(
         qkv_back_kernel,
         "project_back",
         [pack_spec(3 * HEAD), pack_spec(2 * HEAD), pack_spec(HEAD), pack_spec(HEAD)]
-        + [pack_spec(HEAD), pack_spec(HEAD), pack_spec(WIDTH)]
-        + [whole_spec((512, WIDTH)), whole_spec((1, HEAD)), whole_spec((1, HEAD))],
-        [pack_spec(512), whole_spec((1, WIDTH)), whole_spec((2, HEAD))] + ring_specs(WIDTH),
-        [shaped((PACK, 512), jnp.bfloat16), shaped((1, WIDTH), jnp.float32)]
-        + [shaped((2, HEAD), jnp.float32), half, half],
-        11, spots, in_hbm(pre), d_query, d_key, d_value, in_hbm(cosine), in_hbm(sine), in_hbm(normed),
-        in_hbm(weights), gain_query, gain_key,
-        scratch=[pltpu.VMEM((2 * TOK, WIDTH), jnp.bfloat16)],
+        + [pack_spec(HEAD), pack_spec(HEAD), whole_spec((1, HEAD)), whole_spec((1, HEAD))],
+        [pack_spec(512), whole_spec((2, HEAD))],
+        [shaped((PACK, 512), jnp.bfloat16), shaped((2, HEAD), jnp.float32)],
+        5, spots, in_hbm(pre), d_query, d_key, d_value, in_hbm(cosine), in_hbm(sine), gain_query, gain_key,
+    )
+
+
+def normed_back_kernel(spots, d_pre_ref, w_ref, own_ref, other_ref):
+    own_ref[...] = low(dot(d_pre_ref[own_rows(spots), :], w_ref[...]))
+    other_ref[...] = low(dot(d_pre_ref[other_rows(spots), :], w_ref[...]))
+
+
+def normed_back(spots, d_pre, weights):
+    half = shaped((PACK // 2, WIDTH), jnp.bfloat16)
+    return ring_call(
+        normed_back_kernel, "normed_back", [pack_spec(512), whole_spec((512, WIDTH))], ring_specs(WIDTH),
+        [half, half], 4, spots, d_pre, in_hbm(weights),
     )
 
 
@@ -495,12 +496,23 @@
     return plane_order(index & 1, block.reshape((4, 4) + shape)).reshape((16,) + shape)
 
 
-def scatter_plane_step(index, blocks, step, *beside):
+def plane_halves(index, blocks, step):
     later = plane_bit(index, PLANE_STEPS[step])
     half = blocks.shape[0] // 2
     keep = lax.dynamic_slice_in_dim(blocks, later * half, half, axis=0)
     send = lax.dynamic_slice_in_dim(blocks, (1 - later) * half, half, axis=0)
-    return low(wide(keep) + wide(after(swap(send, *PLANE_STEPS[step]), *beside)))
+    return keep, swap(send, *PLANE_STEPS[step])
+
+
+def scatter_plane_step(index, blocks, step, *beside):
+    keep, got = plane_halves(index, blocks, step)
+    return low(wide(keep) + wide(after(got, *beside)))
+
+
+def plane_rest(index, blocks):
+    place = jnp.where(index & 1 == 1, index >> 3, index >> 1) & 3
+    block = lambda at: lax.dynamic_index_in_dim(blocks, at, 0, keepdims=False)
+    return block(place), [swap(block(place ^ k), k << 1, k << 3) for k in range(1, 4)]
 
 
 def plane_blocks(core, blocks):
@@ -593,22 +605,21 @@
         axis=2,
     )
     digits = jnp.pad(low(jnp.stack([lengths[0] // 64, lengths[0] % 64])), ((0, 14), (0, WIDTH - 3)))
-    rows = after(jnp.concatenate([hidden[0], w_out, digits], axis=0), local)
-    d_rows = after(cotangent[0], local)
+    pieces = cross(jnp.concatenate([w_out, digits], axis=0))
+    rows = after(hidden[0], local)
+    inputs = cross(rows)
+    second = cross_and_swap(rows, RING_STEPS[0])
+    digits = pieces[16:18, :3].astype(jnp.int32)
+    lengths = (digits[0] * 64 + digits[1])[None]
+    pieces = pieces[:16].reshape(16, 4, 256).transpose(1, 0, 2).reshape(64, 256)
     local = exchange_ring(index, local).reshape(64, 1408)
-    first = cross(rows)
-    second = cross_and_swap(rows[:TOK], RING_STEPS[0])
-    d_result = cross(d_rows)
-    d_result_second = cross_and_swap(d_rows, RING_STEPS[0])
-    inputs = first[:TOK]
-    digits = first[TOK + 16 : TOK + 18, :3].astype(jnp.int32)
-    lengths = (digits[0] * 64 + digits[1])[None]
-    pieces = first[TOK : TOK + 16].reshape(16, 4, 256).transpose(1, 0, 2).reshape(64, 256)
+    d_result = cross(after(cotangent[0], local))
     heads = jnp.concatenate([local[:, :640], pieces], axis=1)[None]
-    heads = gather_plane_step(index, heads, 0)
-    second = after(second, heads)
-    for step in range(1, 4):
-        heads = gather_plane_step(index, heads, step)
+    heads = gather_plane_step(index, after(heads, inputs, second), 0)
+    heads = gather_plane_step(index, after(heads, d_result), 1)
+    d_result_own = jnp.concatenate([d_result, swap(d_result, *RING_STEPS[0])], axis=0)
+    heads = gather_plane_step(index, heads, 2)
+    heads = gather_plane_step(index, after(heads, d_result_own), 3)
     gain_all = plane_order(core, heads[:, ::8, 512:530].reshape(4, 4, 8, 18))
     gain_all = gain_all.reshape(16, 4, 2, 18).transpose(1, 0, 2, 3)
     gain_all = wide(gain_all.reshape(1, -1))
@@ -630,10 +641,8 @@
     cosine = jnp.concatenate([cosine, cosine], axis=1)
     sine = jnp.concatenate([-sine, sine], axis=1)
 
-    d_result_own = jnp.concatenate([d_result, d_result_second], axis=0)
     d_result_own = jnp.concatenate([d_result_own, swap(d_result_own, *RING_STEPS[1])], axis=0)
-    heads, d_result, d_result_second = lax.optimization_barrier((heads, d_result, d_result_second))
-    normed, pre, qkv, qkv_kept, w_heads_across = project(
+    normed, pre, qkv, qkv_kept, w_heads_across, w_heads = project(
         spots, inputs_own, inputs_other, heads, gain_attn, gain_query, gain_key, cosine, sine
     )
     qkv, d_result_own = lax.optimization_barrier((qkv, d_result_own))
@@ -683,51 +692,74 @@
     grads = plane_blocks(core, grads)
     act_own, act_other = (after(act, d_middle) for act in (act_own, act_other))
     result = to_pack(spots, act_own, act_other, full_down)
-    d_branch_own = gather_ring(after(low(d_middle), grads), ((), (result,)))
-    sums = scatter_plane_step(index, grads, 3, d_branch_own)
+    keep, got = plane_halves(index, grads, 3)
+    d_branch_own = gather_ring(after(low(d_middle), grads), ((), (result, got)))
+    sums = low(wide(keep) + wide(got))
     d_branch_other = swap(d_branch_own, CORE)
     result = lax.psum_scatter(after(result, d_branch_own), RING, scatter_dimension=0, tiled=True)
-    d_middle_home = jnp.where(straight, d_middle, wide(cross(after(low(d_middle), d_branch_own))))
 
     d_attended, grad_out = out_back(spots, d_branch_own, d_branch_other, attended_kept, w_rows)
+    grad_out = plane_blocks(core, grad_out)
+    d_attended, grad_out = lax.optimization_barrier((d_attended, grad_out))
+    sums_keep, sums_got = plane_halves(index, sums, 2)
+    out_keep, out_got = plane_halves(index, grad_out, 3)
     d_query, d_key, d_value = attend_back(ends, qkv_kept, d_attended, attended_kept, inverse_total)
-    sums = scatter_plane_step(index, sums, 2, d_query)
-    grad_out = grad_out.reshape(8, 2, 16, 4, 256).transpose(1, 0, 3, 2, 4).reshape(16, 64, 256)
-    grad_out = plane_blocks(core, grad_out)
-    d_query, sums, grad_out = lax.optimization_barrier((d_query, sums, grad_out))
-    d_pre, d_gain_attn, d_gain_heads, d_normed_own, d_normed_other = project_back(
-        spots, pre, d_query, d_key, d_value, cosine, sine, normed, w_heads_across, gain_query, gain_key
-    )
-    d_normed_steps = scatter_ring(d_normed_own, d_normed_other, 1)
-    halves = low(d_normed_steps[1][:TOK]), low(d_normed_steps[1][TOK:])
-    d_normed = wide(cross(halves[0])) + wide(swap_and_cross(halves[1], RING_STEPS[0]))
-    input_grad = d_middle_home + norm_back(wide(hidden[0]), gain_attn, d_normed)
-
-    d_gains = jnp.concatenate(
-        [(d_gain_attn / gain_attn)[0], d_gain_mlp, d_gain_heads.reshape(-1)]
-    )
+    d_query, sums_got, out_got = lax.optimization_barrier((d_query, sums_got, out_got))
+    sums_keep, sums_got = plane_rest(index, low(wide(sums_keep) + wide(sums_got)))
+    sums_out = low(wide(out_keep) + wide(out_got))
+    d_pre, d_gain_heads = project_back(
+        spots, pre, d_query, d_key, d_value, cosine, sine, gain_query, gain_key
+    )
+    d_pre, sums_got = lax.optimization_barrier((d_pre, sums_got))
+    sums = wide(sums_keep) + sum(wide(got) for got in sums_got)
+    grad_heads = contract_rows(normed, d_pre)
+    d_gain_attn = jnp.sum(grad_heads * wide(w_heads), axis=1) / gain_attn[0]
+    d_gains = jnp.concatenate([d_gain_attn, d_gain_mlp, d_gain_heads.reshape(-1)])
     d_gains = d_gains.reshape(4, 16, 2, 1, 18).transpose(1, 0, 2, 3, 4)
     payload = jnp.concatenate(
         [
-            rows_by_plane(low(contract_rows(normed, d_pre))),
+            rows_by_plane(low(grad_heads)),
             low(jnp.pad(d_gains, ((0, 0),) * 3 + ((0, 7), (0, 110)))).reshape(16, 64, 128),
         ],
         axis=2,
     )
-    heads_sums = jnp.concatenate([plane_blocks(core, payload), grad_out], axis=2)
-    heads_sums = scatter_plane_step(index, heads_sums, 3, d_normed_steps[0])
-    sums = scatter_plane_step(index, sums, 1, d_normed_steps[0])
-    sums = scatter_plane_step(index, sums, 0)[0]
-    for step in (2, 1, 0):
-        heads_sums = scatter_plane_step(index, heads_sums, step)
-    ring_grads = jnp.concatenate([heads_sums[0, :, :640], sums[:, :768]], axis=1)
+    payload = plane_blocks(core, payload)
+    d_pre, payload, result = lax.optimization_barrier((d_pre, payload, result))
+    d_normed_own, d_normed_other = normed_back(spots, d_pre, w_heads_across)
+    out_keep, out_got = plane_halves(index, sums_out, 2)
+    got, out_got = lax.optimization_barrier((swap(d_normed_other, CORE), out_got))
+    sums_out = low(wide(out_keep) + wide(out_got))
+    total = wide(d_normed_own) + wide(got)
+    keep, send = total[: 2 * TOK], low(total[2 * TOK :])
+    payload, sums_out = (after(array, send) for array in (payload, sums_out))
+    heads_keep, heads_got = plane_halves(index, payload, 3)
+    out_keep, out_got = plane_rest(index, sums_out)
+    got, heads_got, out_got = lax.optimization_barrier(
+        (swap(send, *RING_STEPS[1]), heads_got, out_got)
+    )
+    sum_out = wide(out_keep) + sum(wide(part) for part in out_got)
+    heads_sums = low(wide(heads_keep) + wide(heads_got))
+    total = keep + wide(got)
+    heads_keep, heads_got = plane_halves(index, heads_sums, 2)
+    got, heads_got = lax.optimization_barrier(
+        (swap(low(total[TOK:]), *RING_STEPS[0]), heads_got)
+    )
+    heads_sums = low(wide(heads_keep) + wide(heads_got))
+    d_normed = total[:TOK] + wide(got)
+    input_grad = d_middle + norm_back(wide(inputs), gain_attn, d_normed)
+    heads_keep, heads_got = plane_rest(index, heads_sums)
+    home, heads_got = lax.optimization_barrier((cross(low(input_grad)), heads_got))
+    input_grad = jnp.where(straight, input_grad, wide(home))
+    heads_sums = low(wide(heads_keep) + sum(wide(part) for part in heads_got))
+    sum_down = tiles_flat(sums[:, 768:])
+    sum_out = sum_out.reshape(4, 16, 256).transpose(1, 0, 2).reshape(16, WIDTH)
+    result = jnp.concatenate([middle + wide(result), sum_out], axis=0)
+    result = cross(after(low(result), heads_sums))
+    ring_grads = jnp.concatenate([heads_sums, low(sums[:, :768])], axis=1)
     ring_grads = exchange_ring(index, ring_grads.reshape(8, 8, 1408))
     heads_grad, units_grad = wide(ring_grads[..., :640]), ring_grads[..., 640:]
-    sum_down = wide(tiles_flat(sums[:, 768:]))
-    sum_out = heads_sums[0, :, 640:].reshape(4, 16, 256).transpose(1, 0, 2).reshape(16, WIDTH)
-    sum_out = wide(sum_out)
-    sum_out = jnp.where(straight, sum_out, wide(cross(low(sum_out))))
-    activations = cross(after(low(middle + wide(result)), d_normed_steps[0]))
+    activations = result[:TOK]
+    sum_out = jnp.where(straight, sum_out, wide(result[TOK:]))
     column = jnp.arange(768, dtype=jnp.int32)
     column = column // 24 % 2 * 384 + column // 48 * 24 + column % 24
     column = after(column, middle)

time: 357 us -> 331 us (0.927)
  waiting for transfers between devices: 108 us -> 89.1 us
  other arithmetic: 37 us -> 27.7 us
  matrix products: 15.3 us -> 19.7 us
    ppermute x6 -> x5, waiting for transfers between devices: 15.2 us -> 0.01 us  [cross(): return lax.ppermute(values, AXES, [(k, crossed(k)) for k in range(DEVICES)])]
    ppermute x42 -> x51, starting transfers between devices: 58.4 us -> 65.1 us  [swap(): lax.ppermute(values, AXES, [(k, k ^ masks[k & 1]) for k in range(DEVICES)])]
    ppermute x2 -> x1, starting transfers between devices: 6.36 us -> 1.01 us  [cross_and_swap(): lax.ppermute(values, AXES, [(crossed(k ^ masks[k & 1]), k) for k in range...]
    unnamed x73 -> x113, local copies, waits for them, and re-layouts: 5.67 us -> 11 us
    concatenate x7 -> x5, other arithmetic: 4.85 us -> 0.96 us  [the longest x1 0.76 us: on_device(): pieces = cross(jnp.concatenate([w_out, digits], axis=0))]
    pallas_call x5 -> x6, Pallas kernels: 36 us -> 34 us  [ring_call(): pl.pallas_call(kernel, grid_spec=pltpu.PrefetchScalarGridSpec(num_scalar_...]
    ppermute x42 -> x51, waiting for transfers between devices: 90.2 us -> 89.1 us  [swap(): lax.ppermute(values, AXES, [(k, k ^ masks[k & 1]) for k in range(DEVICES)])]
    ppermute x6 -> x5, starting transfers between devices: 26.1 us -> 25.8 us  [cross(): return lax.ppermute(values, AXES, [(k, crossed(k)) for k in range(DEVICES)])]
  transfers between devices with their start and end apart: 52 -> 58, of which waited for: 27 -> 32; matrix products, arithmetic and copies ran while one was open for 15% -> 16% of each run, Pallas kernels for 6% -> 8%
where the time goes in v2:
time: 331 us; the launch traced here: 325 us
  starting transfers between devices  91.9 us (28%)
  waiting for transfers between devices  89.1 us (27%)
  Pallas kernels  51.6 us (16%)
  other arithmetic  27.7 us (8%)
  local copies, waits for them, and re-layouts  27.5 us (8%)
  matrix products  19.7 us (6%)
  between operations  17.5 us (5%)
    ppermute x51, waiting for transfers between devices, swap(): lax.ppermute(values, AXES, [(k, k ^ masks[k & 1]) for k in range(DEVICES)])  89.1 us
    ppermute x51, starting transfers between devices, swap(): lax.ppermute(values, AXES, [(k, k ^ masks[k & 1]) for k in range(DEVICES)])  65.1 us
    pallas_call x6, Pallas kernels, ring_call(): pl.pallas_call(kernel, grid_spec=pltpu.PrefetchScalarGridSpec(num_scalar_...  34 us
    ppermute x5, starting transfers between devices, cross(): return lax.ppermute(values, AXES, [(k, crossed(k)) for k in range(DEVICES)])  25.8 us
    unnamed x113, local copies, waits for them, and re-layouts  11 us
    pallas_call x1, Pallas kernels, attend_back(): pl.pallas_call(attend_back_kernel, grid_spec=pltpu.PrefetchScalarGridSpec...  10.9 us
    dot_general x4, matrix products, contract_cols(): lax.dot_general(left, right, (((1,), (1,)), ((), ())), preferred_element_...  8.05 us
    pallas_call x1, Pallas kernels, attend(): pl.pallas_call(attend_kernel, grid_spec=pltpu.PrefetchScalarGridSpec(num_...  6.72 us
  transfers between devices with their start and end apart: 58, of which 32 were waited for; matrix products, arithmetic and copies ran while one was open for 16% of the time, Pallas kernels for 8%

profile of v2, /device:TPU:1, one launch (start us, length us, event | category | flops | bytes accessed | tf_op | source)
XLA Modules:
  0.0 325.0 jit_solution(10886780298528637259)
XLA Ops:
  7.3 6.9 %collective-permute-start = (bf16[192,1024]{1,0:T(8,128)(2,1)}, bf16[192,1024]{1,0:T(8,128)(2,1)S(1)}, u32[]{:S(2)}, u32[]{:S(2)}) collective-permute-start(bf16[192,1024]{1,0:T(8,128)(2,1)} %bitcast.266), channel_id=1, source_target_pairs={{0,0},{1,16},{2,2},{3,18},{4,4},{5,20},{6,6},{7,22},{8,8},{9,24},{... | collective-permute-start | bytes 1179656 | tf_op jit(solution)/shard_map/ppermute | solution.py:44
  16.6 6.4 %collective-permute-start.1 = (bf16[32,1024]{1,0:T(8,128)(2,1)S(1)}, bf16[32,1024]{1,0:T(8,128)(2,1)S(1)}, u32[]{:S(2)}, u32[]{:S(2)}) collective-permute-start(bf16[32,1024]{1,0:T(8,128)(2,1)S(1)} %pad_maximum_fusion.15), channel_id=1, source_target_pairs={{0,0},{1,16},{2,2},{3,18},{4,4},{5,20},{6,6},{7,22},{8,8},{9,24},{... | collective-permute-start | bytes 196616 | tf_op jit(solution)/shard_map/ppermute | solution.py:44
  35.0 3.5 %collective-permute-start.10 = (bf16[192,1024]{1,0:T(8,128)(2,1)S(1)}, bf16[192,1024]{1,0:T(8,128)(2,1)S(1)}, u32[]{:S(2)}, u32[]{:S(2)}) collective-permute-start(bf16[192,1024]{1,0:T(8,128)(2,1)S(1)} %bitcast.268), channel_id=1, source_target_pairs={{0,0},{1,16},{2,2},{3,18},{4,4},{5,20},{6,6},{7,22},{8,8},{9,24},{... | collective-permute-start | bytes 1179656 | tf_op jit(solution)/shard_map/ppermute | solution.py:44
  42.3 3.7 %collective-permute-done.9 = bf16[1,64,896]{2,1,0:T(8,128)(2,1)S(1)} collective-permute-done((bf16[1,64,896]{2,1,0:T(8,128)(2,1)S(1)}, bf16[1,64,896]{2,1,0:T(8,128)(2,1)S(1)}, u32[]{:S(2)}, u32[]{:S(2)}) %collective-permute-start.9) | collective-permute-done | bytes 114720 | tf_op jit(solution)/shard_map/ppermute | solution.py:36
  49.3 3.2 collective-permute-done.11
  54.8 3.0 collective-permute-done.13
  60.4 3.0 collective-permute-start.14
  63.4 2.8 fusion.11
  70.3 4.1 %collective-permute-done.14 = bf16[8,64,896]{2,1,0:T(8,128)(2,1)S(1)} collective-permute-done((bf16[8,64,896]{2,1,0:T(8,128)(2,1)S(1)}, bf16[8,64,896]{2,1,0:T(8,128)(2,1)S(1)}, u32[]{:S(2)}, u32[]{:S(2)}) %collective-permute-start.14) | collective-permute-done | bytes 917536 | tf_op jit(solution)/shard_map/ppermute | solution.py:36
  76.1 10.7 %project.1 = (bf16[1536,1024]{1,0:T(8,128)(2,1)}, f32[1536,384]{1,0:T(8,128)}, bf16[1536,512]{1,0:T(8,128)(2,1)S(1)}, bf16[1536,512]{1,0:T(8,128)(2,1)}, bf16[51...) custom-call(s32[10]{0:T(128)S(1)} %pad_add_fusion.spots, bf16[768,1024]{1,0:T(8,128)(2,1)} %constant_dynamic-update-slice_fusion.own_ref, ...), custom_call_target="tpu_custom_call" | custom-call | bytes 800000 | tf_op jit(solution)/shard_map/project/pallas_call | solution.py:138
  86.8 6.7 %attend.1 = (bf16[1536,256]{1,0:T(8,128)(2,1)S(1)}, bf16[1536,256]{1,0:T(8,128)(2,1)}, f32[2,1536]{1,0:T(2,128)}) custom-call(s32[2]{0:T(128)S(1)} %pad_add_fusion.1.ends_ref, bf16[1536,512]{1,0:T(8,128)(2,1)S(1)} %get-tuple-element.86.q_ref.k_ref.v_ref, bf16[1536,512]{1,0:T(8,128)(2,1)S(1)} %get-tuple-element.86.q_ref.k_ref.v_ref, ...), custom_call_target="tpu_custom_call" | custom-call | bytes 600000 | tf_op jit(solution)/shard_map/attend/pallas_call | solution.py:331
  93.5 2.9 to_ring.1
  97.5 3.0 collective-permute-done.16
  102.8 4.3 %collective-permute-done.19 = bf16[1,64,1152]{2,1,0:T(8,128)(2,1)S(1)} collective-permute-done((bf16[1,64,1152]{2,1,0:T(8,128)(2,1)S(1)}, bf16[1,64,1152]{2,1,0:T(8,128)(2,1)S(1)}, u32[]{:S(2)}, u32[]{:S(2)}) %collective-permute-start.19) | collective-permute-done | bytes 147488 | tf_op jit(solution)/shard_map/ppermute | solution.py:36
  107.1 2.9 collective-permute-start.20
  110.0 2.5 collective-permute-done.17
  115.2 5.5 %collective-permute-done.18 = bf16[192,1024]{1,0:T(8,128)(2,1)S(1)} collective-permute-done((bf16[192,1024]{1,0:T(8,128)(2,1)S(1)}, bf16[192,1024]{1,0:T(8,128)(2,1)S(1)}, u32[]{:S(2)}, u32[]{:S(2)}) %collective-permute-start.18) | collective-permute-done | bytes 393248 | tf_op jit(solution)/shard_map/ppermute | solution.py:36
  123.9 2.8 collective-permute-start.22
  126.7 2.4 collective-permute-done.23
  129.2 11.1 %collective-permute-done.24 = bf16[384,1024]{1,0:T(8,128)(2,1)S(1)} collective-permute-done((bf16[384,1024]{1,0:T(8,128)(2,1)S(1)}, bf16[384,1024]{1,0:T(8,128)(2,1)S(1)}, u32[]{:S(2)}, u32[]{:S(2)}) %collective-permute-start.24) | collective-permute-done | bytes 786464 | tf_op jit(solution)/shard_map/ppermute | solution.py:36
  140.5 4.5 %collective-permute-start.26 = (bf16[768,1024]{1,0:T(8,128)(2,1)S(1)}, bf16[768,1024]{1,0:T(8,128)(2,1)S(1)}, u32[]{:S(2)}, u32[]{:S(2)}) collective-permute-start(bf16[768,1024]{1,0:T(8,128)(2,1)S(1)} %pad_maximum_fusion.2), channel_id=1, source_target_pairs={{0,1},{1,0},{2,3},{3,2},{4,5},{5,4},{6,7},{7,6},{8,9},{9,8},{10,11... | collective-permute-start | bytes 4718600 | tf_op jit(solution)/shard_map/ppermute | solution.py:36
  151.7 2.6 convolution_convert_fusion
  154.7 3.2 fusion.47
  161.8 2.8 convert_add_fusion.1
  172.2 3.9 %collective-permute-done.28 = bf16[384,1024]{1,0:T(8,128)(2,1)S(1)} collective-permute-done((bf16[384,1024]{1,0:T(8,128)(2,1)S(1)}, bf16[384,1024]{1,0:T(8,128)(2,1)S(1)}, u32[]{:S(2)}, u32[]{:S(2)}) %collective-permute-start.28) | collective-permute-done | bytes 786464 | tf_op jit(solution)/shard_map/ppermute | solution.py:36
  178.9 5.6 %collective-permute-done.29 = bf16[192,1024]{1,0:T(8,128)(2,1)S(1)} collective-permute-done((bf16[192,1024]{1,0:T(8,128)(2,1)S(1)}, bf16[192,1024]{1,0:T(8,128)(2,1)S(1)}, u32[]{:S(2)}, u32[]{:S(2)}) %collective-permute-start.29) | collective-permute-done | bytes 393248 | tf_op jit(solution)/shard_map/ppermute | solution.py:36
  188.8 2.7 collective-permute-start.32
  191.5 2.8 collective-permute-done.30
  195.2 4.1 %to_pack.1 = bf16[1536,1024]{1,0:T(8,128)(2,1)} custom-call(s32[10]{0:T(128)S(1)} %pad_add_fusion.spots, bf16[768,384]{1,0:T(8,128)(2,1)S(1)} %get-tuple-element.104.own_ref, bf16[768,384]{1,0:T(8,128)(2,1)S(1)} %get-tuple-element.105.other_ref, bf16[384,1024]{1,0:T(8,128)(2,1)S(1)} %bitcast.211), custom_call_target="tpu_custom_call" | custom-call | bytes 400000 | tf_op jit(solution)/shard_map/to_pack/pallas_call | solution.py:138
  199.4 6.3 %collective-permute-done.32 = bf16[8,64,1152]{2,1,0:T(8,128)(2,1)} collective-permute-done((bf16[8,64,1152]{2,1,0:T(8,128)(2,1)}, bf16[8,64,1152]{2,1,0:T(8,128)(2,1)}, u32[]{:S(2)}, u32[]{:S(2)}) %collective-permute-start.32) | collective-permute-done | bytes 1179680 | tf_op jit(solution)/shard_map/ppermute | solution.py:36
  207.9 3.8 %collective-permute-start.33 = (bf16[768,1024]{1,0:T(8,128)(2,1)S(1)}, bf16[768,1024]{1,0:T(8,128)(2,1)S(1)}, u32[]{:S(2)}, u32[]{:S(2)}) collective-permute-start(bf16[768,1024]{1,0:T(8,128)(2,1)S(1)} %constant_dynamic-update-slice_fusion.11.own_ref), channel_id=1, source_target_pairs={{0,1},{1,0},{2,3},{3,2},{4,5},{5,4},{6,7},{7,6},{8,9},{9,8},{10,11... | collective-permute-start | bytes 4718600 | tf_op jit(solution)/shard_map/ppermute | solution.py:36
  215.6 5.8 %out_back.1 = (bf16[1536,256]{1,0:T(8,128)(2,1)S(1)}, bf16[16,64,256]{2,1,0:T(8,128)(2,1)}) custom-call(s32[10]{0:T(128)S(1)} %pad_add_fusion.spots, bf16[768,1024]{1,0:T(8,128)(2,1)S(1)} %constant_dynamic-update-slice_fusion.11.own_ref, bf16[768,1024]{1,0:T(8,128)(2,1)S(1)} %collective-permute-done.33.other_ref, ...), custom_call_target="tpu_custom_call" | custom-call | bytes 500000 | tf_op jit(solution)/shard_map/out_back/pallas_call | solution.py:138
  222.3 2.1 bitcast_select_fusion.2
  225.4 2.3 collective-permute-start.35
  227.7 10.9 %attend_back.1 = (f32[1536,256]{1,0:T(8,128)S(1)}, f32[1536,128]{1,0:T(8,128)S(1)}, f32[1536,128]{1,0:T(8,128)S(1)}) custom-call(s32[2]{0:T(128)S(1)} %pad_add_fusion.1.ends_ref, bf16[1536,512]{1,0:T(8,128)(2,1)} %get-tuple-element.91.q_ref.k_ref.v_ref, bf16[1536,512]{1,0:T(8,128)(2,1)} %get-tuple-element.91.q_ref.k_ref.v_ref, ...), custom_call_target="tpu_custom_call" | custom-call | bytes 1100000 | tf_op jit(solution)/shard_map/attend_back/pallas_call | solution.py:403
  240.1 4.1 %collective-permute-start.37 = (bf16[64,1152]{1,0:T(8,128)(2,1)S(1)}, bf16[64,1152]{1,0:T(8,128)(2,1)S(1)}, u32[]{:S(2)}, u32[]{:S(2)}) collective-permute-start(bf16[64,1152]{1,0:T(8,128)(2,1)S(1)} %get-tuple-element.169), channel_id=1, source_target_pairs={{0,4},{1,17},{2,6},{3,19},{4,0},{5,21},{6,2},{7,23},{8,12},{9,25},... | collective-permute-start | bytes 442376 | tf_op jit(solution)/shard_map/ppermute | solution.py:36
  244.4 5.5 %project_back.1 = (bf16[1536,512]{1,0:T(8,128)(2,1)S(1)}, f32[2,128]{1,0:T(2,128)S(1)}) custom-call(s32[10]{0:T(128)S(1)} %pad_add_fusion.spots, f32[1536,384]{1,0:T(8,128)} %get-tuple-element.90.pre_ref, f32[1536,256]{1,0:T(8,128)S(1)} %get-tuple-element.115.dq_ref, f32[1536,128]{1,0:T(8,128)S(1)} %get-tuple-element.116.dk_ref, ...), custom_call_target="tpu_custom_call" | custom-call | bytes 500000 | tf_op jit(solution)/shard_map/project_back/pallas_call | solution.py:138
  253.9 5.1 %normed_back.1 = (bf16[768,1024]{1,0:T(8,128)(2,1)S(1)}, bf16[768,1024]{1,0:T(8,128)(2,1)}) custom-call(s32[10]{0:T(128)S(1)} %pad_add_fusion.spots, bf16[1536,512]{1,0:T(8,128)(2,1)S(1)} %get-tuple-element.127.d_pre_ref, bf16[512,1024]{1,0:T(8,128)(2,1)} %get-tuple-element.128.w_ref), custom_call_target="tpu_custom_call" | custom-call | bytes 400000 | tf_op jit(solution)/shard_map/normed_back/pallas_call | solution.py:138
  261.9 4.1 %collective-permute-done.40 = bf16[4,64,256]{2,1,0:T(8,128)(2,1)S(1)} collective-permute-done((bf16[4,64,256]{2,1,0:T(8,128)(2,1)S(1)}, bf16[4,64,256]{2,1,0:T(8,128)(2,1)S(1)}, u32[]{:S(2)}, u32[]{:S(2)}) %collective-permute-start.40) | collective-permute-done | bytes 131104 | tf_op jit(solution)/shard_map/ppermute | solution.py:36
  268.0 2.3 collective-permute-start.42
  271.4 3.0 collective-permute-start.45
  276.6 3.1 collective-permute-done.42
  282.8 5.4 %collective-permute-done.47 = bf16[4,64,640]{2,1,0:T(8,128)(2,1)S(1)} collective-permute-done((bf16[4,64,640]{2,1,0:T(8,128)(2,1)S(1)}, bf16[4,64,640]{2,1,0:T(8,128)(2,1)S(1)}, u32[]{:S(2)}, u32[]{:S(2)}) %collective-permute-start.47) | collective-permute-done | bytes 327712 | tf_op jit(solution)/shard_map/ppermute | solution.py:36
  288.8 4.4 %collective-permute-start.48 = (bf16[192,1024]{1,0:T(8,128)(2,1)S(1)}, bf16[192,1024]{1,0:T(8,128)(2,1)S(1)}, u32[]{:S(2)}, u32[]{:S(2)}) collective-permute-start(bf16[192,1024]{1,0:T(8,128)(2,1)S(1)} %get-tuple-element.154), channel_id=1, source_target_pairs={{0,0},{1,16},{2,2},{3,18},{4,4},{5,20},{6,6},{7,22},{8,8},{9,24},{... | collective-permute-start | bytes 1179656 | tf_op jit(solution)/shard_map/ppermute | solution.py:44
  295.0 2.5 collective-permute-start.51
  297.5 3.3 %collective-permute-done.49 = bf16[64,640]{1,0:T(8,128)(2,1)S(1)} collective-permute-done((bf16[64,640]{1,0:T(8,128)(2,1)S(1)}, bf16[64,640]{1,0:T(8,128)(2,1)S(1)}, u32[]{:S(2)}, u32[]{:S(2)}) %collective-permute-start.49) | collective-permute-done | bytes 81952 | tf_op jit(solution)/shard_map/ppermute | solution.py:36
  301.4 4.5 %collective-permute-start.52 = (bf16[208,1024]{1,0:T(8,128)(2,1)S(1)}, bf16[208,1024]{1,0:T(8,128)(2,1)S(1)}, u32[]{:S(2)}, u32[]{:S(2)}) collective-permute-start(bf16[208,1024]{1,0:T(8,128)(2,1)S(1)} %pad_maximum_fusion.11), channel_id=1, source_target_pairs={{0,0},{1,16},{2,2},{3,18},{4,4},{5,20},{6,6},{7,22},{8,8},{9,24},{... | collective-permute-start | bytes 1277960 | tf_op jit(solution)/shard_map/ppermute | solution.py:44
  307.4 2.0 collective-permute-start.55
  (353 shorter events, 103.5 us)
Async XLA Ops:
  7.2 246.6 %reduce-scatter.2.cloned.1.call-start = ((), (), s32[]{:S(2)}) async-start(), calls=%async_computation.1 | async-start | bytes 3538944 | tf_op jit(solution)/shard_map/reduce_scatter | solution.py:699
  7.3 33.3 %collective-permute-start = (bf16[192,1024]{1,0:T(8,128)(2,1)}, bf16[192,1024]{1,0:T(8,128)(2,1)S(1)}, u32[]{:S(2)}, u32[]{:S(2)}) collective-permute-start(bf16[192,1024]{1,0:T(8,128)(2,1)} %bitcast.266), channel_id=1, source_target_pairs={{0,0},{1,16},{2,2},{3,18},{4,4},{5,20},{6,6},{7,22},{8,8},{9,24},{... | collective-permute-start | bytes 1179656 | tf_op jit(solution)/shard_map/ppermute | solution.py:44
  14.2 26.4 %collective-permute-start.2 = (bf16[192,1024]{1,0:T(8,128)(2,1)}, bf16[192,1024]{1,0:T(8,128)(2,1)S(1)}, u32[]{:S(2)}, u32[]{:S(2)}) collective-permute-start(bf16[192,1024]{1,0:T(8,128)(2,1)} %bitcast.267), channel_id=1, source_target_pairs={{32,0},{112,1},{34,2},{114,3},{36,4},{116,5},{38,6},{118,7},{40,8}... | collective-permute-start | bytes 1179656 | tf_op jit(solution)/shard_map/ppermute | solution.py:48
  16.6 12.5 %collective-permute-start.1 = (bf16[32,1024]{1,0:T(8,128)(2,1)S(1)}, bf16[32,1024]{1,0:T(8,128)(2,1)S(1)}, u32[]{:S(2)}, u32[]{:S(2)}) collective-permute-start(bf16[32,1024]{1,0:T(8,128)(2,1)S(1)} %pad_maximum_fusion.15), channel_id=1, source_target_pairs={{0,0},{1,16},{2,2},{3,18},{4,4},{5,20},{6,6},{7,22},{8,8},{9,24},{... | collective-permute-start | bytes 196616 | tf_op jit(solution)/shard_map/ppermute | solution.py:44
  35.0 11.0 %collective-permute-start.10 = (bf16[192,1024]{1,0:T(8,128)(2,1)S(1)}, bf16[192,1024]{1,0:T(8,128)(2,1)S(1)}, u32[]{:S(2)}, u32[]{:S(2)}) collective-permute-start(bf16[192,1024]{1,0:T(8,128)(2,1)S(1)} %bitcast.268), channel_id=1, source_target_pairs={{0,0},{1,16},{2,2},{3,18},{4,4},{5,20},{6,6},{7,22},{8,8},{9,24},{... | collective-permute-start | bytes 1179656 | tf_op jit(solution)/shard_map/ppermute | solution.py:44
  40.6 5.4 %collective-permute-start.9 = (bf16[1,64,896]{2,1,0:T(8,128)(2,1)S(1)}, bf16[1,64,896]{2,1,0:T(8,128)(2,1)S(1)}, u32[]{:S(2)}, u32[]{:S(2)}) collective-permute-start(bf16[1,64,896]{2,1,0:T(8,128)(2,1)S(1)} %maximum_bitcast_fusion.1), channel_id=1, source_target_pairs={{0,2},{1,9},{2,0},{3,11},{4,6},{5,13},{6,4},{7,15},{8,10},{9,1},{1... | collective-permute-start | bytes 344072 | tf_op jit(solution)/shard_map/ppermute | solution.py:36
  41.4 16.8 %collective-permute-start.3 = (bf16[384,1024]{1,0:T(8,128)(2,1)S(1)}, bf16[384,1024]{1,0:T(8,128)(2,1)S(1)}, u32[]{:S(2)}, u32[]{:S(2)}) collective-permute-start(bf16[384,1024]{1,0:T(8,128)(2,1)S(1)} %pad_maximum_fusion.6), channel_id=1, source_target_pairs={{0,96},{1,33},{2,98},{3,35},{4,100},{5,37},{6,102},{7,39},{8,104},... | collective-permute-start | bytes 2359304 | tf_op jit(solution)/shard_map/ppermute | solution.py:36
  46.1 6.5 %collective-permute-start.11 = (bf16[2,64,896]{2,1,0:T(8,128)(2,1)S(1)}, bf16[2,64,896]{2,1,0:T(8,128)(2,1)S(1)}, u32[]{:S(2)}, u32[]{:S(2)}) collective-permute-start(bf16[2,64,896]{2,1,0:T(8,128)(2,1)S(1)} %maximum_select_fusion.7), channel_id=1, source_target_pairs={{0,6},{1,25},{2,4},{3,27},{4,2},{5,29},{6,0},{7,31},{8,14},{9,17},... | collective-permute-start | bytes 688136 | tf_op jit(solution)/shard_map/ppermute | solution.py:36
  46.8 11.0 %collective-permute-start.13 = (bf16[192,1024]{1,0:T(8,128)(2,1)S(1)}, bf16[192,1024]{1,0:T(8,128)(2,1)S(1)}, u32[]{:S(2)}, u32[]{:S(2)}) collective-permute-start(bf16[192,1024]{1,0:T(8,128)(2,1)S(1)} %collective-permute-done.10), channel_id=1, source_target_pairs={{0,32},{1,97},{2,34},{3,99},{4,36},{5,101},{6,38},{7,103},{8,40},{... | collective-permute-start | bytes 1179656 | tf_op jit(solution)/shard_map/ppermute | solution.py:36
  52.6 7.6 %collective-permute-start.12 = (bf16[4,64,896]{2,1,0:T(8,128)(2,1)S(1)}, bf16[4,64,896]{2,1,0:T(8,128)(2,1)S(1)}, u32[]{:S(2)}, u32[]{:S(2)}) collective-permute-start(bf16[4,64,896]{2,1,0:T(8,128)(2,1)S(1)} %maximum_select_fusion.5), channel_id=1, source_target_pairs={{0,8},{1,3},{2,10},{3,1},{4,12},{5,7},{6,14},{7,5},{8,0},{9,11},{1... | collective-permute-start | bytes 1376264 | tf_op jit(solution)/shard_map/ppermute | solution.py:36
  57.8 11.2 %collective-permute-start.15 = (bf16[384,1024]{1,0:T(8,128)(2,1)S(1)}, bf16[384,1024]{1,0:T(8,128)(2,1)S(1)}, u32[]{:S(2)}, u32[]{:S(2)}) collective-permute-start(bf16[384,1024]{1,0:T(8,128)(2,1)S(1)} %constant_dynamic-update-slice_fusion.9), channel_id=1, source_target_pairs={{0,96},{1,33},{2,98},{3,35},{4,100},{5,37},{6,102},{7,39},{8,104},... | collective-permute-start | bytes 2359304 | tf_op jit(solution)/shard_map/ppermute | solution.py:36
  59.2 16.0 %collective-permute-start.4 = (bf16[768,1024]{1,0:T(8,128)(2,1)}, bf16[768,1024]{1,0:T(8,128)(2,1)}, u32[]{:S(2)}, u32[]{:S(2)}) collective-permute-start(bf16[768,1024]{1,0:T(8,128)(2,1)} %constant_dynamic-update-slice_fusion.own_ref), channel_id=1, source_target_pairs={{0,1},{1,0},{2,3},{3,2},{4,5},{5,4},{6,7},{7,6},{8,9},{9,8},{10,11... | collective-permute-start | bytes 4718600 | tf_op jit(solution)/shard_map/ppermute | solution.py:36
  60.4 14.1 %collective-permute-start.14 = (bf16[8,64,896]{2,1,0:T(8,128)(2,1)S(1)}, bf16[8,64,896]{2,1,0:T(8,128)(2,1)S(1)}, u32[]{:S(2)}, u32[]{:S(2)}) collective-permute-start(bf16[8,64,896]{2,1,0:T(8,128)(2,1)S(1)} %maximum_select_fusion.3), channel_id=1, source_target_pairs={{0,24},{1,7},{2,26},{3,5},{4,28},{5,3},{6,30},{7,1},{8,16},{9,15},... | collective-permute-start | bytes 2752520 | tf_op jit(solution)/shard_map/ppermute | solution.py:36
  101.3 11.2 %collective-permute-start.17 = (bf16[384,1024]{1,0:T(8,128)(2,1)S(1)}, bf16[384,1024]{1,0:T(8,128)(2,1)S(1)}, u32[]{:S(2)}, u32[]{:S(2)}) collective-permute-start(bf16[384,1024]{1,0:T(8,128)(2,1)S(1)} %slice.296), channel_id=1, source_target_pairs={{0,96},{1,33},{2,98},{3,35},{4,100},{5,37},{6,102},{7,39},{8,104},... | collective-permute-start | bytes 2359304 | tf_op jit(solution)/shard_map/ppermute | solution.py:36
  102.3 4.8 %collective-permute-start.19 = (bf16[1,64,1152]{2,1,0:T(8,128)(2,1)S(1)}, bf16[1,64,1152]{2,1,0:T(8,128)(2,1)S(1)}, u32[]{:S(2)}, u32[]{:S(2)}) collective-permute-start(bf16[1,64,1152]{2,1,0:T(8,128)(2,1)S(1)} %maximum_bitcast_fusion), channel_id=1, source_target_pairs={{0,2},{1,9},{2,0},{3,11},{4,6},{5,13},{6,4},{7,15},{8,10},{9,1},{1... | collective-permute-start | bytes 442376 | tf_op jit(solution)/shard_map/ppermute | solution.py:36
  107.1 7.3 %collective-permute-start.20 = (bf16[2,64,1152]{2,1,0:T(8,128)(2,1)S(1)}, bf16[2,64,1152]{2,1,0:T(8,128)(2,1)S(1)}, u32[]{:S(2)}, u32[]{:S(2)}) collective-permute-start(bf16[2,64,1152]{2,1,0:T(8,128)(2,1)S(1)} %maximum_select_fusion.6), channel_id=1, source_target_pairs={{0,6},{1,25},{2,4},{3,27},{4,2},{5,29},{6,0},{7,31},{8,14},{9,17},... | collective-permute-start | bytes 884744 | tf_op jit(solution)/shard_map/ppermute | solution.py:36
  112.8 7.9 %collective-permute-start.18 = (bf16[192,1024]{1,0:T(8,128)(2,1)S(1)}, bf16[192,1024]{1,0:T(8,128)(2,1)S(1)}, u32[]{:S(2)}, u32[]{:S(2)}) collective-permute-start(bf16[192,1024]{1,0:T(8,128)(2,1)S(1)} %slice.299), channel_id=1, source_target_pairs={{0,32},{1,97},{2,34},{3,99},{4,36},{5,101},{6,38},{7,103},{8,40},{... | collective-permute-start | bytes 1179656 | tf_op jit(solution)/shard_map/ppermute | solution.py:36
  114.6 9.1 %collective-permute-start.21 = (bf16[4,64,1152]{2,1,0:T(8,128)(2,1)S(1)}, bf16[4,64,1152]{2,1,0:T(8,128)(2,1)S(1)}, u32[]{:S(2)}, u32[]{:S(2)}) collective-permute-start(bf16[4,64,1152]{2,1,0:T(8,128)(2,1)S(1)} %maximum_select_fusion.4), channel_id=1, source_target_pairs={{0,8},{1,3},{2,10},{3,1},{4,12},{5,7},{6,14},{7,5},{8,0},{9,11},{1... | collective-permute-start | bytes 1769480 | tf_op jit(solution)/shard_map/ppermute | solution.py:36
  121.2 7.9 %collective-permute-start.23 = (bf16[192,1024]{1,0:T(8,128)(2,1)S(1)}, bf16[192,1024]{1,0:T(8,128)(2,1)S(1)}, u32[]{:S(2)}, u32[]{:S(2)}) collective-permute-start(bf16[192,1024]{1,0:T(8,128)(2,1)S(1)} %multiply_convert_fusion.6), channel_id=1, source_target_pairs={{0,32},{1,97},{2,34},{3,99},{4,36},{5,101},{6,38},{7,103},{8,40},{... | collective-permute-start | bytes 1179656 | tf_op jit(solution)/shard_map/ppermute | solution.py:36
  123.9 21.2 %collective-permute-start.22 = (bf16[8,64,1152]{2,1,0:T(8,128)(2,1)S(1)}, bf16[8,64,1152]{2,1,0:T(8,128)(2,1)S(1)}, u32[]{:S(2)}, u32[]{:S(2)}) collective-permute-start(bf16[8,64,1152]{2,1,0:T(8,128)(2,1)S(1)} %maximum_select_fusion.2), channel_id=1, source_target_pairs={{0,24},{1,7},{2,26},{3,5},{4,28},{5,3},{6,30},{7,1},{8,16},{9,15},... | collective-permute-start | bytes 3538952 | tf_op jit(solution)/shard_map/ppermute | solution.py:36
  129.2 11.2 %collective-permute-start.24 = (bf16[384,1024]{1,0:T(8,128)(2,1)S(1)}, bf16[384,1024]{1,0:T(8,128)(2,1)S(1)}, u32[]{:S(2)}, u32[]{:S(2)}) collective-permute-start(bf16[384,1024]{1,0:T(8,128)(2,1)S(1)} %pad_maximum_fusion.9), channel_id=1, source_target_pairs={{0,96},{1,33},{2,98},{3,35},{4,100},{5,37},{6,102},{7,39},{8,104},... | collective-permute-start | bytes 2359304 | tf_op jit(solution)/shard_map/ppermute | solution.py:36
  140.5 7.5 %collective-permute-start.26 = (bf16[768,1024]{1,0:T(8,128)(2,1)S(1)}, bf16[768,1024]{1,0:T(8,128)(2,1)S(1)}, u32[]{:S(2)}, u32[]{:S(2)}) collective-permute-start(bf16[768,1024]{1,0:T(8,128)(2,1)S(1)} %pad_maximum_fusion.2), channel_id=1, source_target_pairs={{0,1},{1,0},{2,3},{3,2},{4,5},{5,4},{6,7},{7,6},{8,9},{9,8},{10,11... | collective-permute-start | bytes 4718600 | tf_op jit(solution)/shard_map/ppermute | solution.py:36
  145.0 5.3 %collective-permute-start.25 = (bf16[768,1024]{1,0:T(8,128)(2,1)S(1)}, bf16[768,1024]{1,0:T(8,128)(2,1)S(1)}, u32[]{:S(2)}, u32[]{:S(2)}) collective-permute-start(bf16[768,1024]{1,0:T(8,128)(2,1)S(1)} %copy-done.14), channel_id=1, source_target_pairs={{0,1},{1,0},{2,3},{3,2},{4,5},{5,4},{6,7},{7,6},{8,9},{9,8},{10,11... | collective-permute-start | bytes 4718600 | tf_op jit(solution)/shard_map/ppermute | solution.py:36
  154.3 6.2 %collective-permute-start.27 = (bf16[768,1024]{1,0:T(8,128)(2,1)}, bf16[768,1024]{1,0:T(8,128)(2,1)}, u32[]{:S(2)}, u32[]{:S(2)}) collective-permute-start(bf16[768,1024]{1,0:T(8,128)(2,1)} %convolution_convert_fusion), channel_id=1, source_target_pairs={{0,1},{1,0},{2,3},{3,2},{4,5},{5,4},{6,7},{7,6},{8,9},{9,8},{10,11... | collective-permute-start | bytes 4718600 | tf_op jit(solution)/shard_map/ppermute | solution.py:36
  164.8 11.4 %collective-permute-start.28 = (bf16[384,1024]{1,0:T(8,128)(2,1)S(1)}, bf16[384,1024]{1,0:T(8,128)(2,1)S(1)}, u32[]{:S(2)}, u32[]{:S(2)}) collective-permute-start(bf16[384,1024]{1,0:T(8,128)(2,1)S(1)} %slice.295), channel_id=1, source_target_pairs={{0,96},{1,33},{2,98},{3,35},{4,100},{5,37},{6,102},{7,39},{8,104},... | collective-permute-start | bytes 2359304 | tf_op jit(solution)/shard_map/ppermute | solution.py:36
  176.5 7.9 %collective-permute-start.29 = (bf16[192,1024]{1,0:T(8,128)(2,1)S(1)}, bf16[192,1024]{1,0:T(8,128)(2,1)S(1)}, u32[]{:S(2)}, u32[]{:S(2)}) collective-permute-start(bf16[192,1024]{1,0:T(8,128)(2,1)S(1)} %slice.298), channel_id=1, source_target_pairs={{0,32},{1,97},{2,34},{3,99},{4,36},{5,101},{6,38},{7,103},{8,40},{... | collective-permute-start | bytes 1179656 | tf_op jit(solution)/shard_map/ppermute | solution.py:36
  186.1 8.2 %collective-permute-start.30 = (bf16[192,1024]{1,0:T(8,128)(2,1)S(1)}, bf16[192,1024]{1,0:T(8,128)(2,1)S(1)}, u32[]{:S(2)}, u32[]{:S(2)}) collective-permute-start(bf16[192,1024]{1,0:T(8,128)(2,1)S(1)} %get-tuple-element.103), channel_id=1, source_target_pairs={{0,32},{1,97},{2,34},{3,99},{4,36},{5,101},{6,38},{7,103},{8,40},{... | collective-permute-start | bytes 1179656 | tf_op jit(solution)/shard_map/ppermute | solution.py:36
  188.8 16.9 %collective-permute-start.32 = (bf16[8,64,1152]{2,1,0:T(8,128)(2,1)}, bf16[8,64,1152]{2,1,0:T(8,128)(2,1)}, u32[]{:S(2)}, u32[]{:S(2)}) collective-permute-start(bf16[8,64,1152]{2,1,0:T(8,128)(2,1)} %constant_dynamic-slice_fusion.6), channel_id=1, source_target_pairs={{0,24},{1,7},{2,26},{3,5},{4,28},{5,3},{6,30},{7,1},{8,16},{9,15},... | collective-permute-start | bytes 3538952 | tf_op jit(solution)/shard_map/ppermute | solution.py:36
  195.2 11.5 %collective-permute-start.31 = (bf16[384,1024]{1,0:T(8,128)(2,1)}, bf16[384,1024]{1,0:T(8,128)(2,1)}, u32[]{:S(2)}, u32[]{:S(2)}) collective-permute-start(bf16[384,1024]{1,0:T(8,128)(2,1)} %pad_maximum_fusion.10), channel_id=1, source_target_pairs={{0,96},{1,33},{2,98},{3,35},{4,100},{5,37},{6,102},{7,39},{8,104},... | collective-permute-start | bytes 2359304 | tf_op jit(solution)/shard_map/ppermute | solution.py:36
  207.9 7.7 %collective-permute-start.33 = (bf16[768,1024]{1,0:T(8,128)(2,1)S(1)}, bf16[768,1024]{1,0:T(8,128)(2,1)S(1)}, u32[]{:S(2)}, u32[]{:S(2)}) collective-permute-start(bf16[768,1024]{1,0:T(8,128)(2,1)S(1)} %constant_dynamic-update-slice_fusion.11.own_ref), channel_id=1, source_target_pairs={{0,1},{1,0},{2,3},{3,2},{4,5},{5,4},{6,7},{7,6},{8,9},{9,8},{10,11... | collective-permute-start | bytes 4718600 | tf_op jit(solution)/shard_map/ppermute | solution.py:36
  214.6 24.0 %collective-permute-start.34 = (bf16[4,64,1152]{2,1,0:T(8,128)(2,1)}, bf16[4,64,1152]{2,1,0:T(8,128)(2,1)}, u32[]{:S(2)}, u32[]{:S(2)}) collective-permute-start(bf16[4,64,1152]{2,1,0:T(8,128)(2,1)} %constant_dynamic-slice_fusion.5), channel_id=1, source_target_pairs={{0,8},{1,3},{2,10},{3,1},{4,12},{5,7},{6,14},{7,5},{8,0},{9,11},{1... | collective-permute-start | bytes 1769480 | tf_op jit(solution)/shard_map/ppermute | solution.py:36
  225.4 13.3 %collective-permute-start.35 = (bf16[8,64,256]{2,1,0:T(8,128)(2,1)S(1)}, bf16[8,64,256]{2,1,0:T(8,128)(2,1)S(1)}, u32[]{:S(2)}, u32[]{:S(2)}) collective-permute-start(bf16[8,64,256]{2,1,0:T(8,128)(2,1)S(1)} %constant_dynamic-slice_fusion.4), channel_id=1, source_target_pairs={{0,24},{1,7},{2,26},{3,5},{4,28},{5,3},{6,30},{7,1},{8,16},{9,15},... | collective-permute-start | bytes 786440 | tf_op jit(solution)/shard_map/ppermute | solution.py:36
  240.0 10.0 %collective-permute-start.36 = (bf16[64,1152]{1,0:T(8,128)(2,1)S(1)}, bf16[64,1152]{1,0:T(8,128)(2,1)S(1)}, u32[]{:S(2)}, u32[]{:S(2)}) collective-permute-start(bf16[64,1152]{1,0:T(8,128)(2,1)S(1)} %get-tuple-element.170), channel_id=1, source_target_pairs={{0,2},{1,9},{2,0},{3,11},{4,6},{5,13},{6,4},{7,15},{8,10},{9,1},{1... | collective-permute-start | bytes 442376 | tf_op jit(solution)/shard_map/ppermute | solution.py:36
  240.1 9.9 %collective-permute-start.37 = (bf16[64,1152]{1,0:T(8,128)(2,1)S(1)}, bf16[64,1152]{1,0:T(8,128)(2,1)S(1)}, u32[]{:S(2)}, u32[]{:S(2)}) collective-permute-start(bf16[64,1152]{1,0:T(8,128)(2,1)S(1)} %get-tuple-element.169), channel_id=1, source_target_pairs={{0,4},{1,17},{2,6},{3,19},{4,0},{5,21},{6,2},{7,23},{8,12},{9,25},... | collective-permute-start | bytes 442376 | tf_op jit(solution)/shard_map/ppermute | solution.py:36
  244.2 6.0 %collective-permute-start.38 = (bf16[64,1152]{1,0:T(8,128)(2,1)S(1)}, bf16[64,1152]{1,0:T(8,128)(2,1)S(1)}, u32[]{:S(2)}, u32[]{:S(2)}) collective-permute-start(bf16[64,1152]{1,0:T(8,128)(2,1)S(1)} %get-tuple-element.168), channel_id=1, source_target_pairs={{0,6},{1,25},{2,4},{3,27},{4,2},{5,29},{6,0},{7,31},{8,14},{9,17},... | collective-permute-start | bytes 442376 | tf_op jit(solution)/shard_map/ppermute | solution.py:36
  259.0 7.0 %collective-permute-start.39 = (bf16[768,1024]{1,0:T(8,128)(2,1)}, bf16[768,1024]{1,0:T(8,128)(2,1)S(1)}, u32[]{:S(2)}, u32[]{:S(2)}) collective-permute-start(bf16[768,1024]{1,0:T(8,128)(2,1)} %get-tuple-element.129), channel_id=1, source_target_pairs={{0,1},{1,0},{2,3},{3,2},{4,5},{5,4},{6,7},{7,6},{8,9},{9,8},{10,11... | collective-permute-start | bytes 4718600 | tf_op jit(solution)/shard_map/ppermute | solution.py:36
  266.8 13.0 %collective-permute-start.41 = (bf16[384,1024]{1,0:T(8,128)(2,1)S(1)}, bf16[384,1024]{1,0:T(8,128)(2,1)S(1)}, u32[]{:S(2)}, u32[]{:S(2)}) collective-permute-start(bf16[384,1024]{1,0:T(8,128)(2,1)S(1)} %slice.294), channel_id=1, source_target_pairs={{0,96},{1,33},{2,98},{3,35},{4,100},{5,37},{6,102},{7,39},{8,104},... | collective-permute-start | bytes 2359304 | tf_op jit(solution)/shard_map/ppermute | solution.py:36
  268.0 11.7 %collective-permute-start.42 = (bf16[8,64,640]{2,1,0:T(8,128)(2,1)S(1)}, bf16[8,64,640]{2,1,0:T(8,128)(2,1)S(1)}, u32[]{:S(2)}, u32[]{:S(2)}) collective-permute-start(bf16[8,64,640]{2,1,0:T(8,128)(2,1)S(1)} %constant_dynamic-slice_fusion.2), channel_id=1, source_target_pairs={{0,24},{1,7},{2,26},{3,5},{4,28},{5,3},{6,30},{7,1},{8,16},{9,15},... | collective-permute-start | bytes 1966088 | tf_op jit(solution)/shard_map/ppermute | solution.py:36
  270.4 4.9 %collective-permute-start.43 = (bf16[64,256]{1,0:T(8,128)(2,1)S(1)}, bf16[64,256]{1,0:T(8,128)(2,1)S(1)}, u32[]{:S(2)}, u32[]{:S(2)}) collective-permute-start(bf16[64,256]{1,0:T(8,128)(2,1)S(1)} %get-tuple-element.193), channel_id=1, source_target_pairs={{0,2},{1,9},{2,0},{3,11},{4,6},{5,13},{6,4},{7,15},{8,10},{9,1},{1... | collective-permute-start | bytes 98312 | tf_op jit(solution)/shard_map/ppermute | solution.py:36
  271.4 5.2 %collective-permute-start.45 = (bf16[64,256]{1,0:T(8,128)(2,1)S(1)}, bf16[64,256]{1,0:T(8,128)(2,1)S(1)}, u32[]{:S(2)}, u32[]{:S(2)}) collective-permute-start(bf16[64,256]{1,0:T(8,128)(2,1)S(1)} %get-tuple-element.191), channel_id=1, source_target_pairs={{0,6},{1,25},{2,4},{3,27},{4,2},{5,29},{6,0},{7,31},{8,14},{9,17},... | collective-permute-start | bytes 98312 | tf_op jit(solution)/shard_map/ppermute | solution.py:36
  280.0 8.2 %collective-permute-start.46 = (bf16[192,1024]{1,0:T(8,128)(2,1)S(1)}, bf16[192,1024]{1,0:T(8,128)(2,1)S(1)}, u32[]{:S(2)}, u32[]{:S(2)}) collective-permute-start(bf16[192,1024]{1,0:T(8,128)(2,1)S(1)} %slice.297), channel_id=1, source_target_pairs={{0,32},{1,97},{2,34},{3,99},{4,36},{5,101},{6,38},{7,103},{8,40},{... | collective-permute-start | bytes 1179656 | tf_op jit(solution)/shard_map/ppermute | solution.py:36
  281.9 6.3 %collective-permute-start.47 = (bf16[4,64,640]{2,1,0:T(8,128)(2,1)S(1)}, bf16[4,64,640]{2,1,0:T(8,128)(2,1)S(1)}, u32[]{:S(2)}, u32[]{:S(2)}) collective-permute-start(bf16[4,64,640]{2,1,0:T(8,128)(2,1)S(1)} %constant_dynamic-slice_fusion.1), channel_id=1, source_target_pairs={{0,8},{1,3},{2,10},{3,1},{4,12},{5,7},{6,14},{7,5},{8,0},{9,11},{1... | collective-permute-start | bytes 983048 | tf_op jit(solution)/shard_map/ppermute | solution.py:36
  288.8 12.4 %collective-permute-start.48 = (bf16[192,1024]{1,0:T(8,128)(2,1)S(1)}, bf16[192,1024]{1,0:T(8,128)(2,1)S(1)}, u32[]{:S(2)}, u32[]{:S(2)}) collective-permute-start(bf16[192,1024]{1,0:T(8,128)(2,1)S(1)} %get-tuple-element.154), channel_id=1, source_target_pairs={{0,0},{1,16},{2,2},{3,18},{4,4},{5,20},{6,6},{7,22},{8,8},{9,24},{... | collective-permute-start | bytes 1179656 | tf_op jit(solution)/shard_map/ppermute | solution.py:44
  293.4 7.4 %collective-permute-start.49 = (bf16[64,640]{1,0:T(8,128)(2,1)S(1)}, bf16[64,640]{1,0:T(8,128)(2,1)S(1)}, u32[]{:S(2)}, u32[]{:S(2)}) collective-permute-start(bf16[64,640]{1,0:T(8,128)(2,1)S(1)} %get-tuple-element.174), channel_id=1, source_target_pairs={{0,2},{1,9},{2,0},{3,11},{4,6},{5,13},{6,4},{7,15},{8,10},{9,1},{1... | collective-permute-start | bytes 245768 | tf_op jit(solution)/shard_map/ppermute | solution.py:36
  295.0 5.8 %collective-permute-start.50 = (bf16[64,640]{1,0:T(8,128)(2,1)S(1)}, bf16[64,640]{1,0:T(8,128)(2,1)S(1)}, u32[]{:S(2)}, u32[]{:S(2)}) collective-permute-start(bf16[64,640]{1,0:T(8,128)(2,1)S(1)} %get-tuple-element.173), channel_id=1, source_target_pairs={{0,4},{1,17},{2,6},{3,19},{4,0},{5,21},{6,2},{7,23},{8,12},{9,25},... | collective-permute-start | bytes 245768 | tf_op jit(solution)/shard_map/ppermute | solution.py:36
  295.0 6.2 %collective-permute-start.51 = (bf16[64,640]{1,0:T(8,128)(2,1)S(1)}, bf16[64,640]{1,0:T(8,128)(2,1)S(1)}, u32[]{:S(2)}, u32[]{:S(2)}) collective-permute-start(bf16[64,640]{1,0:T(8,128)(2,1)S(1)} %get-tuple-element.172), channel_id=1, source_target_pairs={{0,6},{1,25},{2,4},{3,27},{4,2},{5,29},{6,0},{7,31},{8,14},{9,17},... | collective-permute-start | bytes 245768 | tf_op jit(solution)/shard_map/ppermute | solution.py:36
  301.3 4.7 %collective-permute-start.53 = (bf16[4,1,8,1408]{3,2,1,0:T(8,128)(2,1)S(1)}, bf16[4,1,8,1408]{3,2,1,0:T(8,128)(2,1)S(1)}, u32[]{:S(2)}, u32[]{:S(2)}) collective-permute-start(bf16[4,1,8,1408]{3,2,1,0:T(8,128)(2,1)S(1)} %constant_dynamic-slice_fusion), channel_id=1, source_target_pairs={{0,1},{1,0},{2,3},{3,2},{4,5},{5,4},{6,7},{7,6},{8,9},{9,8},{10,11... | collective-permute-start | bytes 270344 | tf_op jit(solution)/shard_map/ppermute | solution.py:36
  301.4 14.9 %collective-permute-start.52 = (bf16[208,1024]{1,0:T(8,128)(2,1)S(1)}, bf16[208,1024]{1,0:T(8,128)(2,1)S(1)}, u32[]{:S(2)}, u32[]{:S(2)}) collective-permute-start(bf16[208,1024]{1,0:T(8,128)(2,1)S(1)} %pad_maximum_fusion.11), channel_id=1, source_target_pairs={{0,0},{1,16},{2,2},{3,18},{4,4},{5,20},{6,6},{7,22},{8,8},{9,24},{... | collective-permute-start | bytes 1277960 | tf_op jit(solution)/shard_map/ppermute | solution.py:44
  (61 other events, 514.6 us)
Sparse Core Ops, SparseCore 0:
  208.0 36.0 reduce-scatter.1

commit v3 on v2

--- a/solution.py
+++ b/solution.py
@@ -255,11 +255,14 @@
 
     @pl.when(step == pl.num_programs(0) - 1)
     def _():
-        for block in range(16):
-            row = (block % 8 * 2 + block // 8) * 16
-            for n in range(4):
-                piece = total_ref[row : row + 16, n * 256 : n * 256 + 256]
-                d_w_ref[block, n * 16 : n * 16 + 16, :] = low(piece)
+        for z in range(4):
+            for y in range(4):
+                spot = jnp.where(spots[9] == 1, y * 4 + z, z * 4 + y)
+                spot = jnp.where(spots[10] == 1, (spot + 8) % 16, spot)
+                row = (z % 2 * 8 + y * 2 + z // 2) * 16
+                for n in range(4):
+                    piece = total_ref[row : row + 16, n * 256 : n * 256 + 256]
+                    d_w_ref[spot, n * 16 : n * 16 + 16, :] = low(piece)
 
 
 def out_back(spots, own, other, attended, weights):
@@ -589,6 +592,7 @@
     chips = x ^ jnp.arange(4, dtype=jnp.int32)
     spots = jnp.concatenate(
         [spot_of(core)[chips], spot_of(1 - core)[chips], core[None], core[None]]
+        + [plane_bit(index, PLANE_STEPS[3])[None]]
     ).astype(jnp.int32)
 
     local = jnp.concatenate(
@@ -699,19 +703,14 @@
     result = lax.psum_scatter(after(result, d_branch_own), RING, scatter_dimension=0, tiled=True)
 
     d_attended, grad_out = out_back(spots, d_branch_own, d_branch_other, attended_kept, w_rows)
-    grad_out = plane_blocks(core, grad_out)
     d_attended, grad_out = lax.optimization_barrier((d_attended, grad_out))
     sums_keep, sums_got = plane_halves(index, sums, 2)
-    out_keep, out_got = plane_halves(index, grad_out, 3)
+    out_got = swap(grad_out[8:], *PLANE_STEPS[3])
     d_query, d_key, d_value = attend_back(ends, qkv_kept, d_attended, attended_kept, inverse_total)
     d_query, sums_got, out_got = lax.optimization_barrier((d_query, sums_got, out_got))
-    sums_keep, sums_got = plane_rest(index, low(wide(sums_keep) + wide(sums_got)))
-    sums_out = low(wide(out_keep) + wide(out_got))
     d_pre, d_gain_heads = project_back(
         spots, pre, d_query, d_key, d_value, cosine, sine, gain_query, gain_key
     )
-    d_pre, sums_got = lax.optimization_barrier((d_pre, sums_got))
-    sums = wide(sums_keep) + sum(wide(got) for got in sums_got)
     grad_heads = contract_rows(normed, d_pre)
     d_gain_attn = jnp.sum(grad_heads * wide(w_heads), axis=1) / gain_attn[0]
     d_gains = jnp.concatenate([d_gain_attn, d_gain_mlp, d_gain_heads.reshape(-1)])
@@ -724,26 +723,29 @@
         axis=2,
     )
     payload = plane_blocks(core, payload)
-    d_pre, payload, result = lax.optimization_barrier((d_pre, payload, result))
+    d_pre, payload = lax.optimization_barrier((d_pre, payload))
     d_normed_own, d_normed_other = normed_back(spots, d_pre, w_heads_across)
-    out_keep, out_got = plane_halves(index, sums_out, 2)
-    got, out_got = lax.optimization_barrier((swap(d_normed_other, CORE), out_got))
-    sums_out = low(wide(out_keep) + wide(out_got))
+    got = swap(d_normed_other, CORE)
     total = wide(d_normed_own) + wide(got)
     keep, send = total[: 2 * TOK], low(total[2 * TOK :])
-    payload, sums_out = (after(array, send) for array in (payload, sums_out))
+    payload, sums_got, out_got = (after(array, send) for array in (payload, sums_got, out_got))
+    sums_keep, sums_got = plane_rest(index, low(wide(sums_keep) + wide(sums_got)))
+    sums_out = low(wide(grad_out[:8]) + wide(out_got))
     heads_keep, heads_got = plane_halves(index, payload, 3)
-    out_keep, out_got = plane_rest(index, sums_out)
-    got, heads_got, out_got = lax.optimization_barrier(
-        (swap(send, *RING_STEPS[1]), heads_got, out_got)
-    )
-    sum_out = wide(out_keep) + sum(wide(part) for part in out_got)
+    out_keep, out_got = plane_halves(index, sums_out, 2)
+    got, heads_got, out_got, sums_got, result = lax.optimization_barrier(
+        (swap(send, *RING_STEPS[1]), heads_got, out_got, sums_got, result)
+    )
+    sums = wide(sums_keep) + sum(wide(part) for part in sums_got)
+    sums_out = low(wide(out_keep) + wide(out_got))
     heads_sums = low(wide(heads_keep) + wide(heads_got))
     total = keep + wide(got)
     heads_keep, heads_got = plane_halves(index, heads_sums, 2)
-    got, heads_got = lax.optimization_barrier(
-        (swap(low(total[TOK:]), *RING_STEPS[0]), heads_got)
-    )
+    out_keep, out_got = plane_rest(index, sums_out)
+    got, heads_got, out_got = lax.optimization_barrier(
+        (swap(low(total[TOK:]), *RING_STEPS[0]), heads_got, out_got)
+    )
+    sum_out = wide(out_keep) + sum(wide(part) for part in out_got)
     heads_sums = low(wide(heads_keep) + wide(heads_got))
     d_normed = total[:TOK] + wide(got)
     input_grad = d_middle + norm_back(wide(inputs), gain_attn, d_normed)

time: 331 us -> 329 us (level)
    unnamed x113 -> x108, local copies, waits for them, and re-layouts: 11 us -> 11.1 us
  transfers between devices with their start and end apart: 58 -> 58, of which waited for: 32 -> 34; matrix products, arithmetic and copies ran while one was open for 16% -> 15% of each run, Pallas kernels for 8% -> 10%
where the time goes in v3:
time: 329 us; the launch traced here: 323 us
  starting transfers between devices  91.6 us (28%)
  waiting for transfers between devices  89.9 us (27%)
  Pallas kernels  52.1 us (16%)
  local copies, waits for them, and re-layouts  26.8 us (8%)
  other arithmetic  25.2 us (8%)
  matrix products  19.7 us (6%)
  between operations  17.5 us (5%)
    ppermute x51, waiting for transfers between devices, swap(): lax.ppermute(values, AXES, [(k, k ^ masks[k & 1]) for k in range(DEVICES)])  89.8 us
    ppermute x51, starting transfers between devices, swap(): lax.ppermute(values, AXES, [(k, k ^ masks[k & 1]) for k in range(DEVICES)])  63 us
    pallas_call x6, Pallas kernels, ring_call(): pl.pallas_call(kernel, grid_spec=pltpu.PrefetchScalarGridSpec(num_scalar_...  34.3 us
    ppermute x5, starting transfers between devices, cross(): return lax.ppermute(values, AXES, [(k, crossed(k)) for k in range(DEVICES)])  27.6 us
    unnamed x108, local copies, waits for them, and re-layouts  11.1 us
    pallas_call x1, Pallas kernels, attend_back(): pl.pallas_call(attend_back_kernel, grid_spec=pltpu.PrefetchScalarGridSpec...  11 us
    dot_general x4, matrix products, contract_cols(): lax.dot_general(left, right, (((1,), (1,)), ((), ())), preferred_element_...  8.07 us
    pallas_call x1, Pallas kernels, attend(): pl.pallas_call(attend_kernel, grid_spec=pltpu.PrefetchScalarGridSpec(num_...  6.71 us
  transfers between devices with their start and end apart: 58, of which 34 were waited for; matrix products, arithmetic and copies ran while one was open for 15% of the time, Pallas kernels for 10%

profile of v3, /device:TPU:1, one launch (start us, length us, event | category | flops | bytes accessed | tf_op | source)
XLA Modules:
  0.0 322.7 jit_solution(4612105557861677675)
XLA Ops:
  7.3 6.9 %collective-permute-start = (bf16[192,1024]{1,0:T(8,128)(2,1)}, bf16[192,1024]{1,0:T(8,128)(2,1)S(1)}, u32[]{:S(2)}, u32[]{:S(2)}) collective-permute-start(bf16[192,1024]{1,0:T(8,128)(2,1)} %bitcast.262), channel_id=1, source_target_pairs={{0,0},{1,16},{2,2},{3,18},{4,4},{5,20},{6,6},{7,22},{8,8},{9,24},{... | collective-permute-start | bytes 1179656 | tf_op jit(solution)/shard_map/ppermute | solution.py:44
  16.6 6.4 %collective-permute-start.1 = (bf16[32,1024]{1,0:T(8,128)(2,1)S(1)}, bf16[32,1024]{1,0:T(8,128)(2,1)S(1)}, u32[]{:S(2)}, u32[]{:S(2)}) collective-permute-start(bf16[32,1024]{1,0:T(8,128)(2,1)S(1)} %pad_maximum_fusion.15), channel_id=1, source_target_pairs={{0,0},{1,16},{2,2},{3,18},{4,4},{5,20},{6,6},{7,22},{8,8},{9,24},{... | collective-permute-start | bytes 196616 | tf_op jit(solution)/shard_map/ppermute | solution.py:44
  35.1 3.5 %collective-permute-start.10 = (bf16[192,1024]{1,0:T(8,128)(2,1)S(1)}, bf16[192,1024]{1,0:T(8,128)(2,1)S(1)}, u32[]{:S(2)}, u32[]{:S(2)}) collective-permute-start(bf16[192,1024]{1,0:T(8,128)(2,1)S(1)} %bitcast.264), channel_id=1, source_target_pairs={{0,0},{1,16},{2,2},{3,18},{4,4},{5,20},{6,6},{7,22},{8,8},{9,24},{... | collective-permute-start | bytes 1179656 | tf_op jit(solution)/shard_map/ppermute | solution.py:44
  42.3 3.7 %collective-permute-done.9 = bf16[1,64,896]{2,1,0:T(8,128)(2,1)S(1)} collective-permute-done((bf16[1,64,896]{2,1,0:T(8,128)(2,1)S(1)}, bf16[1,64,896]{2,1,0:T(8,128)(2,1)S(1)}, u32[]{:S(2)}, u32[]{:S(2)}) %collective-permute-start.9) | collective-permute-done | bytes 114720 | tf_op jit(solution)/shard_map/ppermute | solution.py:36
  49.3 3.2 collective-permute-done.11
  54.8 3.0 collective-permute-done.13
  60.4 3.0 collective-permute-start.14
  63.4 2.8 fusion.11
  70.4 4.1 %collective-permute-done.14 = bf16[8,64,896]{2,1,0:T(8,128)(2,1)S(1)} collective-permute-done((bf16[8,64,896]{2,1,0:T(8,128)(2,1)S(1)}, bf16[8,64,896]{2,1,0:T(8,128)(2,1)S(1)}, u32[]{:S(2)}, u32[]{:S(2)}) %collective-permute-start.14) | collective-permute-done | bytes 917536 | tf_op jit(solution)/shard_map/ppermute | solution.py:36
  76.1 10.7 %project.1 = (bf16[1536,1024]{1,0:T(8,128)(2,1)}, f32[1536,384]{1,0:T(8,128)}, bf16[1536,512]{1,0:T(8,128)(2,1)S(1)}, bf16[1536,512]{1,0:T(8,128)(2,1)}, bf16[51...) custom-call(s32[11]{0:T(128)S(1)} %concatenate.161.spots, bf16[768,1024]{1,0:T(8,128)(2,1)} %constant_dynamic-update-slice_fusion.own_ref, ...), custom_call_target="tpu_custom_call" | custom-call | bytes 800000 | tf_op jit(solution)/shard_map/project/pallas_call | solution.py:138
  86.8 6.7 %attend.1 = (bf16[1536,256]{1,0:T(8,128)(2,1)S(1)}, bf16[1536,256]{1,0:T(8,128)(2,1)}, f32[2,1536]{1,0:T(2,128)}) custom-call(s32[2]{0:T(128)S(1)} %pad_add_fusion.ends_ref, bf16[1536,512]{1,0:T(8,128)(2,1)S(1)} %get-tuple-element.83.q_ref.k_ref.v_ref, bf16[1536,512]{1,0:T(8,128)(2,1)S(1)} %get-tuple-element.83.q_ref.k_ref.v_ref, ...), custom_call_target="tpu_custom_call" | custom-call | bytes 600000 | tf_op jit(solution)/shard_map/attend/pallas_call | solution.py:334
  93.5 2.9 to_ring.1
  97.5 3.0 collective-permute-done.16
  102.9 4.3 %collective-permute-done.19 = bf16[1,64,1152]{2,1,0:T(8,128)(2,1)S(1)} collective-permute-done((bf16[1,64,1152]{2,1,0:T(8,128)(2,1)S(1)}, bf16[1,64,1152]{2,1,0:T(8,128)(2,1)S(1)}, u32[]{:S(2)}, u32[]{:S(2)}) %collective-permute-start.19) | collective-permute-done | bytes 147488 | tf_op jit(solution)/shard_map/ppermute | solution.py:36
  107.2 2.9 collective-permute-start.20
  110.1 2.5 collective-permute-done.17
  115.3 5.5 %collective-permute-done.18 = bf16[192,1024]{1,0:T(8,128)(2,1)S(1)} collective-permute-done((bf16[192,1024]{1,0:T(8,128)(2,1)S(1)}, bf16[192,1024]{1,0:T(8,128)(2,1)S(1)}, u32[]{:S(2)}, u32[]{:S(2)}) %collective-permute-start.18) | collective-permute-done | bytes 393248 | tf_op jit(solution)/shard_map/ppermute | solution.py:36
  124.0 2.8 collective-permute-start.22
  126.8 2.4 collective-permute-done.23
  129.3 11.1 %collective-permute-done.24 = bf16[384,1024]{1,0:T(8,128)(2,1)S(1)} collective-permute-done((bf16[384,1024]{1,0:T(8,128)(2,1)S(1)}, bf16[384,1024]{1,0:T(8,128)(2,1)S(1)}, u32[]{:S(2)}, u32[]{:S(2)}) %collective-permute-start.24) | collective-permute-done | bytes 786464 | tf_op jit(solution)/shard_map/ppermute | solution.py:36
  140.6 4.5 %collective-permute-start.26 = (bf16[768,1024]{1,0:T(8,128)(2,1)S(1)}, bf16[768,1024]{1,0:T(8,128)(2,1)S(1)}, u32[]{:S(2)}, u32[]{:S(2)}) collective-permute-start(bf16[768,1024]{1,0:T(8,128)(2,1)S(1)} %pad_maximum_fusion.2), channel_id=1, source_target_pairs={{0,1},{1,0},{2,3},{3,2},{4,5},{5,4},{6,7},{7,6},{8,9},{9,8},{10,11... | collective-permute-start | bytes 4718600 | tf_op jit(solution)/shard_map/ppermute | solution.py:36
  151.7 2.6 convolution_convert_fusion
  154.7 3.2 fusion.47
  161.9 2.8 convert_add_fusion.1
  172.3 3.9 %collective-permute-done.28 = bf16[384,1024]{1,0:T(8,128)(2,1)S(1)} collective-permute-done((bf16[384,1024]{1,0:T(8,128)(2,1)S(1)}, bf16[384,1024]{1,0:T(8,128)(2,1)S(1)}, u32[]{:S(2)}, u32[]{:S(2)}) %collective-permute-start.28) | collective-permute-done | bytes 786464 | tf_op jit(solution)/shard_map/ppermute | solution.py:36
  178.9 5.6 %collective-permute-done.29 = bf16[192,1024]{1,0:T(8,128)(2,1)S(1)} collective-permute-done((bf16[192,1024]{1,0:T(8,128)(2,1)S(1)}, bf16[192,1024]{1,0:T(8,128)(2,1)S(1)}, u32[]{:S(2)}, u32[]{:S(2)}) %collective-permute-start.29) | collective-permute-done | bytes 393248 | tf_op jit(solution)/shard_map/ppermute | solution.py:36
  188.8 2.7 collective-permute-start.32
  191.6 2.8 collective-permute-done.30
  195.3 4.1 %to_pack.1 = bf16[1536,1024]{1,0:T(8,128)(2,1)} custom-call(s32[11]{0:T(128)S(1)} %concatenate.161.spots, bf16[768,384]{1,0:T(8,128)(2,1)S(1)} %get-tuple-element.101.own_ref, bf16[768,384]{1,0:T(8,128)(2,1)S(1)} %get-tuple-element.102.other_ref, bf16[384,1024]{1,0:T(8,128)(2,1)S(1)} %bitcast.207), custom_call_target="tpu_custom_call" | custom-call | bytes 400000 | tf_op jit(solution)/shard_map/to_pack/pallas_call | solution.py:138
  199.4 6.3 %collective-permute-done.32 = bf16[8,64,1152]{2,1,0:T(8,128)(2,1)} collective-permute-done((bf16[8,64,1152]{2,1,0:T(8,128)(2,1)}, bf16[8,64,1152]{2,1,0:T(8,128)(2,1)}, u32[]{:S(2)}, u32[]{:S(2)}) %collective-permute-start.32) | collective-permute-done | bytes 1179680 | tf_op jit(solution)/shard_map/ppermute | solution.py:36
  207.9 3.8 %collective-permute-start.33 = (bf16[768,1024]{1,0:T(8,128)(2,1)S(1)}, bf16[768,1024]{1,0:T(8,128)(2,1)S(1)}, u32[]{:S(2)}, u32[]{:S(2)}) collective-permute-start(bf16[768,1024]{1,0:T(8,128)(2,1)S(1)} %constant_dynamic-update-slice_fusion.11.own_ref), channel_id=1, source_target_pairs={{0,1},{1,0},{2,3},{3,2},{4,5},{5,4},{6,7},{7,6},{8,9},{9,8},{10,11... | collective-permute-start | bytes 4718600 | tf_op jit(solution)/shard_map/ppermute | solution.py:36
  211.8 1.9 add_convert_fusion.1
  214.8 5.8 %out_back.1 = (bf16[1536,256]{1,0:T(8,128)(2,1)S(1)}, bf16[16,64,256]{2,1,0:T(8,128)(2,1)}) custom-call(s32[11]{0:T(128)S(1)} %concatenate.161.spots, bf16[768,1024]{1,0:T(8,128)(2,1)S(1)} %constant_dynamic-update-slice_fusion.11.own_ref, bf16[768,1024]{1,0:T(8,128)(2,1)S(1)} %collective-permute-done.33.other_ref, ...), custom_call_target="tpu_custom_call" | custom-call | bytes 500000 | tf_op jit(solution)/shard_map/out_back/pallas_call | solution.py:138
  221.6 3.0 collective-permute-start.35
  224.6 11.0 %attend_back.1 = (f32[1536,256]{1,0:T(8,128)S(1)}, f32[1536,128]{1,0:T(8,128)S(1)}, f32[1536,128]{1,0:T(8,128)S(1)}) custom-call(s32[2]{0:T(128)S(1)} %pad_add_fusion.ends_ref, bf16[1536,512]{1,0:T(8,128)(2,1)} %get-tuple-element.88.q_ref.k_ref.v_ref, bf16[1536,512]{1,0:T(8,128)(2,1)} %get-tuple-element.88.q_ref.k_ref.v_ref, ...), custom_call_target="tpu_custom_call" | custom-call | bytes 1100000 | tf_op jit(solution)/shard_map/attend_back/pallas_call | solution.py:406
  235.7 5.8 %project_back.1 = (bf16[1536,512]{1,0:T(8,128)(2,1)S(1)}, f32[2,128]{1,0:T(2,128)S(1)}) custom-call(s32[11]{0:T(128)S(1)} %concatenate.161.spots, f32[1536,384]{1,0:T(8,128)} %get-tuple-element.87.pre_ref, f32[1536,256]{1,0:T(8,128)S(1)} %get-tuple-element.110.dq_ref, f32[1536,128]{1,0:T(8,128)S(1)} %get-tuple-element.111.dk_ref, ...), custom_call_target="tpu_custom_call" | custom-call | bytes 500000 | tf_op jit(solution)/shard_map/project_back/pallas_call | solution.py:138
  241.5 1.9 fusion.51
  245.2 5.1 %normed_back.1 = (bf16[768,1024]{1,0:T(8,128)(2,1)S(1)}, bf16[768,1024]{1,0:T(8,128)(2,1)}) custom-call(s32[11]{0:T(128)S(1)} %concatenate.161.spots, bf16[1536,512]{1,0:T(8,128)(2,1)S(1)} %get-tuple-element.117.d_pre_ref, bf16[512,1024]{1,0:T(8,128)(2,1)} %get-tuple-element.118.w_ref), custom_call_target="tpu_custom_call" | custom-call | bytes 400000 | tf_op jit(solution)/shard_map/normed_back/pallas_call | solution.py:138
  251.4 3.2 %collective-permute-done.36 = bf16[768,1024]{1,0:T(8,128)(2,1)S(1)} collective-permute-done((bf16[768,1024]{1,0:T(8,128)(2,1)}, bf16[768,1024]{1,0:T(8,128)(2,1)S(1)}, u32[]{:S(2)}, u32[]{:S(2)}) %collective-permute-start.36) | collective-permute-done | bytes 1572896 | tf_op jit(solution)/shard_map/ppermute | solution.py:36
  255.5 2.0 copy-done.15
  257.6 2.8 collective-permute-start.38
  262.4 2.8 collective-permute-done.39
  268.1 4.4 %collective-permute-done.42 = bf16[64,1152]{1,0:T(8,128)(2,1)S(1)} collective-permute-done((bf16[64,1152]{1,0:T(8,128)(2,1)S(1)}, bf16[64,1152]{1,0:T(8,128)(2,1)S(1)}, u32[]{:S(2)}, u32[]{:S(2)}) %collective-permute-start.42) | collective-permute-done | bytes 147488 | tf_op jit(solution)/shard_map/ppermute | solution.py:36
  277.6 3.0 collective-permute-start.46
  285.2 5.7 %collective-permute-start.48 = (bf16[192,1024]{1,0:T(8,128)(2,1)S(1)}, bf16[192,1024]{1,0:T(8,128)(2,1)S(1)}, u32[]{:S(2)}, u32[]{:S(2)}) collective-permute-start(bf16[192,1024]{1,0:T(8,128)(2,1)S(1)} %get-tuple-element.148), channel_id=1, source_target_pairs={{0,0},{1,16},{2,2},{3,18},{4,4},{5,20},{6,6},{7,22},{8,8},{9,24},{... | collective-permute-start | bytes 1179656 | tf_op jit(solution)/shard_map/ppermute | solution.py:44
  291.3 3.8 %collective-permute-start.51 = (bf16[64,640]{1,0:T(8,128)(2,1)S(1)}, bf16[64,640]{1,0:T(8,128)(2,1)S(1)}, u32[]{:S(2)}, u32[]{:S(2)}) collective-permute-start(bf16[64,640]{1,0:T(8,128)(2,1)S(1)} %get-tuple-element.166), channel_id=1, source_target_pairs={{0,6},{1,25},{2,4},{3,27},{4,2},{5,29},{6,0},{7,31},{8,14},{9,17},... | collective-permute-start | bytes 245768 | tf_op jit(solution)/shard_map/ppermute | solution.py:36
  298.4 5.0 %collective-permute-start.52 = (bf16[208,1024]{1,0:T(8,128)(2,1)S(1)}, bf16[208,1024]{1,0:T(8,128)(2,1)S(1)}, u32[]{:S(2)}, u32[]{:S(2)}) collective-permute-start(bf16[208,1024]{1,0:T(8,128)(2,1)S(1)} %pad_maximum_fusion.11), channel_id=1, source_target_pairs={{0,0},{1,16},{2,2},{3,18},{4,4},{5,20},{6,6},{7,22},{8,8},{9,24},{... | collective-permute-start | bytes 1277960 | tf_op jit(solution)/shard_map/ppermute | solution.py:44
  305.2 1.8 collective-permute-start.55
  (347 shorter events, 102.5 us)
Async XLA Ops:
  7.2 265.3 %reduce-scatter.2.cloned.1.call-start = ((), (), s32[]{:S(2)}) async-start(), calls=%async_computation.1 | async-start | bytes 3538944 | tf_op jit(solution)/shard_map/reduce_scatter | solution.py:703
  7.3 33.3 %collective-permute-start = (bf16[192,1024]{1,0:T(8,128)(2,1)}, bf16[192,1024]{1,0:T(8,128)(2,1)S(1)}, u32[]{:S(2)}, u32[]{:S(2)}) collective-permute-start(bf16[192,1024]{1,0:T(8,128)(2,1)} %bitcast.262), channel_id=1, source_target_pairs={{0,0},{1,16},{2,2},{3,18},{4,4},{5,20},{6,6},{7,22},{8,8},{9,24},{... | collective-permute-start | bytes 1179656 | tf_op jit(solution)/shard_map/ppermute | solution.py:44
  14.2 26.4 %collective-permute-start.2 = (bf16[192,1024]{1,0:T(8,128)(2,1)}, bf16[192,1024]{1,0:T(8,128)(2,1)S(1)}, u32[]{:S(2)}, u32[]{:S(2)}) collective-permute-start(bf16[192,1024]{1,0:T(8,128)(2,1)} %bitcast.263), channel_id=1, source_target_pairs={{32,0},{112,1},{34,2},{114,3},{36,4},{116,5},{38,6},{118,7},{40,8}... | collective-permute-start | bytes 1179656 | tf_op jit(solution)/shard_map/ppermute | solution.py:48
  16.6 12.5 %collective-permute-start.1 = (bf16[32,1024]{1,0:T(8,128)(2,1)S(1)}, bf16[32,1024]{1,0:T(8,128)(2,1)S(1)}, u32[]{:S(2)}, u32[]{:S(2)}) collective-permute-start(bf16[32,1024]{1,0:T(8,128)(2,1)S(1)} %pad_maximum_fusion.15), channel_id=1, source_target_pairs={{0,0},{1,16},{2,2},{3,18},{4,4},{5,20},{6,6},{7,22},{8,8},{9,24},{... | collective-permute-start | bytes 196616 | tf_op jit(solution)/shard_map/ppermute | solution.py:44
  35.1 11.0 %collective-permute-start.10 = (bf16[192,1024]{1,0:T(8,128)(2,1)S(1)}, bf16[192,1024]{1,0:T(8,128)(2,1)S(1)}, u32[]{:S(2)}, u32[]{:S(2)}) collective-permute-start(bf16[192,1024]{1,0:T(8,128)(2,1)S(1)} %bitcast.264), channel_id=1, source_target_pairs={{0,0},{1,16},{2,2},{3,18},{4,4},{5,20},{6,6},{7,22},{8,8},{9,24},{... | collective-permute-start | bytes 1179656 | tf_op jit(solution)/shard_map/ppermute | solution.py:44
  40.6 5.4 %collective-permute-start.9 = (bf16[1,64,896]{2,1,0:T(8,128)(2,1)S(1)}, bf16[1,64,896]{2,1,0:T(8,128)(2,1)S(1)}, u32[]{:S(2)}, u32[]{:S(2)}) collective-permute-start(bf16[1,64,896]{2,1,0:T(8,128)(2,1)S(1)} %maximum_bitcast_fusion.1), channel_id=1, source_target_pairs={{0,2},{1,9},{2,0},{3,11},{4,6},{5,13},{6,4},{7,15},{8,10},{9,1},{1... | collective-permute-start | bytes 344072 | tf_op jit(solution)/shard_map/ppermute | solution.py:36
  41.4 16.8 %collective-permute-start.3 = (bf16[384,1024]{1,0:T(8,128)(2,1)S(1)}, bf16[384,1024]{1,0:T(8,128)(2,1)S(1)}, u32[]{:S(2)}, u32[]{:S(2)}) collective-permute-start(bf16[384,1024]{1,0:T(8,128)(2,1)S(1)} %pad_maximum_fusion.6), channel_id=1, source_target_pairs={{0,96},{1,33},{2,98},{3,35},{4,100},{5,37},{6,102},{7,39},{8,104},... | collective-permute-start | bytes 2359304 | tf_op jit(solution)/shard_map/ppermute | solution.py:36
  46.1 6.5 %collective-permute-start.11 = (bf16[2,64,896]{2,1,0:T(8,128)(2,1)S(1)}, bf16[2,64,896]{2,1,0:T(8,128)(2,1)S(1)}, u32[]{:S(2)}, u32[]{:S(2)}) collective-permute-start(bf16[2,64,896]{2,1,0:T(8,128)(2,1)S(1)} %maximum_select_fusion.7), channel_id=1, source_target_pairs={{0,6},{1,25},{2,4},{3,27},{4,2},{5,29},{6,0},{7,31},{8,14},{9,17},... | collective-permute-start | bytes 688136 | tf_op jit(solution)/shard_map/ppermute | solution.py:36
  46.8 11.0 %collective-permute-start.13 = (bf16[192,1024]{1,0:T(8,128)(2,1)S(1)}, bf16[192,1024]{1,0:T(8,128)(2,1)S(1)}, u32[]{:S(2)}, u32[]{:S(2)}) collective-permute-start(bf16[192,1024]{1,0:T(8,128)(2,1)S(1)} %collective-permute-done.10), channel_id=1, source_target_pairs={{0,32},{1,97},{2,34},{3,99},{4,36},{5,101},{6,38},{7,103},{8,40},{... | collective-permute-start | bytes 1179656 | tf_op jit(solution)/shard_map/ppermute | solution.py:36
  52.6 7.6 %collective-permute-start.12 = (bf16[4,64,896]{2,1,0:T(8,128)(2,1)S(1)}, bf16[4,64,896]{2,1,0:T(8,128)(2,1)S(1)}, u32[]{:S(2)}, u32[]{:S(2)}) collective-permute-start(bf16[4,64,896]{2,1,0:T(8,128)(2,1)S(1)} %maximum_select_fusion.5), channel_id=1, source_target_pairs={{0,8},{1,3},{2,10},{3,1},{4,12},{5,7},{6,14},{7,5},{8,0},{9,11},{1... | collective-permute-start | bytes 1376264 | tf_op jit(solution)/shard_map/ppermute | solution.py:36
  57.8 11.2 %collective-permute-start.15 = (bf16[384,1024]{1,0:T(8,128)(2,1)S(1)}, bf16[384,1024]{1,0:T(8,128)(2,1)S(1)}, u32[]{:S(2)}, u32[]{:S(2)}) collective-permute-start(bf16[384,1024]{1,0:T(8,128)(2,1)S(1)} %constant_dynamic-update-slice_fusion.9), channel_id=1, source_target_pairs={{0,96},{1,33},{2,98},{3,35},{4,100},{5,37},{6,102},{7,39},{8,104},... | collective-permute-start | bytes 2359304 | tf_op jit(solution)/shard_map/ppermute | solution.py:36
  59.2 16.0 %collective-permute-start.4 = (bf16[768,1024]{1,0:T(8,128)(2,1)}, bf16[768,1024]{1,0:T(8,128)(2,1)}, u32[]{:S(2)}, u32[]{:S(2)}) collective-permute-start(bf16[768,1024]{1,0:T(8,128)(2,1)} %constant_dynamic-update-slice_fusion.own_ref), channel_id=1, source_target_pairs={{0,1},{1,0},{2,3},{3,2},{4,5},{5,4},{6,7},{7,6},{8,9},{9,8},{10,11... | collective-permute-start | bytes 4718600 | tf_op jit(solution)/shard_map/ppermute | solution.py:36
  60.4 14.1 %collective-permute-start.14 = (bf16[8,64,896]{2,1,0:T(8,128)(2,1)S(1)}, bf16[8,64,896]{2,1,0:T(8,128)(2,1)S(1)}, u32[]{:S(2)}, u32[]{:S(2)}) collective-permute-start(bf16[8,64,896]{2,1,0:T(8,128)(2,1)S(1)} %maximum_select_fusion.3), channel_id=1, source_target_pairs={{0,24},{1,7},{2,26},{3,5},{4,28},{5,3},{6,30},{7,1},{8,16},{9,15},... | collective-permute-start | bytes 2752520 | tf_op jit(solution)/shard_map/ppermute | solution.py:36
  101.3 11.2 %collective-permute-start.17 = (bf16[384,1024]{1,0:T(8,128)(2,1)S(1)}, bf16[384,1024]{1,0:T(8,128)(2,1)S(1)}, u32[]{:S(2)}, u32[]{:S(2)}) collective-permute-start(bf16[384,1024]{1,0:T(8,128)(2,1)S(1)} %slice.305), channel_id=1, source_target_pairs={{0,96},{1,33},{2,98},{3,35},{4,100},{5,37},{6,102},{7,39},{8,104},... | collective-permute-start | bytes 2359304 | tf_op jit(solution)/shard_map/ppermute | solution.py:36
  102.4 4.8 %collective-permute-start.19 = (bf16[1,64,1152]{2,1,0:T(8,128)(2,1)S(1)}, bf16[1,64,1152]{2,1,0:T(8,128)(2,1)S(1)}, u32[]{:S(2)}, u32[]{:S(2)}) collective-permute-start(bf16[1,64,1152]{2,1,0:T(8,128)(2,1)S(1)} %maximum_bitcast_fusion), channel_id=1, source_target_pairs={{0,2},{1,9},{2,0},{3,11},{4,6},{5,13},{6,4},{7,15},{8,10},{9,1},{1... | collective-permute-start | bytes 442376 | tf_op jit(solution)/shard_map/ppermute | solution.py:36
  107.2 7.3 %collective-permute-start.20 = (bf16[2,64,1152]{2,1,0:T(8,128)(2,1)S(1)}, bf16[2,64,1152]{2,1,0:T(8,128)(2,1)S(1)}, u32[]{:S(2)}, u32[]{:S(2)}) collective-permute-start(bf16[2,64,1152]{2,1,0:T(8,128)(2,1)S(1)} %maximum_select_fusion.6), channel_id=1, source_target_pairs={{0,6},{1,25},{2,4},{3,27},{4,2},{5,29},{6,0},{7,31},{8,14},{9,17},... | collective-permute-start | bytes 884744 | tf_op jit(solution)/shard_map/ppermute | solution.py:36
  112.8 7.9 %collective-permute-start.18 = (bf16[192,1024]{1,0:T(8,128)(2,1)S(1)}, bf16[192,1024]{1,0:T(8,128)(2,1)S(1)}, u32[]{:S(2)}, u32[]{:S(2)}) collective-permute-start(bf16[192,1024]{1,0:T(8,128)(2,1)S(1)} %slice.308), channel_id=1, source_target_pairs={{0,32},{1,97},{2,34},{3,99},{4,36},{5,101},{6,38},{7,103},{8,40},{... | collective-permute-start | bytes 1179656 | tf_op jit(solution)/shard_map/ppermute | solution.py:36
  114.6 9.1 %collective-permute-start.21 = (bf16[4,64,1152]{2,1,0:T(8,128)(2,1)S(1)}, bf16[4,64,1152]{2,1,0:T(8,128)(2,1)S(1)}, u32[]{:S(2)}, u32[]{:S(2)}) collective-permute-start(bf16[4,64,1152]{2,1,0:T(8,128)(2,1)S(1)} %maximum_select_fusion.4), channel_id=1, source_target_pairs={{0,8},{1,3},{2,10},{3,1},{4,12},{5,7},{6,14},{7,5},{8,0},{9,11},{1... | collective-permute-start | bytes 1769480 | tf_op jit(solution)/shard_map/ppermute | solution.py:36
  121.2 7.9 %collective-permute-start.23 = (bf16[192,1024]{1,0:T(8,128)(2,1)S(1)}, bf16[192,1024]{1,0:T(8,128)(2,1)S(1)}, u32[]{:S(2)}, u32[]{:S(2)}) collective-permute-start(bf16[192,1024]{1,0:T(8,128)(2,1)S(1)} %multiply_convert_fusion.6), channel_id=1, source_target_pairs={{0,32},{1,97},{2,34},{3,99},{4,36},{5,101},{6,38},{7,103},{8,40},{... | collective-permute-start | bytes 1179656 | tf_op jit(solution)/shard_map/ppermute | solution.py:36
  124.0 21.2 %collective-permute-start.22 = (bf16[8,64,1152]{2,1,0:T(8,128)(2,1)S(1)}, bf16[8,64,1152]{2,1,0:T(8,128)(2,1)S(1)}, u32[]{:S(2)}, u32[]{:S(2)}) collective-permute-start(bf16[8,64,1152]{2,1,0:T(8,128)(2,1)S(1)} %maximum_select_fusion.2), channel_id=1, source_target_pairs={{0,24},{1,7},{2,26},{3,5},{4,28},{5,3},{6,30},{7,1},{8,16},{9,15},... | collective-permute-start | bytes 3538952 | tf_op jit(solution)/shard_map/ppermute | solution.py:36
  129.2 11.2 %collective-permute-start.24 = (bf16[384,1024]{1,0:T(8,128)(2,1)S(1)}, bf16[384,1024]{1,0:T(8,128)(2,1)S(1)}, u32[]{:S(2)}, u32[]{:S(2)}) collective-permute-start(bf16[384,1024]{1,0:T(8,128)(2,1)S(1)} %pad_maximum_fusion.9), channel_id=1, source_target_pairs={{0,96},{1,33},{2,98},{3,35},{4,100},{5,37},{6,102},{7,39},{8,104},... | collective-permute-start | bytes 2359304 | tf_op jit(solution)/shard_map/ppermute | solution.py:36
  140.6 7.5 %collective-permute-start.26 = (bf16[768,1024]{1,0:T(8,128)(2,1)S(1)}, bf16[768,1024]{1,0:T(8,128)(2,1)S(1)}, u32[]{:S(2)}, u32[]{:S(2)}) collective-permute-start(bf16[768,1024]{1,0:T(8,128)(2,1)S(1)} %pad_maximum_fusion.2), channel_id=1, source_target_pairs={{0,1},{1,0},{2,3},{3,2},{4,5},{5,4},{6,7},{7,6},{8,9},{9,8},{10,11... | collective-permute-start | bytes 4718600 | tf_op jit(solution)/shard_map/ppermute | solution.py:36
  145.1 5.3 %collective-permute-start.25 = (bf16[768,1024]{1,0:T(8,128)(2,1)S(1)}, bf16[768,1024]{1,0:T(8,128)(2,1)S(1)}, u32[]{:S(2)}, u32[]{:S(2)}) collective-permute-start(bf16[768,1024]{1,0:T(8,128)(2,1)S(1)} %copy-done.13), channel_id=1, source_target_pairs={{0,1},{1,0},{2,3},{3,2},{4,5},{5,4},{6,7},{7,6},{8,9},{9,8},{10,11... | collective-permute-start | bytes 4718600 | tf_op jit(solution)/shard_map/ppermute | solution.py:36
  154.3 6.2 %collective-permute-start.27 = (bf16[768,1024]{1,0:T(8,128)(2,1)}, bf16[768,1024]{1,0:T(8,128)(2,1)}, u32[]{:S(2)}, u32[]{:S(2)}) collective-permute-start(bf16[768,1024]{1,0:T(8,128)(2,1)} %convolution_convert_fusion), channel_id=1, source_target_pairs={{0,1},{1,0},{2,3},{3,2},{4,5},{5,4},{6,7},{7,6},{8,9},{9,8},{10,11... | collective-permute-start | bytes 4718600 | tf_op jit(solution)/shard_map/ppermute | solution.py:36
  164.8 11.4 %collective-permute-start.28 = (bf16[384,1024]{1,0:T(8,128)(2,1)S(1)}, bf16[384,1024]{1,0:T(8,128)(2,1)S(1)}, u32[]{:S(2)}, u32[]{:S(2)}) collective-permute-start(bf16[384,1024]{1,0:T(8,128)(2,1)S(1)} %slice.304), channel_id=1, source_target_pairs={{0,96},{1,33},{2,98},{3,35},{4,100},{5,37},{6,102},{7,39},{8,104},... | collective-permute-start | bytes 2359304 | tf_op jit(solution)/shard_map/ppermute | solution.py:36
  176.6 7.9 %collective-permute-start.29 = (bf16[192,1024]{1,0:T(8,128)(2,1)S(1)}, bf16[192,1024]{1,0:T(8,128)(2,1)S(1)}, u32[]{:S(2)}, u32[]{:S(2)}) collective-permute-start(bf16[192,1024]{1,0:T(8,128)(2,1)S(1)} %slice.307), channel_id=1, source_target_pairs={{0,32},{1,97},{2,34},{3,99},{4,36},{5,101},{6,38},{7,103},{8,40},{... | collective-permute-start | bytes 1179656 | tf_op jit(solution)/shard_map/ppermute | solution.py:36
  186.1 8.2 %collective-permute-start.30 = (bf16[192,1024]{1,0:T(8,128)(2,1)S(1)}, bf16[192,1024]{1,0:T(8,128)(2,1)S(1)}, u32[]{:S(2)}, u32[]{:S(2)}) collective-permute-start(bf16[192,1024]{1,0:T(8,128)(2,1)S(1)} %get-tuple-element.100), channel_id=1, source_target_pairs={{0,32},{1,97},{2,34},{3,99},{4,36},{5,101},{6,38},{7,103},{8,40},{... | collective-permute-start | bytes 1179656 | tf_op jit(solution)/shard_map/ppermute | solution.py:36
  188.8 16.9 %collective-permute-start.32 = (bf16[8,64,1152]{2,1,0:T(8,128)(2,1)}, bf16[8,64,1152]{2,1,0:T(8,128)(2,1)}, u32[]{:S(2)}, u32[]{:S(2)}) collective-permute-start(bf16[8,64,1152]{2,1,0:T(8,128)(2,1)} %constant_dynamic-slice_fusion.5), channel_id=1, source_target_pairs={{0,24},{1,7},{2,26},{3,5},{4,28},{5,3},{6,30},{7,1},{8,16},{9,15},... | collective-permute-start | bytes 3538952 | tf_op jit(solution)/shard_map/ppermute | solution.py:36
  195.3 11.5 %collective-permute-start.31 = (bf16[384,1024]{1,0:T(8,128)(2,1)}, bf16[384,1024]{1,0:T(8,128)(2,1)}, u32[]{:S(2)}, u32[]{:S(2)}) collective-permute-start(bf16[384,1024]{1,0:T(8,128)(2,1)} %pad_maximum_fusion.10), channel_id=1, source_target_pairs={{0,96},{1,33},{2,98},{3,35},{4,100},{5,37},{6,102},{7,39},{8,104},... | collective-permute-start | bytes 2359304 | tf_op jit(solution)/shard_map/ppermute | solution.py:36
  207.9 6.9 %collective-permute-start.33 = (bf16[768,1024]{1,0:T(8,128)(2,1)S(1)}, bf16[768,1024]{1,0:T(8,128)(2,1)S(1)}, u32[]{:S(2)}, u32[]{:S(2)}) collective-permute-start(bf16[768,1024]{1,0:T(8,128)(2,1)S(1)} %constant_dynamic-update-slice_fusion.11.own_ref), channel_id=1, source_target_pairs={{0,1},{1,0},{2,3},{3,2},{4,5},{5,4},{6,7},{7,6},{8,9},{9,8},{10,11... | collective-permute-start | bytes 4718600 | tf_op jit(solution)/shard_map/ppermute | solution.py:36
  213.8 21.9 %collective-permute-start.34 = (bf16[4,64,1152]{2,1,0:T(8,128)(2,1)S(1)}, bf16[4,64,1152]{2,1,0:T(8,128)(2,1)S(1)}, u32[]{:S(2)}, u32[]{:S(2)}) collective-permute-start(bf16[4,64,1152]{2,1,0:T(8,128)(2,1)S(1)} %constant_dynamic-slice_fusion.4), channel_id=1, source_target_pairs={{0,8},{1,3},{2,10},{3,1},{4,12},{5,7},{6,14},{7,5},{8,0},{9,11},{1... | collective-permute-start | bytes 1769480 | tf_op jit(solution)/shard_map/ppermute | solution.py:36
  221.6 14.0 %collective-permute-start.35 = (bf16[8,64,256]{2,1,0:T(8,128)(2,1)S(1)}, bf16[8,64,256]{2,1,0:T(8,128)(2,1)S(1)}, u32[]{:S(2)}, u32[]{:S(2)}) collective-permute-start(bf16[8,64,256]{2,1,0:T(8,128)(2,1)S(1)} %slice.172), channel_id=1, source_target_pairs={{0,24},{1,7},{2,26},{3,5},{4,28},{5,3},{6,30},{7,1},{8,16},{9,15},... | collective-permute-start | bytes 786440 | tf_op jit(solution)/shard_map/ppermute | solution.py:36
  255.4 17.1 %collective-permute-start.37 = (bf16[384,1024]{1,0:T(8,128)(2,1)S(1)}, bf16[384,1024]{1,0:T(8,128)(2,1)S(1)}, u32[]{:S(2)}, u32[]{:S(2)}) collective-permute-start(bf16[384,1024]{1,0:T(8,128)(2,1)S(1)} %slice.303), channel_id=1, source_target_pairs={{0,96},{1,33},{2,98},{3,35},{4,100},{5,37},{6,102},{7,39},{8,104},... | collective-permute-start | bytes 2359304 | tf_op jit(solution)/shard_map/ppermute | solution.py:36
  257.6 14.9 %collective-permute-start.38 = (bf16[8,64,640]{2,1,0:T(8,128)(2,1)S(1)}, bf16[8,64,640]{2,1,0:T(8,128)(2,1)}, u32[]{:S(2)}, u32[]{:S(2)}) collective-permute-start(bf16[8,64,640]{2,1,0:T(8,128)(2,1)S(1)} %constant_dynamic-slice_fusion.3), channel_id=1, source_target_pairs={{0,24},{1,7},{2,26},{3,5},{4,28},{5,3},{6,30},{7,1},{8,16},{9,15},... | collective-permute-start | bytes 1966088 | tf_op jit(solution)/shard_map/ppermute | solution.py:36
  260.6 4.7 %collective-permute-start.39 = (bf16[4,64,256]{2,1,0:T(8,128)(2,1)S(1)}, bf16[4,64,256]{2,1,0:T(8,128)(2,1)S(1)}, u32[]{:S(2)}, u32[]{:S(2)}) collective-permute-start(bf16[4,64,256]{2,1,0:T(8,128)(2,1)S(1)} %constant_dynamic-slice_fusion.2), channel_id=1, source_target_pairs={{0,8},{1,3},{2,10},{3,1},{4,12},{5,7},{6,14},{7,5},{8,0},{9,11},{1... | collective-permute-start | bytes 393224 | tf_op jit(solution)/shard_map/ppermute | solution.py:36
  260.9 5.8 %collective-permute-start.40 = (bf16[64,1152]{1,0:T(8,128)(2,1)S(1)}, bf16[64,1152]{1,0:T(8,128)(2,1)S(1)}, u32[]{:S(2)}, u32[]{:S(2)}) collective-permute-start(bf16[64,1152]{1,0:T(8,128)(2,1)S(1)} %get-tuple-element.164), channel_id=1, source_target_pairs={{0,2},{1,9},{2,0},{3,11},{4,6},{5,13},{6,4},{7,15},{8,10},{9,1},{1... | collective-permute-start | bytes 442376 | tf_op jit(solution)/shard_map/ppermute | solution.py:36
  261.0 7.1 %collective-permute-start.41 = (bf16[64,1152]{1,0:T(8,128)(2,1)S(1)}, bf16[64,1152]{1,0:T(8,128)(2,1)S(1)}, u32[]{:S(2)}, u32[]{:S(2)}) collective-permute-start(bf16[64,1152]{1,0:T(8,128)(2,1)S(1)} %get-tuple-element.163), channel_id=1, source_target_pairs={{0,4},{1,17},{2,6},{3,19},{4,0},{5,21},{6,2},{7,23},{8,12},{9,25},... | collective-permute-start | bytes 442376 | tf_op jit(solution)/shard_map/ppermute | solution.py:36
  265.2 7.2 %collective-permute-start.42 = (bf16[64,1152]{1,0:T(8,128)(2,1)S(1)}, bf16[64,1152]{1,0:T(8,128)(2,1)S(1)}, u32[]{:S(2)}, u32[]{:S(2)}) collective-permute-start(bf16[64,1152]{1,0:T(8,128)(2,1)S(1)} %get-tuple-element.162), channel_id=1, source_target_pairs={{0,6},{1,25},{2,4},{3,27},{4,2},{5,29},{6,0},{7,31},{8,14},{9,17},... | collective-permute-start | bytes 442376 | tf_op jit(solution)/shard_map/ppermute | solution.py:36
  274.3 10.3 %collective-permute-start.43 = (bf16[192,1024]{1,0:T(8,128)(2,1)S(1)}, bf16[192,1024]{1,0:T(8,128)(2,1)S(1)}, u32[]{:S(2)}, u32[]{:S(2)}) collective-permute-start(bf16[192,1024]{1,0:T(8,128)(2,1)S(1)} %slice.306), channel_id=1, source_target_pairs={{0,32},{1,97},{2,34},{3,99},{4,36},{5,101},{6,38},{7,103},{8,40},{... | collective-permute-start | bytes 1179656 | tf_op jit(solution)/shard_map/ppermute | solution.py:36
  277.3 7.3 %collective-permute-start.44 = (bf16[4,64,640]{2,1,0:T(8,128)(2,1)S(1)}, bf16[4,64,640]{2,1,0:T(8,128)(2,1)S(1)}, u32[]{:S(2)}, u32[]{:S(2)}) collective-permute-start(bf16[4,64,640]{2,1,0:T(8,128)(2,1)S(1)} %constant_dynamic-slice_fusion.1), channel_id=1, source_target_pairs={{0,8},{1,3},{2,10},{3,1},{4,12},{5,7},{6,14},{7,5},{8,0},{9,11},{1... | collective-permute-start | bytes 983048 | tf_op jit(solution)/shard_map/ppermute | solution.py:36
  277.5 4.9 %collective-permute-start.45 = (bf16[64,256]{1,0:T(8,128)(2,1)S(1)}, bf16[64,256]{1,0:T(8,128)(2,1)S(1)}, u32[]{:S(2)}, u32[]{:S(2)}) collective-permute-start(bf16[64,256]{1,0:T(8,128)(2,1)S(1)} %get-tuple-element.187), channel_id=1, source_target_pairs={{0,2},{1,9},{2,0},{3,11},{4,6},{5,13},{6,4},{7,15},{8,10},{9,1},{1... | collective-permute-start | bytes 98312 | tf_op jit(solution)/shard_map/ppermute | solution.py:36
  277.6 5.6 %collective-permute-start.46 = (bf16[64,256]{1,0:T(8,128)(2,1)S(1)}, bf16[64,256]{1,0:T(8,128)(2,1)S(1)}, u32[]{:S(2)}, u32[]{:S(2)}) collective-permute-start(bf16[64,256]{1,0:T(8,128)(2,1)S(1)} %get-tuple-element.186), channel_id=1, source_target_pairs={{0,4},{1,17},{2,6},{3,19},{4,0},{5,21},{6,2},{7,23},{8,12},{9,25},... | collective-permute-start | bytes 98312 | tf_op jit(solution)/shard_map/ppermute | solution.py:36
  285.2 13.0 %collective-permute-start.48 = (bf16[192,1024]{1,0:T(8,128)(2,1)S(1)}, bf16[192,1024]{1,0:T(8,128)(2,1)S(1)}, u32[]{:S(2)}, u32[]{:S(2)}) collective-permute-start(bf16[192,1024]{1,0:T(8,128)(2,1)S(1)} %get-tuple-element.148), channel_id=1, source_target_pairs={{0,0},{1,16},{2,2},{3,18},{4,4},{5,20},{6,6},{7,22},{8,8},{9,24},{... | collective-permute-start | bytes 1179656 | tf_op jit(solution)/shard_map/ppermute | solution.py:44
  291.1 5.5 %collective-permute-start.49 = (bf16[64,640]{1,0:T(8,128)(2,1)S(1)}, bf16[64,640]{1,0:T(8,128)(2,1)S(1)}, u32[]{:S(2)}, u32[]{:S(2)}) collective-permute-start(bf16[64,640]{1,0:T(8,128)(2,1)S(1)} %get-tuple-element.168), channel_id=1, source_target_pairs={{0,2},{1,9},{2,0},{3,11},{4,6},{5,13},{6,4},{7,15},{8,10},{9,1},{1... | collective-permute-start | bytes 245768 | tf_op jit(solution)/shard_map/ppermute | solution.py:36
  291.2 6.3 %collective-permute-start.50 = (bf16[64,640]{1,0:T(8,128)(2,1)S(1)}, bf16[64,640]{1,0:T(8,128)(2,1)S(1)}, u32[]{:S(2)}, u32[]{:S(2)}) collective-permute-start(bf16[64,640]{1,0:T(8,128)(2,1)S(1)} %get-tuple-element.167), channel_id=1, source_target_pairs={{0,4},{1,17},{2,6},{3,19},{4,0},{5,21},{6,2},{7,23},{8,12},{9,25},... | collective-permute-start | bytes 245768 | tf_op jit(solution)/shard_map/ppermute | solution.py:36
  291.3 6.9 %collective-permute-start.51 = (bf16[64,640]{1,0:T(8,128)(2,1)S(1)}, bf16[64,640]{1,0:T(8,128)(2,1)S(1)}, u32[]{:S(2)}, u32[]{:S(2)}) collective-permute-start(bf16[64,640]{1,0:T(8,128)(2,1)S(1)} %get-tuple-element.166), channel_id=1, source_target_pairs={{0,6},{1,25},{2,4},{3,27},{4,2},{5,29},{6,0},{7,31},{8,14},{9,17},... | collective-permute-start | bytes 245768 | tf_op jit(solution)/shard_map/ppermute | solution.py:36
  298.2 5.1 %collective-permute-start.53 = (bf16[4,1,8,1408]{3,2,1,0:T(8,128)(2,1)S(1)}, bf16[4,1,8,1408]{3,2,1,0:T(8,128)(2,1)S(1)}, u32[]{:S(2)}, u32[]{:S(2)}) collective-permute-start(bf16[4,1,8,1408]{3,2,1,0:T(8,128)(2,1)S(1)} %constant_dynamic-slice_fusion), channel_id=1, source_target_pairs={{0,1},{1,0},{2,3},{3,2},{4,5},{5,4},{6,7},{7,6},{8,9},{9,8},{10,11... | collective-permute-start | bytes 270344 | tf_op jit(solution)/shard_map/ppermute | solution.py:36
  298.4 15.6 %collective-permute-start.52 = (bf16[208,1024]{1,0:T(8,128)(2,1)S(1)}, bf16[208,1024]{1,0:T(8,128)(2,1)S(1)}, u32[]{:S(2)}, u32[]{:S(2)}) collective-permute-start(bf16[208,1024]{1,0:T(8,128)(2,1)S(1)} %pad_maximum_fusion.11), channel_id=1, source_target_pairs={{0,0},{1,16},{2,2},{3,18},{4,4},{5,20},{6,6},{7,22},{8,8},{9,24},{... | collective-permute-start | bytes 1277960 | tf_op jit(solution)/shard_map/ppermute | solution.py:44
  (58 other events, 499.9 us)
Sparse Core Ops, SparseCore 0:
  211.9 32.4 reduce-scatter.1

commit v4 on v3

--- a/solution.py
+++ b/solution.py
@@ -728,29 +728,31 @@
     got = swap(d_normed_other, CORE)
     total = wide(d_normed_own) + wide(got)
     keep, send = total[: 2 * TOK], low(total[2 * TOK :])
-    payload, sums_got, out_got = (after(array, send) for array in (payload, sums_got, out_got))
-    sums_keep, sums_got = plane_rest(index, low(wide(sums_keep) + wide(sums_got)))
+    payload, out_got = (after(array, send) for array in (payload, out_got))
     sums_out = low(wide(grad_out[:8]) + wide(out_got))
     heads_keep, heads_got = plane_halves(index, payload, 3)
     out_keep, out_got = plane_halves(index, sums_out, 2)
-    got, heads_got, out_got, sums_got, result = lax.optimization_barrier(
-        (swap(send, *RING_STEPS[1]), heads_got, out_got, sums_got, result)
-    )
-    sums = wide(sums_keep) + sum(wide(part) for part in sums_got)
+    got, heads_got, out_got, result = lax.optimization_barrier(
+        (swap(send, *RING_STEPS[1]), heads_got, out_got, result)
+    )
     sums_out = low(wide(out_keep) + wide(out_got))
     heads_sums = low(wide(heads_keep) + wide(heads_got))
     total = keep + wide(got)
     heads_keep, heads_got = plane_halves(index, heads_sums, 2)
-    out_keep, out_got = plane_rest(index, sums_out)
-    got, heads_got, out_got = lax.optimization_barrier(
-        (swap(low(total[TOK:]), *RING_STEPS[0]), heads_got, out_got)
-    )
-    sum_out = wide(out_keep) + sum(wide(part) for part in out_got)
+    sums_keep, sums_got = plane_rest(index, low(wide(sums_keep) + wide(sums_got)))
+    got, heads_got, sums_got = lax.optimization_barrier(
+        (swap(low(total[TOK:]), *RING_STEPS[0]), heads_got, sums_got)
+    )
+    sums = wide(sums_keep) + sum(wide(part) for part in sums_got)
     heads_sums = low(wide(heads_keep) + wide(heads_got))
     d_normed = total[:TOK] + wide(got)
     input_grad = d_middle + norm_back(wide(inputs), gain_attn, d_normed)
     heads_keep, heads_got = plane_rest(index, heads_sums)
-    home, heads_got = lax.optimization_barrier((cross(low(input_grad)), heads_got))
+    out_keep, out_got = plane_rest(index, sums_out)
+    home, heads_got, out_got = lax.optimization_barrier(
+        (cross(low(input_grad)), heads_got, out_got)
+    )
+    sum_out = wide(out_keep) + sum(wide(part) for part in out_got)
     input_grad = jnp.where(straight, input_grad, wide(home))
     heads_sums = low(wide(heads_keep) + sum(wide(part) for part in heads_got))
     sum_down = tiles_flat(sums[:, 768:])

time: 329 us -> 326 us (level)
  waiting for transfers between devices: 89.9 us -> 84.7 us
    ppermute x51, waiting for transfers between devices: 89.8 us -> 84.7 us  [swap(): lax.ppermute(values, AXES, [(k, k ^ masks[k & 1]) for k in range(DEVICES)])]
  transfers between devices with their start and end apart: 58 -> 58, of which waited for: 34 -> 29; matrix products, arithmetic and copies ran while one was open for 15% -> 16% of each run, Pallas kernels for 10% -> 10%
where the time goes in v4:
time: 326 us; the launch traced here: 320 us
  starting transfers between devices  92.5 us (28%)
  waiting for transfers between devices  84.7 us (26%)
  Pallas kernels  52.1 us (16%)
  local copies, waits for them, and re-layouts  28.1 us (9%)
  other arithmetic  25.2 us (8%)
  matrix products  19.7 us (6%)
  between operations  17.5 us (5%)
    ppermute x51, waiting for transfers between devices, swap(): lax.ppermute(values, AXES, [(k, k ^ masks[k & 1]) for k in range(DEVICES)])  84.7 us
    ppermute x51, starting transfers between devices, swap(): lax.ppermute(values, AXES, [(k, k ^ masks[k & 1]) for k in range(DEVICES)])  63.4 us
    pallas_call x6, Pallas kernels, ring_call(): pl.pallas_call(kernel, grid_spec=pltpu.PrefetchScalarGridSpec(num_scalar_...  34.3 us
    ppermute x5, starting transfers between devices, cross(): return lax.ppermute(values, AXES, [(k, crossed(k)) for k in range(DEVICES)])  28 us
    unnamed x108, local copies, waits for them, and re-layouts  11.7 us
    pallas_call x1, Pallas kernels, attend_back(): pl.pallas_call(attend_back_kernel, grid_spec=pltpu.PrefetchScalarGridSpec...  11 us
    dot_general x4, matrix products, contract_cols(): lax.dot_general(left, right, (((1,), (1,)), ((), ())), preferred_element_...  8.07 us
    pallas_call x1, Pallas kernels, attend(): pl.pallas_call(attend_kernel, grid_spec=pltpu.PrefetchScalarGridSpec(num_...  6.71 us
  transfers between devices with their start and end apart: 58, of which 29 were waited for; matrix products, arithmetic and copies ran while one was open for 16% of the time, Pallas kernels for 10%

profile of v4, /device:TPU:1, one launch (start us, length us, event | category | flops | bytes accessed | tf_op | source)
XLA Modules:
  0.0 319.7 jit_solution(14865770279682858795)
XLA Ops:
  7.3 6.9 %collective-permute-start = (bf16[192,1024]{1,0:T(8,128)(2,1)}, bf16[192,1024]{1,0:T(8,128)(2,1)S(1)}, u32[]{:S(2)}, u32[]{:S(2)}) collective-permute-start(bf16[192,1024]{1,0:T(8,128)(2,1)} %bitcast.262), channel_id=1, source_target_pairs={{0,0},{1,16},{2,2},{3,18},{4,4},{5,20},{6,6},{7,22},{8,8},{9,24},{... | collective-permute-start | bytes 1179656 | tf_op jit(solution)/shard_map/ppermute | solution.py:44
  16.6 6.4 %collective-permute-start.1 = (bf16[32,1024]{1,0:T(8,128)(2,1)S(1)}, bf16[32,1024]{1,0:T(8,128)(2,1)S(1)}, u32[]{:S(2)}, u32[]{:S(2)}) collective-permute-start(bf16[32,1024]{1,0:T(8,128)(2,1)S(1)} %pad_maximum_fusion.15), channel_id=1, source_target_pairs={{0,0},{1,16},{2,2},{3,18},{4,4},{5,20},{6,6},{7,22},{8,8},{9,24},{... | collective-permute-start | bytes 196616 | tf_op jit(solution)/shard_map/ppermute | solution.py:44
  35.1 3.5 %collective-permute-start.10 = (bf16[192,1024]{1,0:T(8,128)(2,1)S(1)}, bf16[192,1024]{1,0:T(8,128)(2,1)S(1)}, u32[]{:S(2)}, u32[]{:S(2)}) collective-permute-start(bf16[192,1024]{1,0:T(8,128)(2,1)S(1)} %bitcast.264), channel_id=1, source_target_pairs={{0,0},{1,16},{2,2},{3,18},{4,4},{5,20},{6,6},{7,22},{8,8},{9,24},{... | collective-permute-start | bytes 1179656 | tf_op jit(solution)/shard_map/ppermute | solution.py:44
  42.3 3.7 %collective-permute-done.9 = bf16[1,64,896]{2,1,0:T(8,128)(2,1)S(1)} collective-permute-done((bf16[1,64,896]{2,1,0:T(8,128)(2,1)S(1)}, bf16[1,64,896]{2,1,0:T(8,128)(2,1)S(1)}, u32[]{:S(2)}, u32[]{:S(2)}) %collective-permute-start.9) | collective-permute-done | bytes 114720 | tf_op jit(solution)/shard_map/ppermute | solution.py:36
  49.3 3.2 %collective-permute-done.11 = bf16[2,64,896]{2,1,0:T(8,128)(2,1)S(1)} collective-permute-done((bf16[2,64,896]{2,1,0:T(8,128)(2,1)S(1)}, bf16[2,64,896]{2,1,0:T(8,128)(2,1)S(1)}, u32[]{:S(2)}, u32[]{:S(2)}) %collective-permute-start.11) | collective-permute-done | bytes 229408 | tf_op jit(solution)/shard_map/ppermute | solution.py:36
  54.8 3.0 collective-permute-done.13
  60.4 3.0 collective-permute-start.14
  63.4 2.8 fusion.11
  70.4 4.1 %collective-permute-done.14 = bf16[8,64,896]{2,1,0:T(8,128)(2,1)S(1)} collective-permute-done((bf16[8,64,896]{2,1,0:T(8,128)(2,1)S(1)}, bf16[8,64,896]{2,1,0:T(8,128)(2,1)S(1)}, u32[]{:S(2)}, u32[]{:S(2)}) %collective-permute-start.14) | collective-permute-done | bytes 917536 | tf_op jit(solution)/shard_map/ppermute | solution.py:36
  76.1 10.7 %project.1 = (bf16[1536,1024]{1,0:T(8,128)(2,1)}, f32[1536,384]{1,0:T(8,128)}, bf16[1536,512]{1,0:T(8,128)(2,1)S(1)}, bf16[1536,512]{1,0:T(8,128)(2,1)}, bf16[51...) custom-call(s32[11]{0:T(128)S(1)} %concatenate.161.spots, bf16[768,1024]{1,0:T(8,128)(2,1)} %constant_dynamic-update-slice_fusion.own_ref, ...), custom_call_target="tpu_custom_call" | custom-call | bytes 800000 | tf_op jit(solution)/shard_map/project/pallas_call | solution.py:138
  86.8 6.7 %attend.1 = (bf16[1536,256]{1,0:T(8,128)(2,1)S(1)}, bf16[1536,256]{1,0:T(8,128)(2,1)}, f32[2,1536]{1,0:T(2,128)}) custom-call(s32[2]{0:T(128)S(1)} %pad_add_fusion.ends_ref, bf16[1536,512]{1,0:T(8,128)(2,1)S(1)} %get-tuple-element.82.q_ref.k_ref.v_ref, bf16[1536,512]{1,0:T(8,128)(2,1)S(1)} %get-tuple-element.82.q_ref.k_ref.v_ref, ...), custom_call_target="tpu_custom_call" | custom-call | bytes 600000 | tf_op jit(solution)/shard_map/attend/pallas_call | solution.py:334
  93.5 2.9 to_ring.1
  97.5 3.0 collective-permute-done.16
  102.9 4.3 %collective-permute-done.19 = bf16[1,64,1152]{2,1,0:T(8,128)(2,1)S(1)} collective-permute-done((bf16[1,64,1152]{2,1,0:T(8,128)(2,1)S(1)}, bf16[1,64,1152]{2,1,0:T(8,128)(2,1)S(1)}, u32[]{:S(2)}, u32[]{:S(2)}) %collective-permute-start.19) | collective-permute-done | bytes 147488 | tf_op jit(solution)/shard_map/ppermute | solution.py:36
  107.2 2.9 collective-permute-start.20
  110.1 2.5 collective-permute-done.17
  115.3 5.5 %collective-permute-done.18 = bf16[192,1024]{1,0:T(8,128)(2,1)S(1)} collective-permute-done((bf16[192,1024]{1,0:T(8,128)(2,1)S(1)}, bf16[192,1024]{1,0:T(8,128)(2,1)S(1)}, u32[]{:S(2)}, u32[]{:S(2)}) %collective-permute-start.18) | collective-permute-done | bytes 393248 | tf_op jit(solution)/shard_map/ppermute | solution.py:36
  124.0 2.8 collective-permute-start.22
  126.8 2.4 collective-permute-done.23
  129.3 11.1 %collective-permute-done.24 = bf16[384,1024]{1,0:T(8,128)(2,1)S(1)} collective-permute-done((bf16[384,1024]{1,0:T(8,128)(2,1)S(1)}, bf16[384,1024]{1,0:T(8,128)(2,1)S(1)}, u32[]{:S(2)}, u32[]{:S(2)}) %collective-permute-start.24) | collective-permute-done | bytes 786464 | tf_op jit(solution)/shard_map/ppermute | solution.py:36
  140.6 4.5 %collective-permute-start.26 = (bf16[768,1024]{1,0:T(8,128)(2,1)S(1)}, bf16[768,1024]{1,0:T(8,128)(2,1)S(1)}, u32[]{:S(2)}, u32[]{:S(2)}) collective-permute-start(bf16[768,1024]{1,0:T(8,128)(2,1)S(1)} %pad_maximum_fusion.2), channel_id=1, source_target_pairs={{0,1},{1,0},{2,3},{3,2},{4,5},{5,4},{6,7},{7,6},{8,9},{9,8},{10,11... | collective-permute-start | bytes 4718600 | tf_op jit(solution)/shard_map/ppermute | solution.py:36
  151.7 2.6 convolution_convert_fusion
  154.7 3.2 fusion.47
  161.9 2.8 convert_add_fusion.1
  172.3 3.9 %collective-permute-done.28 = bf16[384,1024]{1,0:T(8,128)(2,1)S(1)} collective-permute-done((bf16[384,1024]{1,0:T(8,128)(2,1)S(1)}, bf16[384,1024]{1,0:T(8,128)(2,1)S(1)}, u32[]{:S(2)}, u32[]{:S(2)}) %collective-permute-start.28) | collective-permute-done | bytes 786464 | tf_op jit(solution)/shard_map/ppermute | solution.py:36
  178.9 5.6 %collective-permute-done.29 = bf16[192,1024]{1,0:T(8,128)(2,1)S(1)} collective-permute-done((bf16[192,1024]{1,0:T(8,128)(2,1)S(1)}, bf16[192,1024]{1,0:T(8,128)(2,1)S(1)}, u32[]{:S(2)}, u32[]{:S(2)}) %collective-permute-start.29) | collective-permute-done | bytes 393248 | tf_op jit(solution)/shard_map/ppermute | solution.py:36
  188.8 2.7 collective-permute-start.32
  191.6 2.8 collective-permute-done.30
  195.3 4.1 %to_pack.1 = bf16[1536,1024]{1,0:T(8,128)(2,1)} custom-call(s32[11]{0:T(128)S(1)} %concatenate.161.spots, bf16[768,384]{1,0:T(8,128)(2,1)S(1)} %get-tuple-element.100.own_ref, bf16[768,384]{1,0:T(8,128)(2,1)S(1)} %get-tuple-element.101.other_ref, bf16[384,1024]{1,0:T(8,128)(2,1)S(1)} %bitcast.207), custom_call_target="tpu_custom_call" | custom-call | bytes 400000 | tf_op jit(solution)/shard_map/to_pack/pallas_call | solution.py:138
  199.4 6.3 %collective-permute-done.32 = bf16[8,64,1152]{2,1,0:T(8,128)(2,1)} collective-permute-done((bf16[8,64,1152]{2,1,0:T(8,128)(2,1)}, bf16[8,64,1152]{2,1,0:T(8,128)(2,1)}, u32[]{:S(2)}, u32[]{:S(2)}) %collective-permute-start.32) | collective-permute-done | bytes 1179680 | tf_op jit(solution)/shard_map/ppermute | solution.py:36
  207.9 3.8 %collective-permute-start.33 = (bf16[768,1024]{1,0:T(8,128)(2,1)S(1)}, bf16[768,1024]{1,0:T(8,128)(2,1)S(1)}, u32[]{:S(2)}, u32[]{:S(2)}) collective-permute-start(bf16[768,1024]{1,0:T(8,128)(2,1)S(1)} %constant_dynamic-update-slice_fusion.11.own_ref), channel_id=1, source_target_pairs={{0,1},{1,0},{2,3},{3,2},{4,5},{5,4},{6,7},{7,6},{8,9},{9,8},{10,11... | collective-permute-start | bytes 4718600 | tf_op jit(solution)/shard_map/ppermute | solution.py:36
  211.8 1.9 add_convert_fusion.1
  214.8 5.8 %out_back.1 = (bf16[1536,256]{1,0:T(8,128)(2,1)S(1)}, bf16[16,64,256]{2,1,0:T(8,128)(2,1)}) custom-call(s32[11]{0:T(128)S(1)} %concatenate.161.spots, bf16[768,1024]{1,0:T(8,128)(2,1)S(1)} %constant_dynamic-update-slice_fusion.11.own_ref, bf16[768,1024]{1,0:T(8,128)(2,1)S(1)} %collective-permute-done.33.other_ref, ...), custom_call_target="tpu_custom_call" | custom-call | bytes 500000 | tf_op jit(solution)/shard_map/out_back/pallas_call | solution.py:138
  221.6 3.0 collective-permute-start.35
  224.6 11.0 %attend_back.1 = (f32[1536,256]{1,0:T(8,128)S(1)}, f32[1536,128]{1,0:T(8,128)S(1)}, f32[1536,128]{1,0:T(8,128)S(1)}) custom-call(s32[2]{0:T(128)S(1)} %pad_add_fusion.ends_ref, bf16[1536,512]{1,0:T(8,128)(2,1)} %get-tuple-element.87.q_ref.k_ref.v_ref, bf16[1536,512]{1,0:T(8,128)(2,1)} %get-tuple-element.87.q_ref.k_ref.v_ref, ...), custom_call_target="tpu_custom_call" | custom-call | bytes 1100000 | tf_op jit(solution)/shard_map/attend_back/pallas_call | solution.py:406
  235.7 5.8 %project_back.1 = (bf16[1536,512]{1,0:T(8,128)(2,1)S(1)}, f32[2,128]{1,0:T(2,128)S(1)}) custom-call(s32[11]{0:T(128)S(1)} %concatenate.161.spots, f32[1536,384]{1,0:T(8,128)} %get-tuple-element.86.pre_ref, f32[1536,256]{1,0:T(8,128)S(1)} %get-tuple-element.109.dq_ref, f32[1536,128]{1,0:T(8,128)S(1)} %get-tuple-element.110.dk_ref, ...), custom_call_target="tpu_custom_call" | custom-call | bytes 500000 | tf_op jit(solution)/shard_map/project_back/pallas_call | solution.py:138
  241.5 1.9 fusion.51
  245.2 5.1 %normed_back.1 = (bf16[768,1024]{1,0:T(8,128)(2,1)S(1)}, bf16[768,1024]{1,0:T(8,128)(2,1)}) custom-call(s32[11]{0:T(128)S(1)} %concatenate.161.spots, bf16[1536,512]{1,0:T(8,128)(2,1)S(1)} %get-tuple-element.116.d_pre_ref, bf16[512,1024]{1,0:T(8,128)(2,1)} %get-tuple-element.117.w_ref), custom_call_target="tpu_custom_call" | custom-call | bytes 400000 | tf_op jit(solution)/shard_map/normed_back/pallas_call | solution.py:138
  251.4 3.2 %collective-permute-done.36 = bf16[768,1024]{1,0:T(8,128)(2,1)S(1)} collective-permute-done((bf16[768,1024]{1,0:T(8,128)(2,1)}, bf16[768,1024]{1,0:T(8,128)(2,1)S(1)}, u32[]{:S(2)}, u32[]{:S(2)}) %collective-permute-start.36) | collective-permute-done | bytes 1572896 | tf_op jit(solution)/shard_map/ppermute | solution.py:36
  255.5 2.0 copy-done.15
  257.6 2.8 collective-permute-start.38
  263.0 2.0 collective-permute-done.39
  265.5 4.9 %collective-permute-done.38 = bf16[8,64,640]{2,1,0:T(8,128)(2,1)} collective-permute-done((bf16[8,64,640]{2,1,0:T(8,128)(2,1)S(1)}, bf16[8,64,640]{2,1,0:T(8,128)(2,1)}, u32[]{:S(2)}, u32[]{:S(2)}) %collective-permute-start.38) | collective-permute-done | bytes 655392 | tf_op jit(solution)/shard_map/ppermute | solution.py:36
  276.2 4.1 %collective-permute-start.50 = (bf16[64,256]{1,0:T(8,128)(2,1)S(1)}, bf16[64,256]{1,0:T(8,128)(2,1)S(1)}, u32[]{:S(2)}, u32[]{:S(2)}) collective-permute-start(bf16[64,256]{1,0:T(8,128)(2,1)S(1)} %get-tuple-element.184), channel_id=1, source_target_pairs={{0,4},{1,17},{2,6},{3,19},{4,0},{5,21},{6,2},{7,23},{8,12},{9,25},... | collective-permute-start | bytes 98312 | tf_op jit(solution)/shard_map/ppermute | solution.py:36
  282.5 6.0 %collective-permute-start.45 = (bf16[192,1024]{1,0:T(8,128)(2,1)S(1)}, bf16[192,1024]{1,0:T(8,128)(2,1)S(1)}, u32[]{:S(2)}, u32[]{:S(2)}) collective-permute-start(bf16[192,1024]{1,0:T(8,128)(2,1)S(1)} %get-tuple-element.146), channel_id=1, source_target_pairs={{0,0},{1,16},{2,2},{3,18},{4,4},{5,20},{6,6},{7,22},{8,8},{9,24},{... | collective-permute-start | bytes 1179656 | tf_op jit(solution)/shard_map/ppermute | solution.py:44
  289.8 2.9 collective-permute-start.48
  293.4 2.0 collective-permute-done.46
  296.1 5.2 %collective-permute-start.52 = (bf16[208,1024]{1,0:T(8,128)(2,1)S(1)}, bf16[208,1024]{1,0:T(8,128)(2,1)S(1)}, u32[]{:S(2)}, u32[]{:S(2)}) collective-permute-start(bf16[208,1024]{1,0:T(8,128)(2,1)S(1)} %pad_maximum_fusion.11), channel_id=1, source_target_pairs={{0,0},{1,16},{2,2},{3,18},{4,4},{5,20},{6,6},{7,22},{8,8},{9,24},{... | collective-permute-start | bytes 1277960 | tf_op jit(solution)/shard_map/ppermute | solution.py:44
  (347 shorter events, 98.9 us)
Async XLA Ops:
  7.2 263.2 %reduce-scatter.2.cloned.1.call-start = ((), (), s32[]{:S(2)}) async-start(), calls=%async_computation.1 | async-start | bytes 3538944 | tf_op jit(solution)/shard_map/reduce_scatter | solution.py:703
  7.3 33.3 %collective-permute-start = (bf16[192,1024]{1,0:T(8,128)(2,1)}, bf16[192,1024]{1,0:T(8,128)(2,1)S(1)}, u32[]{:S(2)}, u32[]{:S(2)}) collective-permute-start(bf16[192,1024]{1,0:T(8,128)(2,1)} %bitcast.262), channel_id=1, source_target_pairs={{0,0},{1,16},{2,2},{3,18},{4,4},{5,20},{6,6},{7,22},{8,8},{9,24},{... | collective-permute-start | bytes 1179656 | tf_op jit(solution)/shard_map/ppermute | solution.py:44
  14.2 26.4 %collective-permute-start.2 = (bf16[192,1024]{1,0:T(8,128)(2,1)}, bf16[192,1024]{1,0:T(8,128)(2,1)S(1)}, u32[]{:S(2)}, u32[]{:S(2)}) collective-permute-start(bf16[192,1024]{1,0:T(8,128)(2,1)} %bitcast.263), channel_id=1, source_target_pairs={{32,0},{112,1},{34,2},{114,3},{36,4},{116,5},{38,6},{118,7},{40,8}... | collective-permute-start | bytes 1179656 | tf_op jit(solution)/shard_map/ppermute | solution.py:48
  16.6 12.5 %collective-permute-start.1 = (bf16[32,1024]{1,0:T(8,128)(2,1)S(1)}, bf16[32,1024]{1,0:T(8,128)(2,1)S(1)}, u32[]{:S(2)}, u32[]{:S(2)}) collective-permute-start(bf16[32,1024]{1,0:T(8,128)(2,1)S(1)} %pad_maximum_fusion.15), channel_id=1, source_target_pairs={{0,0},{1,16},{2,2},{3,18},{4,4},{5,20},{6,6},{7,22},{8,8},{9,24},{... | collective-permute-start | bytes 196616 | tf_op jit(solution)/shard_map/ppermute | solution.py:44
  35.1 11.0 %collective-permute-start.10 = (bf16[192,1024]{1,0:T(8,128)(2,1)S(1)}, bf16[192,1024]{1,0:T(8,128)(2,1)S(1)}, u32[]{:S(2)}, u32[]{:S(2)}) collective-permute-start(bf16[192,1024]{1,0:T(8,128)(2,1)S(1)} %bitcast.264), channel_id=1, source_target_pairs={{0,0},{1,16},{2,2},{3,18},{4,4},{5,20},{6,6},{7,22},{8,8},{9,24},{... | collective-permute-start | bytes 1179656 | tf_op jit(solution)/shard_map/ppermute | solution.py:44
  40.6 5.4 %collective-permute-start.9 = (bf16[1,64,896]{2,1,0:T(8,128)(2,1)S(1)}, bf16[1,64,896]{2,1,0:T(8,128)(2,1)S(1)}, u32[]{:S(2)}, u32[]{:S(2)}) collective-permute-start(bf16[1,64,896]{2,1,0:T(8,128)(2,1)S(1)} %maximum_bitcast_fusion.1), channel_id=1, source_target_pairs={{0,2},{1,9},{2,0},{3,11},{4,6},{5,13},{6,4},{7,15},{8,10},{9,1},{1... | collective-permute-start | bytes 344072 | tf_op jit(solution)/shard_map/ppermute | solution.py:36
  41.4 16.8 %collective-permute-start.3 = (bf16[384,1024]{1,0:T(8,128)(2,1)S(1)}, bf16[384,1024]{1,0:T(8,128)(2,1)S(1)}, u32[]{:S(2)}, u32[]{:S(2)}) collective-permute-start(bf16[384,1024]{1,0:T(8,128)(2,1)S(1)} %pad_maximum_fusion.6), channel_id=1, source_target_pairs={{0,96},{1,33},{2,98},{3,35},{4,100},{5,37},{6,102},{7,39},{8,104},... | collective-permute-start | bytes 2359304 | tf_op jit(solution)/shard_map/ppermute | solution.py:36
  46.1 6.5 %collective-permute-start.11 = (bf16[2,64,896]{2,1,0:T(8,128)(2,1)S(1)}, bf16[2,64,896]{2,1,0:T(8,128)(2,1)S(1)}, u32[]{:S(2)}, u32[]{:S(2)}) collective-permute-start(bf16[2,64,896]{2,1,0:T(8,128)(2,1)S(1)} %maximum_select_fusion.7), channel_id=1, source_target_pairs={{0,6},{1,25},{2,4},{3,27},{4,2},{5,29},{6,0},{7,31},{8,14},{9,17},... | collective-permute-start | bytes 688136 | tf_op jit(solution)/shard_map/ppermute | solution.py:36
  46.8 11.0 %collective-permute-start.13 = (bf16[192,1024]{1,0:T(8,128)(2,1)S(1)}, bf16[192,1024]{1,0:T(8,128)(2,1)S(1)}, u32[]{:S(2)}, u32[]{:S(2)}) collective-permute-start(bf16[192,1024]{1,0:T(8,128)(2,1)S(1)} %collective-permute-done.10), channel_id=1, source_target_pairs={{0,32},{1,97},{2,34},{3,99},{4,36},{5,101},{6,38},{7,103},{8,40},{... | collective-permute-start | bytes 1179656 | tf_op jit(solution)/shard_map/ppermute | solution.py:36
  52.6 7.6 %collective-permute-start.12 = (bf16[4,64,896]{2,1,0:T(8,128)(2,1)S(1)}, bf16[4,64,896]{2,1,0:T(8,128)(2,1)S(1)}, u32[]{:S(2)}, u32[]{:S(2)}) collective-permute-start(bf16[4,64,896]{2,1,0:T(8,128)(2,1)S(1)} %maximum_select_fusion.5), channel_id=1, source_target_pairs={{0,8},{1,3},{2,10},{3,1},{4,12},{5,7},{6,14},{7,5},{8,0},{9,11},{1... | collective-permute-start | bytes 1376264 | tf_op jit(solution)/shard_map/ppermute | solution.py:36
  57.8 11.2 %collective-permute-start.15 = (bf16[384,1024]{1,0:T(8,128)(2,1)S(1)}, bf16[384,1024]{1,0:T(8,128)(2,1)S(1)}, u32[]{:S(2)}, u32[]{:S(2)}) collective-permute-start(bf16[384,1024]{1,0:T(8,128)(2,1)S(1)} %constant_dynamic-update-slice_fusion.9), channel_id=1, source_target_pairs={{0,96},{1,33},{2,98},{3,35},{4,100},{5,37},{6,102},{7,39},{8,104},... | collective-permute-start | bytes 2359304 | tf_op jit(solution)/shard_map/ppermute | solution.py:36
  59.2 16.0 %collective-permute-start.4 = (bf16[768,1024]{1,0:T(8,128)(2,1)}, bf16[768,1024]{1,0:T(8,128)(2,1)}, u32[]{:S(2)}, u32[]{:S(2)}) collective-permute-start(bf16[768,1024]{1,0:T(8,128)(2,1)} %constant_dynamic-update-slice_fusion.own_ref), channel_id=1, source_target_pairs={{0,1},{1,0},{2,3},{3,2},{4,5},{5,4},{6,7},{7,6},{8,9},{9,8},{10,11... | collective-permute-start | bytes 4718600 | tf_op jit(solution)/shard_map/ppermute | solution.py:36
  60.4 14.1 %collective-permute-start.14 = (bf16[8,64,896]{2,1,0:T(8,128)(2,1)S(1)}, bf16[8,64,896]{2,1,0:T(8,128)(2,1)S(1)}, u32[]{:S(2)}, u32[]{:S(2)}) collective-permute-start(bf16[8,64,896]{2,1,0:T(8,128)(2,1)S(1)} %maximum_select_fusion.3), channel_id=1, source_target_pairs={{0,24},{1,7},{2,26},{3,5},{4,28},{5,3},{6,30},{7,1},{8,16},{9,15},... | collective-permute-start | bytes 2752520 | tf_op jit(solution)/shard_map/ppermute | solution.py:36
  101.3 11.2 %collective-permute-start.17 = (bf16[384,1024]{1,0:T(8,128)(2,1)S(1)}, bf16[384,1024]{1,0:T(8,128)(2,1)S(1)}, u32[]{:S(2)}, u32[]{:S(2)}) collective-permute-start(bf16[384,1024]{1,0:T(8,128)(2,1)S(1)} %slice.305), channel_id=1, source_target_pairs={{0,96},{1,33},{2,98},{3,35},{4,100},{5,37},{6,102},{7,39},{8,104},... | collective-permute-start | bytes 2359304 | tf_op jit(solution)/shard_map/ppermute | solution.py:36
  102.4 4.8 %collective-permute-start.19 = (bf16[1,64,1152]{2,1,0:T(8,128)(2,1)S(1)}, bf16[1,64,1152]{2,1,0:T(8,128)(2,1)S(1)}, u32[]{:S(2)}, u32[]{:S(2)}) collective-permute-start(bf16[1,64,1152]{2,1,0:T(8,128)(2,1)S(1)} %maximum_bitcast_fusion), channel_id=1, source_target_pairs={{0,2},{1,9},{2,0},{3,11},{4,6},{5,13},{6,4},{7,15},{8,10},{9,1},{1... | collective-permute-start | bytes 442376 | tf_op jit(solution)/shard_map/ppermute | solution.py:36
  107.2 7.3 %collective-permute-start.20 = (bf16[2,64,1152]{2,1,0:T(8,128)(2,1)S(1)}, bf16[2,64,1152]{2,1,0:T(8,128)(2,1)S(1)}, u32[]{:S(2)}, u32[]{:S(2)}) collective-permute-start(bf16[2,64,1152]{2,1,0:T(8,128)(2,1)S(1)} %maximum_select_fusion.6), channel_id=1, source_target_pairs={{0,6},{1,25},{2,4},{3,27},{4,2},{5,29},{6,0},{7,31},{8,14},{9,17},... | collective-permute-start | bytes 884744 | tf_op jit(solution)/shard_map/ppermute | solution.py:36
  112.8 7.9 %collective-permute-start.18 = (bf16[192,1024]{1,0:T(8,128)(2,1)S(1)}, bf16[192,1024]{1,0:T(8,128)(2,1)S(1)}, u32[]{:S(2)}, u32[]{:S(2)}) collective-permute-start(bf16[192,1024]{1,0:T(8,128)(2,1)S(1)} %slice.308), channel_id=1, source_target_pairs={{0,32},{1,97},{2,34},{3,99},{4,36},{5,101},{6,38},{7,103},{8,40},{... | collective-permute-start | bytes 1179656 | tf_op jit(solution)/shard_map/ppermute | solution.py:36
  114.6 9.1 %collective-permute-start.21 = (bf16[4,64,1152]{2,1,0:T(8,128)(2,1)S(1)}, bf16[4,64,1152]{2,1,0:T(8,128)(2,1)S(1)}, u32[]{:S(2)}, u32[]{:S(2)}) collective-permute-start(bf16[4,64,1152]{2,1,0:T(8,128)(2,1)S(1)} %maximum_select_fusion.4), channel_id=1, source_target_pairs={{0,8},{1,3},{2,10},{3,1},{4,12},{5,7},{6,14},{7,5},{8,0},{9,11},{1... | collective-permute-start | bytes 1769480 | tf_op jit(solution)/shard_map/ppermute | solution.py:36
  121.2 7.9 %collective-permute-start.23 = (bf16[192,1024]{1,0:T(8,128)(2,1)S(1)}, bf16[192,1024]{1,0:T(8,128)(2,1)S(1)}, u32[]{:S(2)}, u32[]{:S(2)}) collective-permute-start(bf16[192,1024]{1,0:T(8,128)(2,1)S(1)} %multiply_convert_fusion.6), channel_id=1, source_target_pairs={{0,32},{1,97},{2,34},{3,99},{4,36},{5,101},{6,38},{7,103},{8,40},{... | collective-permute-start | bytes 1179656 | tf_op jit(solution)/shard_map/ppermute | solution.py:36
  124.0 21.2 %collective-permute-start.22 = (bf16[8,64,1152]{2,1,0:T(8,128)(2,1)S(1)}, bf16[8,64,1152]{2,1,0:T(8,128)(2,1)S(1)}, u32[]{:S(2)}, u32[]{:S(2)}) collective-permute-start(bf16[8,64,1152]{2,1,0:T(8,128)(2,1)S(1)} %maximum_select_fusion.2), channel_id=1, source_target_pairs={{0,24},{1,7},{2,26},{3,5},{4,28},{5,3},{6,30},{7,1},{8,16},{9,15},... | collective-permute-start | bytes 3538952 | tf_op jit(solution)/shard_map/ppermute | solution.py:36
  129.2 11.2 %collective-permute-start.24 = (bf16[384,1024]{1,0:T(8,128)(2,1)S(1)}, bf16[384,1024]{1,0:T(8,128)(2,1)S(1)}, u32[]{:S(2)}, u32[]{:S(2)}) collective-permute-start(bf16[384,1024]{1,0:T(8,128)(2,1)S(1)} %pad_maximum_fusion.9), channel_id=1, source_target_pairs={{0,96},{1,33},{2,98},{3,35},{4,100},{5,37},{6,102},{7,39},{8,104},... | collective-permute-start | bytes 2359304 | tf_op jit(solution)/shard_map/ppermute | solution.py:36
  140.6 7.5 %collective-permute-start.26 = (bf16[768,1024]{1,0:T(8,128)(2,1)S(1)}, bf16[768,1024]{1,0:T(8,128)(2,1)S(1)}, u32[]{:S(2)}, u32[]{:S(2)}) collective-permute-start(bf16[768,1024]{1,0:T(8,128)(2,1)S(1)} %pad_maximum_fusion.2), channel_id=1, source_target_pairs={{0,1},{1,0},{2,3},{3,2},{4,5},{5,4},{6,7},{7,6},{8,9},{9,8},{10,11... | collective-permute-start | bytes 4718600 | tf_op jit(solution)/shard_map/ppermute | solution.py:36
  145.1 5.3 %collective-permute-start.25 = (bf16[768,1024]{1,0:T(8,128)(2,1)S(1)}, bf16[768,1024]{1,0:T(8,128)(2,1)S(1)}, u32[]{:S(2)}, u32[]{:S(2)}) collective-permute-start(bf16[768,1024]{1,0:T(8,128)(2,1)S(1)} %copy-done.13), channel_id=1, source_target_pairs={{0,1},{1,0},{2,3},{3,2},{4,5},{5,4},{6,7},{7,6},{8,9},{9,8},{10,11... | collective-permute-start | bytes 4718600 | tf_op jit(solution)/shard_map/ppermute | solution.py:36
  154.3 6.2 %collective-permute-start.27 = (bf16[768,1024]{1,0:T(8,128)(2,1)}, bf16[768,1024]{1,0:T(8,128)(2,1)}, u32[]{:S(2)}, u32[]{:S(2)}) collective-permute-start(bf16[768,1024]{1,0:T(8,128)(2,1)} %convolution_convert_fusion), channel_id=1, source_target_pairs={{0,1},{1,0},{2,3},{3,2},{4,5},{5,4},{6,7},{7,6},{8,9},{9,8},{10,11... | collective-permute-start | bytes 4718600 | tf_op jit(solution)/shard_map/ppermute | solution.py:36
  164.8 11.4 %collective-permute-start.28 = (bf16[384,1024]{1,0:T(8,128)(2,1)S(1)}, bf16[384,1024]{1,0:T(8,128)(2,1)S(1)}, u32[]{:S(2)}, u32[]{:S(2)}) collective-permute-start(bf16[384,1024]{1,0:T(8,128)(2,1)S(1)} %slice.304), channel_id=1, source_target_pairs={{0,96},{1,33},{2,98},{3,35},{4,100},{5,37},{6,102},{7,39},{8,104},... | collective-permute-start | bytes 2359304 | tf_op jit(solution)/shard_map/ppermute | solution.py:36
  176.6 7.9 %collective-permute-start.29 = (bf16[192,1024]{1,0:T(8,128)(2,1)S(1)}, bf16[192,1024]{1,0:T(8,128)(2,1)S(1)}, u32[]{:S(2)}, u32[]{:S(2)}) collective-permute-start(bf16[192,1024]{1,0:T(8,128)(2,1)S(1)} %slice.307), channel_id=1, source_target_pairs={{0,32},{1,97},{2,34},{3,99},{4,36},{5,101},{6,38},{7,103},{8,40},{... | collective-permute-start | bytes 1179656 | tf_op jit(solution)/shard_map/ppermute | solution.py:36
  186.1 8.2 %collective-permute-start.30 = (bf16[192,1024]{1,0:T(8,128)(2,1)S(1)}, bf16[192,1024]{1,0:T(8,128)(2,1)S(1)}, u32[]{:S(2)}, u32[]{:S(2)}) collective-permute-start(bf16[192,1024]{1,0:T(8,128)(2,1)S(1)} %get-tuple-element.99), channel_id=1, source_target_pairs={{0,32},{1,97},{2,34},{3,99},{4,36},{5,101},{6,38},{7,103},{8,40},{... | collective-permute-start | bytes 1179656 | tf_op jit(solution)/shard_map/ppermute | solution.py:36
  188.8 16.9 %collective-permute-start.32 = (bf16[8,64,1152]{2,1,0:T(8,128)(2,1)}, bf16[8,64,1152]{2,1,0:T(8,128)(2,1)}, u32[]{:S(2)}, u32[]{:S(2)}) collective-permute-start(bf16[8,64,1152]{2,1,0:T(8,128)(2,1)} %constant_dynamic-slice_fusion.5), channel_id=1, source_target_pairs={{0,24},{1,7},{2,26},{3,5},{4,28},{5,3},{6,30},{7,1},{8,16},{9,15},... | collective-permute-start | bytes 3538952 | tf_op jit(solution)/shard_map/ppermute | solution.py:36
  195.3 11.5 %collective-permute-start.31 = (bf16[384,1024]{1,0:T(8,128)(2,1)}, bf16[384,1024]{1,0:T(8,128)(2,1)}, u32[]{:S(2)}, u32[]{:S(2)}) collective-permute-start(bf16[384,1024]{1,0:T(8,128)(2,1)} %pad_maximum_fusion.10), channel_id=1, source_target_pairs={{0,96},{1,33},{2,98},{3,35},{4,100},{5,37},{6,102},{7,39},{8,104},... | collective-permute-start | bytes 2359304 | tf_op jit(solution)/shard_map/ppermute | solution.py:36
  207.9 6.9 %collective-permute-start.33 = (bf16[768,1024]{1,0:T(8,128)(2,1)S(1)}, bf16[768,1024]{1,0:T(8,128)(2,1)S(1)}, u32[]{:S(2)}, u32[]{:S(2)}) collective-permute-start(bf16[768,1024]{1,0:T(8,128)(2,1)S(1)} %constant_dynamic-update-slice_fusion.11.own_ref), channel_id=1, source_target_pairs={{0,1},{1,0},{2,3},{3,2},{4,5},{5,4},{6,7},{7,6},{8,9},{9,8},{10,11... | collective-permute-start | bytes 4718600 | tf_op jit(solution)/shard_map/ppermute | solution.py:36
  213.8 21.9 %collective-permute-start.34 = (bf16[4,64,1152]{2,1,0:T(8,128)(2,1)S(1)}, bf16[4,64,1152]{2,1,0:T(8,128)(2,1)S(1)}, u32[]{:S(2)}, u32[]{:S(2)}) collective-permute-start(bf16[4,64,1152]{2,1,0:T(8,128)(2,1)S(1)} %constant_dynamic-slice_fusion.4), channel_id=1, source_target_pairs={{0,8},{1,3},{2,10},{3,1},{4,12},{5,7},{6,14},{7,5},{8,0},{9,11},{1... | collective-permute-start | bytes 1769480 | tf_op jit(solution)/shard_map/ppermute | solution.py:36
  221.6 14.0 %collective-permute-start.35 = (bf16[8,64,256]{2,1,0:T(8,128)(2,1)S(1)}, bf16[8,64,256]{2,1,0:T(8,128)(2,1)S(1)}, u32[]{:S(2)}, u32[]{:S(2)}) collective-permute-start(bf16[8,64,256]{2,1,0:T(8,128)(2,1)S(1)} %slice.172), channel_id=1, source_target_pairs={{0,24},{1,7},{2,26},{3,5},{4,28},{5,3},{6,30},{7,1},{8,16},{9,15},... | collective-permute-start | bytes 786440 | tf_op jit(solution)/shard_map/ppermute | solution.py:36
  255.4 15.0 %collective-permute-start.37 = (bf16[384,1024]{1,0:T(8,128)(2,1)S(1)}, bf16[384,1024]{1,0:T(8,128)(2,1)S(1)}, u32[]{:S(2)}, u32[]{:S(2)}) collective-permute-start(bf16[384,1024]{1,0:T(8,128)(2,1)S(1)} %slice.303), channel_id=1, source_target_pairs={{0,96},{1,33},{2,98},{3,35},{4,100},{5,37},{6,102},{7,39},{8,104},... | collective-permute-start | bytes 2359304 | tf_op jit(solution)/shard_map/ppermute | solution.py:36
  257.6 12.8 %collective-permute-start.38 = (bf16[8,64,640]{2,1,0:T(8,128)(2,1)S(1)}, bf16[8,64,640]{2,1,0:T(8,128)(2,1)}, u32[]{:S(2)}, u32[]{:S(2)}) collective-permute-start(bf16[8,64,640]{2,1,0:T(8,128)(2,1)S(1)} %constant_dynamic-slice_fusion.3), channel_id=1, source_target_pairs={{0,24},{1,7},{2,26},{3,5},{4,28},{5,3},{6,30},{7,1},{8,16},{9,15},... | collective-permute-start | bytes 1966088 | tf_op jit(solution)/shard_map/ppermute | solution.py:36
  261.6 14.5 %collective-permute-start.42 = (bf16[64,1152]{1,0:T(8,128)(2,1)}, bf16[64,1152]{1,0:T(8,128)(2,1)S(1)}, u32[]{:S(2)}, u32[]{:S(2)}) collective-permute-start(bf16[64,1152]{1,0:T(8,128)(2,1)} %get-tuple-element.162), channel_id=1, source_target_pairs={{0,2},{1,9},{2,0},{3,11},{4,6},{5,13},{6,4},{7,15},{8,10},{9,1},{1... | collective-permute-start | bytes 442376 | tf_op jit(solution)/shard_map/ppermute | solution.py:36
  261.6 14.6 %collective-permute-start.43 = (bf16[64,1152]{1,0:T(8,128)(2,1)}, bf16[64,1152]{1,0:T(8,128)(2,1)S(1)}, u32[]{:S(2)}, u32[]{:S(2)}) collective-permute-start(bf16[64,1152]{1,0:T(8,128)(2,1)} %get-tuple-element.161), channel_id=1, source_target_pairs={{0,4},{1,17},{2,6},{3,19},{4,0},{5,21},{6,2},{7,23},{8,12},{9,25},... | collective-permute-start | bytes 442376 | tf_op jit(solution)/shard_map/ppermute | solution.py:36
  265.1 15.3 %collective-permute-start.44 = (bf16[64,1152]{1,0:T(8,128)(2,1)}, bf16[64,1152]{1,0:T(8,128)(2,1)S(1)}, u32[]{:S(2)}, u32[]{:S(2)}) collective-permute-start(bf16[64,1152]{1,0:T(8,128)(2,1)} %get-tuple-element.160), channel_id=1, source_target_pairs={{0,6},{1,25},{2,4},{3,27},{4,2},{5,29},{6,0},{7,31},{8,14},{9,17},... | collective-permute-start | bytes 442376 | tf_op jit(solution)/shard_map/ppermute | solution.py:36
  272.2 9.7 %collective-permute-start.40 = (bf16[192,1024]{1,0:T(8,128)(2,1)S(1)}, bf16[192,1024]{1,0:T(8,128)(2,1)S(1)}, u32[]{:S(2)}, u32[]{:S(2)}) collective-permute-start(bf16[192,1024]{1,0:T(8,128)(2,1)S(1)} %slice.306), channel_id=1, source_target_pairs={{0,32},{1,97},{2,34},{3,99},{4,36},{5,101},{6,38},{7,103},{8,40},{... | collective-permute-start | bytes 1179656 | tf_op jit(solution)/shard_map/ppermute | solution.py:36
  275.2 6.7 %collective-permute-start.41 = (bf16[4,64,640]{2,1,0:T(8,128)(2,1)S(1)}, bf16[4,64,640]{2,1,0:T(8,128)(2,1)S(1)}, u32[]{:S(2)}, u32[]{:S(2)}) collective-permute-start(bf16[4,64,640]{2,1,0:T(8,128)(2,1)S(1)} %constant_dynamic-slice_fusion.1), channel_id=1, source_target_pairs={{0,8},{1,3},{2,10},{3,1},{4,12},{5,7},{6,14},{7,5},{8,0},{9,11},{1... | collective-permute-start | bytes 983048 | tf_op jit(solution)/shard_map/ppermute | solution.py:36
  276.1 13.6 %collective-permute-start.49 = (bf16[64,256]{1,0:T(8,128)(2,1)S(1)}, bf16[64,256]{1,0:T(8,128)(2,1)S(1)}, u32[]{:S(2)}, u32[]{:S(2)}) collective-permute-start(bf16[64,256]{1,0:T(8,128)(2,1)S(1)} %get-tuple-element.185), channel_id=1, source_target_pairs={{0,2},{1,9},{2,0},{3,11},{4,6},{5,13},{6,4},{7,15},{8,10},{9,1},{1... | collective-permute-start | bytes 98312 | tf_op jit(solution)/shard_map/ppermute | solution.py:36
  276.2 13.6 %collective-permute-start.50 = (bf16[64,256]{1,0:T(8,128)(2,1)S(1)}, bf16[64,256]{1,0:T(8,128)(2,1)S(1)}, u32[]{:S(2)}, u32[]{:S(2)}) collective-permute-start(bf16[64,256]{1,0:T(8,128)(2,1)S(1)} %get-tuple-element.184), channel_id=1, source_target_pairs={{0,4},{1,17},{2,6},{3,19},{4,0},{5,21},{6,2},{7,23},{8,12},{9,25},... | collective-permute-start | bytes 98312 | tf_op jit(solution)/shard_map/ppermute | solution.py:36
  280.3 13.1 %collective-permute-start.51 = (bf16[64,256]{1,0:T(8,128)(2,1)S(1)}, bf16[64,256]{1,0:T(8,128)(2,1)S(1)}, u32[]{:S(2)}, u32[]{:S(2)}) collective-permute-start(bf16[64,256]{1,0:T(8,128)(2,1)S(1)} %get-tuple-element.183), channel_id=1, source_target_pairs={{0,6},{1,25},{2,4},{3,27},{4,2},{5,29},{6,0},{7,31},{8,14},{9,17},... | collective-permute-start | bytes 98312 | tf_op jit(solution)/shard_map/ppermute | solution.py:36
  282.5 13.2 %collective-permute-start.45 = (bf16[192,1024]{1,0:T(8,128)(2,1)S(1)}, bf16[192,1024]{1,0:T(8,128)(2,1)S(1)}, u32[]{:S(2)}, u32[]{:S(2)}) collective-permute-start(bf16[192,1024]{1,0:T(8,128)(2,1)S(1)} %get-tuple-element.146), channel_id=1, source_target_pairs={{0,0},{1,16},{2,2},{3,18},{4,4},{5,20},{6,6},{7,22},{8,8},{9,24},{... | collective-permute-start | bytes 1179656 | tf_op jit(solution)/shard_map/ppermute | solution.py:44
  288.6 6.9 %collective-permute-start.46 = (bf16[64,640]{1,0:T(8,128)(2,1)S(1)}, bf16[64,640]{1,0:T(8,128)(2,1)S(1)}, u32[]{:S(2)}, u32[]{:S(2)}) collective-permute-start(bf16[64,640]{1,0:T(8,128)(2,1)S(1)} %get-tuple-element.166), channel_id=1, source_target_pairs={{0,2},{1,9},{2,0},{3,11},{4,6},{5,13},{6,4},{7,15},{8,10},{9,1},{1... | collective-permute-start | bytes 245768 | tf_op jit(solution)/shard_map/ppermute | solution.py:36
  289.7 5.7 %collective-permute-start.47 = (bf16[64,640]{1,0:T(8,128)(2,1)S(1)}, bf16[64,640]{1,0:T(8,128)(2,1)S(1)}, u32[]{:S(2)}, u32[]{:S(2)}) collective-permute-start(bf16[64,640]{1,0:T(8,128)(2,1)S(1)} %get-tuple-element.165), channel_id=1, source_target_pairs={{0,4},{1,17},{2,6},{3,19},{4,0},{5,21},{6,2},{7,23},{8,12},{9,25},... | collective-permute-start | bytes 245768 | tf_op jit(solution)/shard_map/ppermute | solution.py:36
  289.8 5.8 %collective-permute-start.48 = (bf16[64,640]{1,0:T(8,128)(2,1)S(1)}, bf16[64,640]{1,0:T(8,128)(2,1)S(1)}, u32[]{:S(2)}, u32[]{:S(2)}) collective-permute-start(bf16[64,640]{1,0:T(8,128)(2,1)S(1)} %get-tuple-element.164), channel_id=1, source_target_pairs={{0,6},{1,25},{2,4},{3,27},{4,2},{5,29},{6,0},{7,31},{8,14},{9,17},... | collective-permute-start | bytes 245768 | tf_op jit(solution)/shard_map/ppermute | solution.py:36
  295.9 5.4 %collective-permute-start.53 = (bf16[4,1,8,1408]{3,2,1,0:T(8,128)(2,1)S(1)}, bf16[4,1,8,1408]{3,2,1,0:T(8,128)(2,1)S(1)}, u32[]{:S(2)}, u32[]{:S(2)}) collective-permute-start(bf16[4,1,8,1408]{3,2,1,0:T(8,128)(2,1)S(1)} %constant_dynamic-slice_fusion), channel_id=1, source_target_pairs={{0,1},{1,0},{2,3},{3,2},{4,5},{5,4},{6,7},{7,6},{8,9},{9,8},{10,11... | collective-permute-start | bytes 270344 | tf_op jit(solution)/shard_map/ppermute | solution.py:36
  296.1 14.9 %collective-permute-start.52 = (bf16[208,1024]{1,0:T(8,128)(2,1)S(1)}, bf16[208,1024]{1,0:T(8,128)(2,1)S(1)}, u32[]{:S(2)}, u32[]{:S(2)}) collective-permute-start(bf16[208,1024]{1,0:T(8,128)(2,1)S(1)} %pad_maximum_fusion.11), channel_id=1, source_target_pairs={{0,0},{1,16},{2,2},{3,18},{4,4},{5,20},{6,6},{7,22},{8,8},{9,24},{... | collective-permute-start | bytes 1277960 | tf_op jit(solution)/shard_map/ppermute | solution.py:44
  (58 other events, 494.9 us)
Sparse Core Ops, SparseCore 0:
  211.9 32.4 reduce-scatter.1

commit v5 on v4

--- a/solution.py
+++ b/solution.py
@@ -42,12 +42,6 @@
 
 def cross(values):
     return lax.ppermute(values, AXES, [(k, crossed(k)) for k in range(DEVICES)])
-
-
-def cross_and_swap(values, masks):
-    return lax.ppermute(
-        values, AXES, [(crossed(k ^ masks[k & 1]), k) for k in range(DEVICES)]
-    )
 
 
 def after(value, *others):
@@ -612,7 +606,7 @@
     pieces = cross(jnp.concatenate([w_out, digits], axis=0))
     rows = after(hidden[0], local)
     inputs = cross(rows)
-    second = cross_and_swap(rows, RING_STEPS[0])
+    second = swap(inputs, *RING_STEPS[0])
     digits = pieces[16:18, :3].astype(jnp.int32)
     lengths = (digits[0] * 64 + digits[1])[None]
     pieces = pieces[:16].reshape(16, 4, 256).transpose(1, 0, 2).reshape(64, 256)

time: 326 us -> 327 us (level)
  waiting for transfers between devices: 84.7 us -> 91.6 us
  starting transfers between devices: 92.5 us -> 86.7 us
    ppermute x51 -> x52, waiting for transfers between devices: 84.7 us -> 91.5 us  [swap(): lax.ppermute(values, AXES, [(k, k ^ masks[k & 1]) for k in range(DEVICES)])]
    ppermute x51 -> x52, starting transfers between devices: 63.4 us -> 60.4 us  [swap(): lax.ppermute(values, AXES, [(k, k ^ masks[k & 1]) for k in range(DEVICES)])]
  transfers between devices with their start and end apart: 58 -> 58, of which waited for: 29 -> 30; matrix products, arithmetic and copies ran while one was open for 16% -> 16% of each run, Pallas kernels for 10% -> 10%
where the time goes in v5:
time: 327 us; the launch traced here: 321 us
  waiting for transfers between devices  91.6 us (28%)
  starting transfers between devices  86.7 us (27%)
  Pallas kernels  52.1 us (16%)
  local copies, waits for them, and re-layouts  28.3 us (9%)
  other arithmetic  25.2 us (8%)
  matrix products  19.7 us (6%)
  between operations  17.5 us (5%)
    ppermute x52, waiting for transfers between devices, swap(): lax.ppermute(values, AXES, [(k, k ^ masks[k & 1]) for k in range(DEVICES)])  91.5 us
    ppermute x52, starting transfers between devices, swap(): lax.ppermute(values, AXES, [(k, k ^ masks[k & 1]) for k in range(DEVICES)])  60.4 us
    pallas_call x6, Pallas kernels, ring_call(): pl.pallas_call(kernel, grid_spec=pltpu.PrefetchScalarGridSpec(num_scalar_...  34.3 us
    ppermute x5, starting transfers between devices, cross(): return lax.ppermute(values, AXES, [(k, crossed(k)) for k in range(DEVICES)])  26.2 us
    unnamed x108, local copies, waits for them, and re-layouts  11.7 us
    pallas_call x1, Pallas kernels, attend_back(): pl.pallas_call(attend_back_kernel, grid_spec=pltpu.PrefetchScalarGridSpec...  11 us
    dot_general x4, matrix products, contract_cols(): lax.dot_general(left, right, (((1,), (1,)), ((), ())), preferred_element_...  8.07 us
    pallas_call x1, Pallas kernels, attend(): pl.pallas_call(attend_kernel, grid_spec=pltpu.PrefetchScalarGridSpec(num_...  6.72 us
  transfers between devices with their start and end apart: 58, of which 30 were waited for; matrix products, arithmetic and copies ran while one was open for 16% of the time, Pallas kernels for 10%

profile of v5, /device:TPU:1, one launch (start us, length us, event | category | flops | bytes accessed | tf_op | source)
XLA Modules:
  0.0 320.9 jit_solution(15597103102916132350)
XLA Ops:
  8.7 6.9 %collective-permute-start.1 = (bf16[32,1024]{1,0:T(8,128)(2,1)S(1)}, bf16[32,1024]{1,0:T(8,128)(2,1)S(1)}, u32[]{:S(2)}, u32[]{:S(2)}) collective-permute-start(bf16[32,1024]{1,0:T(8,128)(2,1)S(1)} %pad_maximum_fusion.15), channel_id=1, source_target_pairs={{0,0},{1,16},{2,2},{3,18},{4,4},{5,20},{6,6},{7,22},{8,8},{9,24},{... | collective-permute-start | bytes 196616 | tf_op jit(solution)/shard_map/ppermute | solution.py:44
  23.8 2.6 collective-permute-start.8
  28.0 2.8 collective-permute-done.7
  32.2 6.1 %collective-permute-start.10 = (bf16[192,1024]{1,0:T(8,128)(2,1)S(1)}, bf16[192,1024]{1,0:T(8,128)(2,1)S(1)}, u32[]{:S(2)}, u32[]{:S(2)}) collective-permute-start(bf16[192,1024]{1,0:T(8,128)(2,1)S(1)} %bitcast.263), channel_id=1, source_target_pairs={{0,0},{1,16},{2,2},{3,18},{4,4},{5,20},{6,6},{7,22},{8,8},{9,24},{... | collective-permute-start | bytes 1179656 | tf_op jit(solution)/shard_map/ppermute | solution.py:44
  42.5 2.8 collective-permute-done.9
  49.2 2.7 collective-permute-done.11
  54.5 4.8 %collective-permute-done.13 = bf16[192,1024]{1,0:T(8,128)(2,1)S(1)} collective-permute-done((bf16[192,1024]{1,0:T(8,128)(2,1)S(1)}, bf16[192,1024]{1,0:T(8,128)(2,1)S(1)}, u32[]{:S(2)}, u32[]{:S(2)}) %collective-permute-start.13) | collective-permute-done | bytes 393248 | tf_op jit(solution)/shard_map/ppermute | solution.py:36
  60.8 2.4 collective-permute-start.14
  63.2 2.8 fusion.11
  67.2 3.3 %collective-permute-done.15 = bf16[384,1024]{1,0:T(8,128)(2,1)S(1)} collective-permute-done((bf16[384,1024]{1,0:T(8,128)(2,1)S(1)}, bf16[384,1024]{1,0:T(8,128)(2,1)S(1)}, u32[]{:S(2)}, u32[]{:S(2)}) %collective-permute-start.15) | collective-permute-done | bytes 786464 | tf_op jit(solution)/shard_map/ppermute | solution.py:36
  71.8 3.0 collective-permute-done.14
  76.4 10.7 %project.1 = (bf16[1536,1024]{1,0:T(8,128)(2,1)}, f32[1536,384]{1,0:T(8,128)}, bf16[1536,512]{1,0:T(8,128)(2,1)S(1)}, bf16[1536,512]{1,0:T(8,128)(2,1)}, bf16[51...) custom-call(s32[11]{0:T(128)S(1)} %concatenate.161.spots, bf16[768,1024]{1,0:T(8,128)(2,1)} %constant_dynamic-update-slice_fusion.own_ref, ...), custom_call_target="tpu_custom_call" | custom-call | bytes 800000 | tf_op jit(solution)/shard_map/project/pallas_call | solution.py:132
  87.1 6.7 %attend.1 = (bf16[1536,256]{1,0:T(8,128)(2,1)S(1)}, bf16[1536,256]{1,0:T(8,128)(2,1)}, f32[2,1536]{1,0:T(2,128)}) custom-call(s32[2]{0:T(128)S(1)} %pad_add_fusion.ends_ref, bf16[1536,512]{1,0:T(8,128)(2,1)S(1)} %get-tuple-element.82.q_ref.k_ref.v_ref, bf16[1536,512]{1,0:T(8,128)(2,1)S(1)} %get-tuple-element.82.q_ref.k_ref.v_ref, ...), custom_call_target="tpu_custom_call" | custom-call | bytes 600000 | tf_op jit(solution)/shard_map/attend/pallas_call | solution.py:328
  93.8 2.9 to_ring.1
  96.7 2.1 collective-permute-start.16
  98.8 3.0 collective-permute-done.16
  103.9 4.3 %collective-permute-done.19 = bf16[1,64,1152]{2,1,0:T(8,128)(2,1)S(1)} collective-permute-done((bf16[1,64,1152]{2,1,0:T(8,128)(2,1)S(1)}, bf16[1,64,1152]{2,1,0:T(8,128)(2,1)S(1)}, u32[]{:S(2)}, u32[]{:S(2)}) %collective-permute-start.19) | collective-permute-done | bytes 147488 | tf_op jit(solution)/shard_map/ppermute | solution.py:36
  108.2 3.0 collective-permute-start.20
  111.2 2.6 collective-permute-done.17
  116.1 5.9 %collective-permute-done.18 = bf16[192,1024]{1,0:T(8,128)(2,1)S(1)} collective-permute-done((bf16[192,1024]{1,0:T(8,128)(2,1)S(1)}, bf16[192,1024]{1,0:T(8,128)(2,1)S(1)}, u32[]{:S(2)}, u32[]{:S(2)}) %collective-permute-start.18) | collective-permute-done | bytes 393248 | tf_op jit(solution)/shard_map/ppermute | solution.py:36
  125.1 2.8 collective-permute-start.22
  127.9 2.5 collective-permute-done.23
  130.6 11.1 %collective-permute-done.24 = bf16[384,1024]{1,0:T(8,128)(2,1)S(1)} collective-permute-done((bf16[384,1024]{1,0:T(8,128)(2,1)S(1)}, bf16[384,1024]{1,0:T(8,128)(2,1)S(1)}, u32[]{:S(2)}, u32[]{:S(2)}) %collective-permute-start.24) | collective-permute-done | bytes 786464 | tf_op jit(solution)/shard_map/ppermute | solution.py:36
  141.9 4.5 %collective-permute-start.26 = (bf16[768,1024]{1,0:T(8,128)(2,1)S(1)}, bf16[768,1024]{1,0:T(8,128)(2,1)S(1)}, u32[]{:S(2)}, u32[]{:S(2)}) collective-permute-start(bf16[768,1024]{1,0:T(8,128)(2,1)S(1)} %pad_maximum_fusion.2), channel_id=1, source_target_pairs={{0,1},{1,0},{2,3},{3,2},{4,5},{5,4},{6,7},{7,6},{8,9},{9,8},{10,11... | collective-permute-start | bytes 4718600 | tf_op jit(solution)/shard_map/ppermute | solution.py:36
  153.0 2.6 convolution_convert_fusion
  156.0 3.2 fusion.47
  163.1 2.8 convert_add_fusion.1
  173.6 3.9 %collective-permute-done.28 = bf16[384,1024]{1,0:T(8,128)(2,1)S(1)} collective-permute-done((bf16[384,1024]{1,0:T(8,128)(2,1)S(1)}, bf16[384,1024]{1,0:T(8,128)(2,1)S(1)}, u32[]{:S(2)}, u32[]{:S(2)}) %collective-permute-start.28) | collective-permute-done | bytes 786464 | tf_op jit(solution)/shard_map/ppermute | solution.py:36
  179.5 6.3 %collective-permute-done.29 = bf16[192,1024]{1,0:T(8,128)(2,1)S(1)} collective-permute-done((bf16[192,1024]{1,0:T(8,128)(2,1)S(1)}, bf16[192,1024]{1,0:T(8,128)(2,1)S(1)}, u32[]{:S(2)}, u32[]{:S(2)}) %collective-permute-start.29) | collective-permute-done | bytes 393248 | tf_op jit(solution)/shard_map/ppermute | solution.py:36
  189.4 2.7 collective-permute-start.32
  192.1 3.5 %collective-permute-done.30 = bf16[192,1024]{1,0:T(8,128)(2,1)S(1)} collective-permute-done((bf16[192,1024]{1,0:T(8,128)(2,1)S(1)}, bf16[192,1024]{1,0:T(8,128)(2,1)S(1)}, u32[]{:S(2)}, u32[]{:S(2)}) %collective-permute-start.30) | collective-permute-done | bytes 393248 | tf_op jit(solution)/shard_map/ppermute | solution.py:36
  196.5 4.1 %to_pack.1 = bf16[1536,1024]{1,0:T(8,128)(2,1)} custom-call(s32[11]{0:T(128)S(1)} %concatenate.161.spots, bf16[768,384]{1,0:T(8,128)(2,1)S(1)} %get-tuple-element.100.own_ref, bf16[768,384]{1,0:T(8,128)(2,1)S(1)} %get-tuple-element.101.other_ref, bf16[384,1024]{1,0:T(8,128)(2,1)S(1)} %bitcast.207), custom_call_target="tpu_custom_call" | custom-call | bytes 400000 | tf_op jit(solution)/shard_map/to_pack/pallas_call | solution.py:132
  200.7 5.6 %collective-permute-done.32 = bf16[8,64,1152]{2,1,0:T(8,128)(2,1)} collective-permute-done((bf16[8,64,1152]{2,1,0:T(8,128)(2,1)}, bf16[8,64,1152]{2,1,0:T(8,128)(2,1)}, u32[]{:S(2)}, u32[]{:S(2)}) %collective-permute-start.32) | collective-permute-done | bytes 1179680 | tf_op jit(solution)/shard_map/ppermute | solution.py:36
  209.2 3.8 %collective-permute-start.33 = (bf16[768,1024]{1,0:T(8,128)(2,1)S(1)}, bf16[768,1024]{1,0:T(8,128)(2,1)S(1)}, u32[]{:S(2)}, u32[]{:S(2)}) collective-permute-start(bf16[768,1024]{1,0:T(8,128)(2,1)S(1)} %constant_dynamic-update-slice_fusion.11.own_ref), channel_id=1, source_target_pairs={{0,1},{1,0},{2,3},{3,2},{4,5},{5,4},{6,7},{7,6},{8,9},{9,8},{10,11... | collective-permute-start | bytes 4718600 | tf_op jit(solution)/shard_map/ppermute | solution.py:36
  216.1 5.8 %out_back.1 = (bf16[1536,256]{1,0:T(8,128)(2,1)S(1)}, bf16[16,64,256]{2,1,0:T(8,128)(2,1)}) custom-call(s32[11]{0:T(128)S(1)} %concatenate.161.spots, bf16[768,1024]{1,0:T(8,128)(2,1)S(1)} %constant_dynamic-update-slice_fusion.11.own_ref, bf16[768,1024]{1,0:T(8,128)(2,1)S(1)} %collective-permute-done.33.other_ref, ...), custom_call_target="tpu_custom_call" | custom-call | bytes 500000 | tf_op jit(solution)/shard_map/out_back/pallas_call | solution.py:132
  222.8 3.0 collective-permute-start.35
  225.9 11.0 %attend_back.1 = (f32[1536,256]{1,0:T(8,128)S(1)}, f32[1536,128]{1,0:T(8,128)S(1)}, f32[1536,128]{1,0:T(8,128)S(1)}) custom-call(s32[2]{0:T(128)S(1)} %pad_add_fusion.ends_ref, bf16[1536,512]{1,0:T(8,128)(2,1)} %get-tuple-element.87.q_ref.k_ref.v_ref, bf16[1536,512]{1,0:T(8,128)(2,1)} %get-tuple-element.87.q_ref.k_ref.v_ref, ...), custom_call_target="tpu_custom_call" | custom-call | bytes 1100000 | tf_op jit(solution)/shard_map/attend_back/pallas_call | solution.py:400
  236.9 5.8 %project_back.1 = (bf16[1536,512]{1,0:T(8,128)(2,1)S(1)}, f32[2,128]{1,0:T(2,128)S(1)}) custom-call(s32[11]{0:T(128)S(1)} %concatenate.161.spots, f32[1536,384]{1,0:T(8,128)} %get-tuple-element.86.pre_ref, f32[1536,256]{1,0:T(8,128)S(1)} %get-tuple-element.109.dq_ref, f32[1536,128]{1,0:T(8,128)S(1)} %get-tuple-element.110.dk_ref, ...), custom_call_target="tpu_custom_call" | custom-call | bytes 500000 | tf_op jit(solution)/shard_map/project_back/pallas_call | solution.py:132
  246.5 5.1 %normed_back.1 = (bf16[768,1024]{1,0:T(8,128)(2,1)S(1)}, bf16[768,1024]{1,0:T(8,128)(2,1)}) custom-call(s32[11]{0:T(128)S(1)} %concatenate.161.spots, bf16[1536,512]{1,0:T(8,128)(2,1)S(1)} %get-tuple-element.116.d_pre_ref, bf16[512,1024]{1,0:T(8,128)(2,1)} %get-tuple-element.117.w_ref), custom_call_target="tpu_custom_call" | custom-call | bytes 400000 | tf_op jit(solution)/shard_map/normed_back/pallas_call | solution.py:132
  252.7 3.2 %collective-permute-done.36 = bf16[768,1024]{1,0:T(8,128)(2,1)S(1)} collective-permute-done((bf16[768,1024]{1,0:T(8,128)(2,1)}, bf16[768,1024]{1,0:T(8,128)(2,1)S(1)}, u32[]{:S(2)}, u32[]{:S(2)}) %collective-permute-start.36) | collective-permute-done | bytes 1572896 | tf_op jit(solution)/shard_map/ppermute | solution.py:36
  256.8 2.0 copy-done.15
  258.9 2.8 collective-permute-start.38
  264.3 2.0 collective-permute-done.39
  266.7 4.9 %collective-permute-done.38 = bf16[8,64,640]{2,1,0:T(8,128)(2,1)} collective-permute-done((bf16[8,64,640]{2,1,0:T(8,128)(2,1)S(1)}, bf16[8,64,640]{2,1,0:T(8,128)(2,1)}, u32[]{:S(2)}, u32[]{:S(2)}) %collective-permute-start.38) | collective-permute-done | bytes 655392 | tf_op jit(solution)/shard_map/ppermute | solution.py:36
  276.8 4.0 %collective-permute-start.50 = (bf16[64,256]{1,0:T(8,128)(2,1)S(1)}, bf16[64,256]{1,0:T(8,128)(2,1)S(1)}, u32[]{:S(2)}, u32[]{:S(2)}) collective-permute-start(bf16[64,256]{1,0:T(8,128)(2,1)S(1)} %get-tuple-element.184), channel_id=1, source_target_pairs={{0,4},{1,17},{2,6},{3,19},{4,0},{5,21},{6,2},{7,23},{8,12},{9,25},... | collective-permute-start | bytes 98312 | tf_op jit(solution)/shard_map/ppermute | solution.py:36
  282.8 6.5 %collective-permute-start.45 = (bf16[192,1024]{1,0:T(8,128)(2,1)S(1)}, bf16[192,1024]{1,0:T(8,128)(2,1)S(1)}, u32[]{:S(2)}, u32[]{:S(2)}) collective-permute-start(bf16[192,1024]{1,0:T(8,128)(2,1)S(1)} %get-tuple-element.146), channel_id=1, source_target_pairs={{0,0},{1,16},{2,2},{3,18},{4,4},{5,20},{6,6},{7,22},{8,8},{9,24},{... | collective-permute-start | bytes 1179656 | tf_op jit(solution)/shard_map/ppermute | solution.py:44
  290.5 3.1 collective-permute-start.48
  297.0 4.9 %collective-permute-start.52 = (bf16[208,1024]{1,0:T(8,128)(2,1)S(1)}, bf16[208,1024]{1,0:T(8,128)(2,1)S(1)}, u32[]{:S(2)}, u32[]{:S(2)}) collective-permute-start(bf16[208,1024]{1,0:T(8,128)(2,1)S(1)} %pad_maximum_fusion.11), channel_id=1, source_target_pairs={{0,0},{1,16},{2,2},{3,18},{4,4},{5,20},{6,6},{7,22},{8,8},{9,24},{... | collective-permute-start | bytes 1277960 | tf_op jit(solution)/shard_map/ppermute | solution.py:44
  (347 shorter events, 98.5 us)
Async XLA Ops:
  7.2 264.5 %reduce-scatter.2.cloned.1.call-start = ((), (), s32[]{:S(2)}) async-start(), calls=%async_computation.1 | async-start | bytes 3538944 | tf_op jit(solution)/shard_map/reduce_scatter | solution.py:697
  8.7 15.0 %collective-permute-start.1 = (bf16[32,1024]{1,0:T(8,128)(2,1)S(1)}, bf16[32,1024]{1,0:T(8,128)(2,1)S(1)}, u32[]{:S(2)}, u32[]{:S(2)}) collective-permute-start(bf16[32,1024]{1,0:T(8,128)(2,1)S(1)} %pad_maximum_fusion.15), channel_id=1, source_target_pairs={{0,0},{1,16},{2,2},{3,18},{4,4},{5,20},{6,6},{7,22},{8,8},{9,24},{... | collective-permute-start | bytes 196616 | tf_op jit(solution)/shard_map/ppermute | solution.py:44
  15.6 15.3 %collective-permute-start = (bf16[192,1024]{1,0:T(8,128)(2,1)}, bf16[192,1024]{1,0:T(8,128)(2,1)S(1)}, u32[]{:S(2)}, u32[]{:S(2)}) collective-permute-start(bf16[192,1024]{1,0:T(8,128)(2,1)} %bitcast.262), channel_id=1, source_target_pairs={{0,0},{1,16},{2,2},{3,18},{4,4},{5,20},{6,6},{7,22},{8,8},{9,24},{... | collective-permute-start | bytes 1179656 | tf_op jit(solution)/shard_map/ppermute | solution.py:44
  30.9 9.3 %collective-permute-start.2 = (bf16[192,1024]{1,0:T(8,128)(2,1)S(1)}, bf16[192,1024]{1,0:T(8,128)(2,1)S(1)}, u32[]{:S(2)}, u32[]{:S(2)}) collective-permute-start(bf16[192,1024]{1,0:T(8,128)(2,1)S(1)} %collective-permute-done), channel_id=1, source_target_pairs={{0,32},{1,97},{2,34},{3,99},{4,36},{5,101},{6,38},{7,103},{8,40},{... | collective-permute-start | bytes 1179656 | tf_op jit(solution)/shard_map/ppermute | solution.py:36
  32.2 13.2 %collective-permute-start.10 = (bf16[192,1024]{1,0:T(8,128)(2,1)S(1)}, bf16[192,1024]{1,0:T(8,128)(2,1)S(1)}, u32[]{:S(2)}, u32[]{:S(2)}) collective-permute-start(bf16[192,1024]{1,0:T(8,128)(2,1)S(1)} %bitcast.263), channel_id=1, source_target_pairs={{0,0},{1,16},{2,2},{3,18},{4,4},{5,20},{6,6},{7,22},{8,8},{9,24},{... | collective-permute-start | bytes 1179656 | tf_op jit(solution)/shard_map/ppermute | solution.py:44
  40.2 5.2 %collective-permute-start.9 = (bf16[1,64,896]{2,1,0:T(8,128)(2,1)S(1)}, bf16[1,64,896]{2,1,0:T(8,128)(2,1)S(1)}, u32[]{:S(2)}, u32[]{:S(2)}) collective-permute-start(bf16[1,64,896]{2,1,0:T(8,128)(2,1)S(1)} %maximum_bitcast_fusion.1), channel_id=1, source_target_pairs={{0,2},{1,9},{2,0},{3,11},{4,6},{5,13},{6,4},{7,15},{8,10},{9,1},{1... | collective-permute-start | bytes 344072 | tf_op jit(solution)/shard_map/ppermute | solution.py:36
  41.1 18.3 %collective-permute-start.3 = (bf16[384,1024]{1,0:T(8,128)(2,1)S(1)}, bf16[384,1024]{1,0:T(8,128)(2,1)S(1)}, u32[]{:S(2)}, u32[]{:S(2)}) collective-permute-start(bf16[384,1024]{1,0:T(8,128)(2,1)S(1)} %pad_maximum_fusion.6), channel_id=1, source_target_pairs={{0,96},{1,33},{2,98},{3,35},{4,100},{5,37},{6,102},{7,39},{8,104},... | collective-permute-start | bytes 2359304 | tf_op jit(solution)/shard_map/ppermute | solution.py:36
  45.4 6.5 %collective-permute-start.11 = (bf16[2,64,896]{2,1,0:T(8,128)(2,1)S(1)}, bf16[2,64,896]{2,1,0:T(8,128)(2,1)S(1)}, u32[]{:S(2)}, u32[]{:S(2)}) collective-permute-start(bf16[2,64,896]{2,1,0:T(8,128)(2,1)S(1)} %maximum_select_fusion.7), channel_id=1, source_target_pairs={{0,6},{1,25},{2,4},{3,27},{4,2},{5,29},{6,0},{7,31},{8,14},{9,17},... | collective-permute-start | bytes 688136 | tf_op jit(solution)/shard_map/ppermute | solution.py:36
  47.0 12.2 %collective-permute-start.13 = (bf16[192,1024]{1,0:T(8,128)(2,1)S(1)}, bf16[192,1024]{1,0:T(8,128)(2,1)S(1)}, u32[]{:S(2)}, u32[]{:S(2)}) collective-permute-start(bf16[192,1024]{1,0:T(8,128)(2,1)S(1)} %collective-permute-done.10), channel_id=1, source_target_pairs={{0,32},{1,97},{2,34},{3,99},{4,36},{5,101},{6,38},{7,103},{8,40},{... | collective-permute-start | bytes 1179656 | tf_op jit(solution)/shard_map/ppermute | solution.py:36
  52.0 8.6 %collective-permute-start.12 = (bf16[4,64,896]{2,1,0:T(8,128)(2,1)S(1)}, bf16[4,64,896]{2,1,0:T(8,128)(2,1)S(1)}, u32[]{:S(2)}, u32[]{:S(2)}) collective-permute-start(bf16[4,64,896]{2,1,0:T(8,128)(2,1)S(1)} %maximum_select_fusion.5), channel_id=1, source_target_pairs={{0,8},{1,3},{2,10},{3,1},{4,12},{5,7},{6,14},{7,5},{8,0},{9,11},{1... | collective-permute-start | bytes 1376264 | tf_op jit(solution)/shard_map/ppermute | solution.py:36
  59.3 11.2 %collective-permute-start.15 = (bf16[384,1024]{1,0:T(8,128)(2,1)S(1)}, bf16[384,1024]{1,0:T(8,128)(2,1)S(1)}, u32[]{:S(2)}, u32[]{:S(2)}) collective-permute-start(bf16[384,1024]{1,0:T(8,128)(2,1)S(1)} %constant_dynamic-update-slice_fusion.9), channel_id=1, source_target_pairs={{0,96},{1,33},{2,98},{3,35},{4,100},{5,37},{6,102},{7,39},{8,104},... | collective-permute-start | bytes 2359304 | tf_op jit(solution)/shard_map/ppermute | solution.py:36
  60.3 15.2 %collective-permute-start.4 = (bf16[768,1024]{1,0:T(8,128)(2,1)}, bf16[768,1024]{1,0:T(8,128)(2,1)}, u32[]{:S(2)}, u32[]{:S(2)}) collective-permute-start(bf16[768,1024]{1,0:T(8,128)(2,1)} %constant_dynamic-update-slice_fusion.own_ref), channel_id=1, source_target_pairs={{0,1},{1,0},{2,3},{3,2},{4,5},{5,4},{6,7},{7,6},{8,9},{9,8},{10,11... | collective-permute-start | bytes 4718600 | tf_op jit(solution)/shard_map/ppermute | solution.py:36
  60.8 14.0 %collective-permute-start.14 = (bf16[8,64,896]{2,1,0:T(8,128)(2,1)S(1)}, bf16[8,64,896]{2,1,0:T(8,128)(2,1)S(1)}, u32[]{:S(2)}, u32[]{:S(2)}) collective-permute-start(bf16[8,64,896]{2,1,0:T(8,128)(2,1)S(1)} %maximum_select_fusion.3), channel_id=1, source_target_pairs={{0,24},{1,7},{2,26},{3,5},{4,28},{5,3},{6,30},{7,1},{8,16},{9,15},... | collective-permute-start | bytes 2752520 | tf_op jit(solution)/shard_map/ppermute | solution.py:36
  96.7 5.1 %collective-permute-start.16 = (bf16[768,1024]{1,0:T(8,128)(2,1)S(1)}, bf16[768,1024]{1,0:T(8,128)(2,1)S(1)}, u32[]{:S(2)}, u32[]{:S(2)}) collective-permute-start(bf16[768,1024]{1,0:T(8,128)(2,1)S(1)} %get-tuple-element.85), channel_id=1, source_target_pairs={{0,1},{1,0},{2,3},{3,2},{4,5},{5,4},{6,7},{7,6},{8,9},{9,8},{10,11... | collective-permute-start | bytes 4718600 | tf_op jit(solution)/shard_map/ppermute | solution.py:36
  102.6 11.2 %collective-permute-start.17 = (bf16[384,1024]{1,0:T(8,128)(2,1)S(1)}, bf16[384,1024]{1,0:T(8,128)(2,1)S(1)}, u32[]{:S(2)}, u32[]{:S(2)}) collective-permute-start(bf16[384,1024]{1,0:T(8,128)(2,1)S(1)} %slice.305), channel_id=1, source_target_pairs={{0,96},{1,33},{2,98},{3,35},{4,100},{5,37},{6,102},{7,39},{8,104},... | collective-permute-start | bytes 2359304 | tf_op jit(solution)/shard_map/ppermute | solution.py:36
  108.2 7.4 %collective-permute-start.20 = (bf16[2,64,1152]{2,1,0:T(8,128)(2,1)S(1)}, bf16[2,64,1152]{2,1,0:T(8,128)(2,1)S(1)}, u32[]{:S(2)}, u32[]{:S(2)}) collective-permute-start(bf16[2,64,1152]{2,1,0:T(8,128)(2,1)S(1)} %maximum_select_fusion.6), channel_id=1, source_target_pairs={{0,6},{1,25},{2,4},{3,27},{4,2},{5,29},{6,0},{7,31},{8,14},{9,17},... | collective-permute-start | bytes 884744 | tf_op jit(solution)/shard_map/ppermute | solution.py:36
  114.1 7.9 %collective-permute-start.18 = (bf16[192,1024]{1,0:T(8,128)(2,1)S(1)}, bf16[192,1024]{1,0:T(8,128)(2,1)S(1)}, u32[]{:S(2)}, u32[]{:S(2)}) collective-permute-start(bf16[192,1024]{1,0:T(8,128)(2,1)S(1)} %slice.308), channel_id=1, source_target_pairs={{0,32},{1,97},{2,34},{3,99},{4,36},{5,101},{6,38},{7,103},{8,40},{... | collective-permute-start | bytes 1179656 | tf_op jit(solution)/shard_map/ppermute | solution.py:36
  115.7 9.1 %collective-permute-start.21 = (bf16[4,64,1152]{2,1,0:T(8,128)(2,1)S(1)}, bf16[4,64,1152]{2,1,0:T(8,128)(2,1)S(1)}, u32[]{:S(2)}, u32[]{:S(2)}) collective-permute-start(bf16[4,64,1152]{2,1,0:T(8,128)(2,1)S(1)} %maximum_select_fusion.4), channel_id=1, source_target_pairs={{0,8},{1,3},{2,10},{3,1},{4,12},{5,7},{6,14},{7,5},{8,0},{9,11},{1... | collective-permute-start | bytes 1769480 | tf_op jit(solution)/shard_map/ppermute | solution.py:36
  122.5 7.9 %collective-permute-start.23 = (bf16[192,1024]{1,0:T(8,128)(2,1)S(1)}, bf16[192,1024]{1,0:T(8,128)(2,1)S(1)}, u32[]{:S(2)}, u32[]{:S(2)}) collective-permute-start(bf16[192,1024]{1,0:T(8,128)(2,1)S(1)} %multiply_convert_fusion.6), channel_id=1, source_target_pairs={{0,32},{1,97},{2,34},{3,99},{4,36},{5,101},{6,38},{7,103},{8,40},{... | collective-permute-start | bytes 1179656 | tf_op jit(solution)/shard_map/ppermute | solution.py:36
  125.1 21.4 %collective-permute-start.22 = (bf16[8,64,1152]{2,1,0:T(8,128)(2,1)S(1)}, bf16[8,64,1152]{2,1,0:T(8,128)(2,1)S(1)}, u32[]{:S(2)}, u32[]{:S(2)}) collective-permute-start(bf16[8,64,1152]{2,1,0:T(8,128)(2,1)S(1)} %maximum_select_fusion.2), channel_id=1, source_target_pairs={{0,24},{1,7},{2,26},{3,5},{4,28},{5,3},{6,30},{7,1},{8,16},{9,15},... | collective-permute-start | bytes 3538952 | tf_op jit(solution)/shard_map/ppermute | solution.py:36
  130.5 11.2 %collective-permute-start.24 = (bf16[384,1024]{1,0:T(8,128)(2,1)S(1)}, bf16[384,1024]{1,0:T(8,128)(2,1)S(1)}, u32[]{:S(2)}, u32[]{:S(2)}) collective-permute-start(bf16[384,1024]{1,0:T(8,128)(2,1)S(1)} %pad_maximum_fusion.9), channel_id=1, source_target_pairs={{0,96},{1,33},{2,98},{3,35},{4,100},{5,37},{6,102},{7,39},{8,104},... | collective-permute-start | bytes 2359304 | tf_op jit(solution)/shard_map/ppermute | solution.py:36
  141.9 7.5 %collective-permute-start.26 = (bf16[768,1024]{1,0:T(8,128)(2,1)S(1)}, bf16[768,1024]{1,0:T(8,128)(2,1)S(1)}, u32[]{:S(2)}, u32[]{:S(2)}) collective-permute-start(bf16[768,1024]{1,0:T(8,128)(2,1)S(1)} %pad_maximum_fusion.2), channel_id=1, source_target_pairs={{0,1},{1,0},{2,3},{3,2},{4,5},{5,4},{6,7},{7,6},{8,9},{9,8},{10,11... | collective-permute-start | bytes 4718600 | tf_op jit(solution)/shard_map/ppermute | solution.py:36
  146.3 5.3 %collective-permute-start.25 = (bf16[768,1024]{1,0:T(8,128)(2,1)S(1)}, bf16[768,1024]{1,0:T(8,128)(2,1)S(1)}, u32[]{:S(2)}, u32[]{:S(2)}) collective-permute-start(bf16[768,1024]{1,0:T(8,128)(2,1)S(1)} %copy-done.13), channel_id=1, source_target_pairs={{0,1},{1,0},{2,3},{3,2},{4,5},{5,4},{6,7},{7,6},{8,9},{9,8},{10,11... | collective-permute-start | bytes 4718600 | tf_op jit(solution)/shard_map/ppermute | solution.py:36
  155.6 6.2 %collective-permute-start.27 = (bf16[768,1024]{1,0:T(8,128)(2,1)}, bf16[768,1024]{1,0:T(8,128)(2,1)}, u32[]{:S(2)}, u32[]{:S(2)}) collective-permute-start(bf16[768,1024]{1,0:T(8,128)(2,1)} %convolution_convert_fusion), channel_id=1, source_target_pairs={{0,1},{1,0},{2,3},{3,2},{4,5},{5,4},{6,7},{7,6},{8,9},{9,8},{10,11... | collective-permute-start | bytes 4718600 | tf_op jit(solution)/shard_map/ppermute | solution.py:36
  166.1 11.4 %collective-permute-start.28 = (bf16[384,1024]{1,0:T(8,128)(2,1)S(1)}, bf16[384,1024]{1,0:T(8,128)(2,1)S(1)}, u32[]{:S(2)}, u32[]{:S(2)}) collective-permute-start(bf16[384,1024]{1,0:T(8,128)(2,1)S(1)} %slice.304), channel_id=1, source_target_pairs={{0,96},{1,33},{2,98},{3,35},{4,100},{5,37},{6,102},{7,39},{8,104},... | collective-permute-start | bytes 2359304 | tf_op jit(solution)/shard_map/ppermute | solution.py:36
  177.9 7.9 %collective-permute-start.29 = (bf16[192,1024]{1,0:T(8,128)(2,1)S(1)}, bf16[192,1024]{1,0:T(8,128)(2,1)S(1)}, u32[]{:S(2)}, u32[]{:S(2)}) collective-permute-start(bf16[192,1024]{1,0:T(8,128)(2,1)S(1)} %slice.307), channel_id=1, source_target_pairs={{0,32},{1,97},{2,34},{3,99},{4,36},{5,101},{6,38},{7,103},{8,40},{... | collective-permute-start | bytes 1179656 | tf_op jit(solution)/shard_map/ppermute | solution.py:36
  187.4 8.2 %collective-permute-start.30 = (bf16[192,1024]{1,0:T(8,128)(2,1)S(1)}, bf16[192,1024]{1,0:T(8,128)(2,1)S(1)}, u32[]{:S(2)}, u32[]{:S(2)}) collective-permute-start(bf16[192,1024]{1,0:T(8,128)(2,1)S(1)} %get-tuple-element.99), channel_id=1, source_target_pairs={{0,32},{1,97},{2,34},{3,99},{4,36},{5,101},{6,38},{7,103},{8,40},{... | collective-permute-start | bytes 1179656 | tf_op jit(solution)/shard_map/ppermute | solution.py:36
  189.4 16.9 %collective-permute-start.32 = (bf16[8,64,1152]{2,1,0:T(8,128)(2,1)}, bf16[8,64,1152]{2,1,0:T(8,128)(2,1)}, u32[]{:S(2)}, u32[]{:S(2)}) collective-permute-start(bf16[8,64,1152]{2,1,0:T(8,128)(2,1)} %constant_dynamic-slice_fusion.5), channel_id=1, source_target_pairs={{0,24},{1,7},{2,26},{3,5},{4,28},{5,3},{6,30},{7,1},{8,16},{9,15},... | collective-permute-start | bytes 3538952 | tf_op jit(solution)/shard_map/ppermute | solution.py:36
  196.5 11.5 %collective-permute-start.31 = (bf16[384,1024]{1,0:T(8,128)(2,1)}, bf16[384,1024]{1,0:T(8,128)(2,1)}, u32[]{:S(2)}, u32[]{:S(2)}) collective-permute-start(bf16[384,1024]{1,0:T(8,128)(2,1)} %pad_maximum_fusion.10), channel_id=1, source_target_pairs={{0,96},{1,33},{2,98},{3,35},{4,100},{5,37},{6,102},{7,39},{8,104},... | collective-permute-start | bytes 2359304 | tf_op jit(solution)/shard_map/ppermute | solution.py:36
  209.2 6.9 %collective-permute-start.33 = (bf16[768,1024]{1,0:T(8,128)(2,1)S(1)}, bf16[768,1024]{1,0:T(8,128)(2,1)S(1)}, u32[]{:S(2)}, u32[]{:S(2)}) collective-permute-start(bf16[768,1024]{1,0:T(8,128)(2,1)S(1)} %constant_dynamic-update-slice_fusion.11.own_ref), channel_id=1, source_target_pairs={{0,1},{1,0},{2,3},{3,2},{4,5},{5,4},{6,7},{7,6},{8,9},{9,8},{10,11... | collective-permute-start | bytes 4718600 | tf_op jit(solution)/shard_map/ppermute | solution.py:36
  215.0 21.8 %collective-permute-start.34 = (bf16[4,64,1152]{2,1,0:T(8,128)(2,1)S(1)}, bf16[4,64,1152]{2,1,0:T(8,128)(2,1)S(1)}, u32[]{:S(2)}, u32[]{:S(2)}) collective-permute-start(bf16[4,64,1152]{2,1,0:T(8,128)(2,1)S(1)} %constant_dynamic-slice_fusion.4), channel_id=1, source_target_pairs={{0,8},{1,3},{2,10},{3,1},{4,12},{5,7},{6,14},{7,5},{8,0},{9,11},{1... | collective-permute-start | bytes 1769480 | tf_op jit(solution)/shard_map/ppermute | solution.py:36
  222.8 14.1 %collective-permute-start.35 = (bf16[8,64,256]{2,1,0:T(8,128)(2,1)S(1)}, bf16[8,64,256]{2,1,0:T(8,128)(2,1)S(1)}, u32[]{:S(2)}, u32[]{:S(2)}) collective-permute-start(bf16[8,64,256]{2,1,0:T(8,128)(2,1)S(1)} %slice.172), channel_id=1, source_target_pairs={{0,24},{1,7},{2,26},{3,5},{4,28},{5,3},{6,30},{7,1},{8,16},{9,15},... | collective-permute-start | bytes 786440 | tf_op jit(solution)/shard_map/ppermute | solution.py:36
  256.7 15.0 %collective-permute-start.37 = (bf16[384,1024]{1,0:T(8,128)(2,1)S(1)}, bf16[384,1024]{1,0:T(8,128)(2,1)S(1)}, u32[]{:S(2)}, u32[]{:S(2)}) collective-permute-start(bf16[384,1024]{1,0:T(8,128)(2,1)S(1)} %slice.303), channel_id=1, source_target_pairs={{0,96},{1,33},{2,98},{3,35},{4,100},{5,37},{6,102},{7,39},{8,104},... | collective-permute-start | bytes 2359304 | tf_op jit(solution)/shard_map/ppermute | solution.py:36
  258.9 12.8 %collective-permute-start.38 = (bf16[8,64,640]{2,1,0:T(8,128)(2,1)S(1)}, bf16[8,64,640]{2,1,0:T(8,128)(2,1)}, u32[]{:S(2)}, u32[]{:S(2)}) collective-permute-start(bf16[8,64,640]{2,1,0:T(8,128)(2,1)S(1)} %constant_dynamic-slice_fusion.3), channel_id=1, source_target_pairs={{0,24},{1,7},{2,26},{3,5},{4,28},{5,3},{6,30},{7,1},{8,16},{9,15},... | collective-permute-start | bytes 1966088 | tf_op jit(solution)/shard_map/ppermute | solution.py:36
  262.9 13.8 %collective-permute-start.42 = (bf16[64,1152]{1,0:T(8,128)(2,1)}, bf16[64,1152]{1,0:T(8,128)(2,1)S(1)}, u32[]{:S(2)}, u32[]{:S(2)}) collective-permute-start(bf16[64,1152]{1,0:T(8,128)(2,1)} %get-tuple-element.162), channel_id=1, source_target_pairs={{0,2},{1,9},{2,0},{3,11},{4,6},{5,13},{6,4},{7,15},{8,10},{9,1},{1... | collective-permute-start | bytes 442376 | tf_op jit(solution)/shard_map/ppermute | solution.py:36
  262.9 13.9 %collective-permute-start.43 = (bf16[64,1152]{1,0:T(8,128)(2,1)}, bf16[64,1152]{1,0:T(8,128)(2,1)S(1)}, u32[]{:S(2)}, u32[]{:S(2)}) collective-permute-start(bf16[64,1152]{1,0:T(8,128)(2,1)} %get-tuple-element.161), channel_id=1, source_target_pairs={{0,4},{1,17},{2,6},{3,19},{4,0},{5,21},{6,2},{7,23},{8,12},{9,25},... | collective-permute-start | bytes 442376 | tf_op jit(solution)/shard_map/ppermute | solution.py:36
  266.3 14.5 %collective-permute-start.44 = (bf16[64,1152]{1,0:T(8,128)(2,1)}, bf16[64,1152]{1,0:T(8,128)(2,1)S(1)}, u32[]{:S(2)}, u32[]{:S(2)}) collective-permute-start(bf16[64,1152]{1,0:T(8,128)(2,1)} %get-tuple-element.160), channel_id=1, source_target_pairs={{0,6},{1,25},{2,4},{3,27},{4,2},{5,29},{6,0},{7,31},{8,14},{9,17},... | collective-permute-start | bytes 442376 | tf_op jit(solution)/shard_map/ppermute | solution.py:36
  273.4 8.8 %collective-permute-start.40 = (bf16[192,1024]{1,0:T(8,128)(2,1)S(1)}, bf16[192,1024]{1,0:T(8,128)(2,1)S(1)}, u32[]{:S(2)}, u32[]{:S(2)}) collective-permute-start(bf16[192,1024]{1,0:T(8,128)(2,1)S(1)} %slice.306), channel_id=1, source_target_pairs={{0,32},{1,97},{2,34},{3,99},{4,36},{5,101},{6,38},{7,103},{8,40},{... | collective-permute-start | bytes 1179656 | tf_op jit(solution)/shard_map/ppermute | solution.py:36
  275.8 6.4 %collective-permute-start.41 = (bf16[4,64,640]{2,1,0:T(8,128)(2,1)S(1)}, bf16[4,64,640]{2,1,0:T(8,128)(2,1)S(1)}, u32[]{:S(2)}, u32[]{:S(2)}) collective-permute-start(bf16[4,64,640]{2,1,0:T(8,128)(2,1)S(1)} %constant_dynamic-slice_fusion.1), channel_id=1, source_target_pairs={{0,8},{1,3},{2,10},{3,1},{4,12},{5,7},{6,14},{7,5},{8,0},{9,11},{1... | collective-permute-start | bytes 983048 | tf_op jit(solution)/shard_map/ppermute | solution.py:36
  276.7 13.7 %collective-permute-start.49 = (bf16[64,256]{1,0:T(8,128)(2,1)S(1)}, bf16[64,256]{1,0:T(8,128)(2,1)S(1)}, u32[]{:S(2)}, u32[]{:S(2)}) collective-permute-start(bf16[64,256]{1,0:T(8,128)(2,1)S(1)} %get-tuple-element.185), channel_id=1, source_target_pairs={{0,2},{1,9},{2,0},{3,11},{4,6},{5,13},{6,4},{7,15},{8,10},{9,1},{1... | collective-permute-start | bytes 98312 | tf_op jit(solution)/shard_map/ppermute | solution.py:36
  276.8 13.7 %collective-permute-start.50 = (bf16[64,256]{1,0:T(8,128)(2,1)S(1)}, bf16[64,256]{1,0:T(8,128)(2,1)S(1)}, u32[]{:S(2)}, u32[]{:S(2)}) collective-permute-start(bf16[64,256]{1,0:T(8,128)(2,1)S(1)} %get-tuple-element.184), channel_id=1, source_target_pairs={{0,4},{1,17},{2,6},{3,19},{4,0},{5,21},{6,2},{7,23},{8,12},{9,25},... | collective-permute-start | bytes 98312 | tf_op jit(solution)/shard_map/ppermute | solution.py:36
  280.8 13.5 %collective-permute-start.51 = (bf16[64,256]{1,0:T(8,128)(2,1)S(1)}, bf16[64,256]{1,0:T(8,128)(2,1)S(1)}, u32[]{:S(2)}, u32[]{:S(2)}) collective-permute-start(bf16[64,256]{1,0:T(8,128)(2,1)S(1)} %get-tuple-element.183), channel_id=1, source_target_pairs={{0,6},{1,25},{2,4},{3,27},{4,2},{5,29},{6,0},{7,31},{8,14},{9,17},... | collective-permute-start | bytes 98312 | tf_op jit(solution)/shard_map/ppermute | solution.py:36
  282.8 13.7 %collective-permute-start.45 = (bf16[192,1024]{1,0:T(8,128)(2,1)S(1)}, bf16[192,1024]{1,0:T(8,128)(2,1)S(1)}, u32[]{:S(2)}, u32[]{:S(2)}) collective-permute-start(bf16[192,1024]{1,0:T(8,128)(2,1)S(1)} %get-tuple-element.146), channel_id=1, source_target_pairs={{0,0},{1,16},{2,2},{3,18},{4,4},{5,20},{6,6},{7,22},{8,8},{9,24},{... | collective-permute-start | bytes 1179656 | tf_op jit(solution)/shard_map/ppermute | solution.py:44
  289.5 6.8 %collective-permute-start.46 = (bf16[64,640]{1,0:T(8,128)(2,1)S(1)}, bf16[64,640]{1,0:T(8,128)(2,1)S(1)}, u32[]{:S(2)}, u32[]{:S(2)}) collective-permute-start(bf16[64,640]{1,0:T(8,128)(2,1)S(1)} %get-tuple-element.166), channel_id=1, source_target_pairs={{0,2},{1,9},{2,0},{3,11},{4,6},{5,13},{6,4},{7,15},{8,10},{9,1},{1... | collective-permute-start | bytes 245768 | tf_op jit(solution)/shard_map/ppermute | solution.py:36
  290.4 5.8 %collective-permute-start.47 = (bf16[64,640]{1,0:T(8,128)(2,1)S(1)}, bf16[64,640]{1,0:T(8,128)(2,1)S(1)}, u32[]{:S(2)}, u32[]{:S(2)}) collective-permute-start(bf16[64,640]{1,0:T(8,128)(2,1)S(1)} %get-tuple-element.165), channel_id=1, source_target_pairs={{0,4},{1,17},{2,6},{3,19},{4,0},{5,21},{6,2},{7,23},{8,12},{9,25},... | collective-permute-start | bytes 245768 | tf_op jit(solution)/shard_map/ppermute | solution.py:36
  290.5 6.0 %collective-permute-start.48 = (bf16[64,640]{1,0:T(8,128)(2,1)S(1)}, bf16[64,640]{1,0:T(8,128)(2,1)S(1)}, u32[]{:S(2)}, u32[]{:S(2)}) collective-permute-start(bf16[64,640]{1,0:T(8,128)(2,1)S(1)} %get-tuple-element.164), channel_id=1, source_target_pairs={{0,6},{1,25},{2,4},{3,27},{4,2},{5,29},{6,0},{7,31},{8,14},{9,17},... | collective-permute-start | bytes 245768 | tf_op jit(solution)/shard_map/ppermute | solution.py:36
  296.8 5.1 %collective-permute-start.53 = (bf16[4,1,8,1408]{3,2,1,0:T(8,128)(2,1)S(1)}, bf16[4,1,8,1408]{3,2,1,0:T(8,128)(2,1)S(1)}, u32[]{:S(2)}, u32[]{:S(2)}) collective-permute-start(bf16[4,1,8,1408]{3,2,1,0:T(8,128)(2,1)S(1)} %constant_dynamic-slice_fusion), channel_id=1, source_target_pairs={{0,1},{1,0},{2,3},{3,2},{4,5},{5,4},{6,7},{7,6},{8,9},{9,8},{10,11... | collective-permute-start | bytes 270344 | tf_op jit(solution)/shard_map/ppermute | solution.py:36
  297.0 15.2 %collective-permute-start.52 = (bf16[208,1024]{1,0:T(8,128)(2,1)S(1)}, bf16[208,1024]{1,0:T(8,128)(2,1)S(1)}, u32[]{:S(2)}, u32[]{:S(2)}) collective-permute-start(bf16[208,1024]{1,0:T(8,128)(2,1)S(1)} %pad_maximum_fusion.11), channel_id=1, source_target_pairs={{0,0},{1,16},{2,2},{3,18},{4,4},{5,20},{6,6},{7,22},{8,8},{9,24},{... | collective-permute-start | bytes 1277960 | tf_op jit(solution)/shard_map/ppermute | solution.py:44
  (58 other events, 494.0 us)
Sparse Core Ops, SparseCore 0:
  213.2 31.7 reduce-scatter.1
